TPU v7x, 256 devices: a whole 4x4x8 slice. The times are simulated.
256 devices in a mesh: site: 32 (over z, y_hi, core), dp: 8 (over x, y_lo).
Axes of the slice: x: 4, y: 4 (y_hi: 2, y_lo: 2; y = y_hi * 2 + y_lo), z: 8, core: 2. Of those that a mesh axis runs over, the one named last changes fastest.
Arguments:
- image_embed: bfloat16 [32768, 1152], P(('site', 'dp')), may hold values from -0.3 to 0.3
- text_embed: bfloat16 [32768, 1152], P(('site', 'dp')), may hold values from -0.3 to 0.3
- log_sharpness_factor: float32 [], replicated, may hold values from 1.5 to 3
- couple_score_shift: float32 [], replicated, may hold values from -4 to 0
Outputs:
- pair_loss: float32 [], replicated
- grad_image: float32 [32768, 1152], P(('site', 'dp'))
- grad_text: float32 [32768, 1152], P(('site', 'dp'))
All inputs are finite; a program needn't handle non-finite values.
Results may differ from a plain program's by a relative error of at most 0.00077.
Values may be sent and summed in bfloat16 or wider, within the bound.
No kernel may reach another device: no remote copies, remote signals or barrier semaphores. Data moves between devices by JAX's collectives and lax.ppermute only.
A program may use at most 128 MiB of HBM per device.

v0:
```python
import jax
import jax.numpy as jnp
from jax import lax
from jax.sharding import PartitionSpec as P

BAND = 4


EPS = 1e-06


def shifted(block, axis, distance):
    devices = range(lax.axis_size(axis))
    route = [((i - distance) % len(devices), i) for i in devices]
    return lax.ppermute(block, axis, route)


def normalize(embed):
    values = embed.astype(jnp.float32)
    inverse = lax.rsqrt(jnp.sum(values * values, axis=-1, keepdims=True) + EPS)
    return (values, inverse)


def back_norm(values, inverse, upstream):
    inner = jnp.sum(values * upstream, axis=-1, keepdims=True)
    return inverse * upstream - inverse * inverse * inverse * values * inner


def shards(image_embed, text_embed, log_sharpness_factor, couple_score_shift):
    row_count = image_embed.shape[0]
    site_count = lax.axis_size("site")
    group_count = lax.axis_size("dp")
    group_rows = group_count * row_count
    img_values, img_inverse = normalize(image_embed)
    txt_values, txt_inverse = normalize(text_embed)
    img_unit = (img_values * img_inverse).astype(jnp.bfloat16)
    txt_unit = (txt_values * txt_inverse).astype(jnp.bfloat16)
    sharpness_factor = jnp.exp(log_sharpness_factor)
    own_group = lax.all_gather(txt_unit, "dp", axis=0, tiled=True)
    blocks = [own_group]
    for segment_shift_amount in range(1, BAND):
        blocks.append(shifted(own_group, "site", -segment_shift_amount))
    own_start = lax.axis_index("dp") * row_count
    columns = lax.broadcasted_iota(jnp.int32, (row_count, group_rows), 1)
    row_ids = lax.broadcasted_iota(jnp.int32, (row_count, group_rows), 0) + own_start
    positive = (columns == row_ids).astype(jnp.float32)
    loss_part = jnp.zeros((), jnp.float32)
    img_grad = jnp.zeros((row_count, image_embed.shape[1]), jnp.float32)
    txt_terms = []
    for segment_shift_amount in range(BAND):
        couple_score_matrix = (
            sharpness_factor
            * lax.dot_general(
                img_unit,
                blocks[segment_shift_amount],
                (((1,), (1,)), ((), ())),
                preferred_element_type=jnp.float32,
            )
            + couple_score_shift
        )
        couple_match_sign = positive if segment_shift_amount == 0 else jnp.zeros_like(positive)
        label = 2.0 * couple_match_sign - 1.0
        loss_part = loss_part + jnp.sum(jax.nn.softplus(-label * couple_score_matrix))
        couple_weight_entry = (
            sharpness_factor * (jax.nn.sigmoid(couple_score_matrix) - couple_match_sign)
        ).astype(jnp.bfloat16)
        img_grad = img_grad + jnp.dot(
            couple_weight_entry, blocks[segment_shift_amount], preferred_element_type=jnp.float32
        )
        txt_terms.append(
            lax.dot_general(
                couple_weight_entry,
                img_unit,
                (((0,), (0,)), ((), ())),
                preferred_element_type=jnp.float32,
            )
        )
    block_total = txt_terms[0]
    for segment_shift_amount in range(1, BAND):
        block_total = block_total + shifted(
            txt_terms[segment_shift_amount], "site", segment_shift_amount
        )
    txt_grad = lax.psum_scatter(block_total, "dp", scatter_dimension=0, tiled=True)
    loss_sum = lax.psum(loss_part, ("site", "dp"))
    pair_loss = loss_sum / jnp.float32(site_count * group_rows * BAND * group_rows)
    grad_image = back_norm(img_values, img_inverse, img_grad)
    grad_text = back_norm(txt_values, txt_inverse, txt_grad)
    return (pair_loss, grad_image, grad_text)


def solution(mesh):
    return jax.shard_map(
        shards,
        mesh=mesh,
        in_specs=(P(("site", "dp"), None), P(("site", "dp"), None), P(), P()),
        out_specs=(P(), P(("site", "dp"), None), P(("site", "dp"), None)),
        check_vma=False,
    )
```

profile of v0, /device:TPU:24, one launch (start us, length us, event | category | flops | bytes accessed | tf_op | source)
XLA Modules:
  0.0 573.4 jit_solution(6808040996062724246)
XLA Ops:
  7.2 0.0 all-gather.2.cloned.1.call-start
  7.2 1.1 fusion.12
  8.3 1.8 fusion.13
  10.1 0.0 all-gather.2.cloned.1.call-update
  10.1 0.0 reduce-scatter.2.cloned.1.call-start
  10.2 61.3 %all-gather.2.cloned.1.call-done = bf16[1024,1152]{1,0:T(8,128)(2,1)} async-done(((bf16[128,1152]{1,0:T(8,128)(2,1)}), bf16[1024,1152]{1,0:T(8,128)(2,1)}) %all-gather.2.cloned.1.call-update) | async-done | bytes 2359312 | tf_op jit(solution)/shard_map/all_gather | solution.py:39
  71.5 1.4 collective-permute-start.1
  72.9 3.4 collective-permute-start
  77.7 1.1 fusion.7
  78.8 49.5 %collective-permute-done.1 = bf16[1024,1152]{1,0:T(8,128)(2,1)S(1)} collective-permute-done((bf16[1024,1152]{1,0:T(8,128)(2,1)}, bf16[1024,1152]{1,0:T(8,128)(2,1)S(1)}, u32[]{:S(2)}, u32[]{:S(2)}) %collective-permute-start.1) | collective-permute-done | bytes 2359328 | tf_op jit(solution)/shard_map/ppermute | solution.py:15
  128.3 2.8 fusion.19
  131.2 42.5 %collective-permute-done = bf16[1024,1152]{1,0:T(8,128)(2,1)} collective-permute-done((bf16[1024,1152]{1,0:T(8,128)(2,1)}, bf16[1024,1152]{1,0:T(8,128)(2,1)}, u32[]{:S(2)}, u32[]{:S(2)}) %collective-permute-start) | collective-permute-done | bytes 2359328 | tf_op jit(solution)/shard_map/ppermute | solution.py:15
  173.7 3.4 fusion.18
  177.1 3.0 fusion.22
  180.0 3.0 fusion.21
  183.0 3.4 fusion.20
  186.4 3.1 fusion.23
  189.5 20.4 %collective-permute-start.5 = (f32[1024,1152]{1,0:T(8,128)}, f32[1024,1152]{1,0:T(8,128)}, u32[]{:S(2)}, u32[]{:S(2)}) collective-permute-start(f32[1024,1152]{1,0:T(8,128)} %fusion.23), channel_id=1, source_target_pairs={{232,0},{240,8},{248,16},{0,24},{8,32},{16,40},{24,48},{32,56},{40... | collective-permute-start | bytes 14155784 | tf_op jit(solution)/shard_map/ppermute | solution.py:15
  209.9 0.4 collective-permute-start.4
  210.3 3.4 fusion.17
  213.7 98.7 %collective-permute-done.5 = f32[1024,1152]{1,0:T(8,128)} collective-permute-done((f32[1024,1152]{1,0:T(8,128)}, f32[1024,1152]{1,0:T(8,128)}, u32[]{:S(2)}, u32[]{:S(2)}) %collective-permute-start.5) | collective-permute-done | bytes 4718624 | tf_op jit(solution)/shard_map/ppermute | solution.py:15
  312.5 3.4 collective-permute-done.3
  315.9 97.7 %collective-permute-done.4 = f32[1024,1152]{1,0:T(8,128)} collective-permute-done((f32[1024,1152]{1,0:T(8,128)}, f32[1024,1152]{1,0:T(8,128)}, u32[]{:S(2)}, u32[]{:S(2)}) %collective-permute-start.4) | collective-permute-done | bytes 4718624 | tf_op jit(solution)/shard_map/ppermute | solution.py:15
  413.6 8.2 %fusion.1 = f32[1024,1152]{1,0:T(8,128)} fusion(f32[1024,1152]{1,0:T(8,128)} %collective-permute-done.5, f32[1024,1152]{1,0:T(8,128)} %collective-permute-done.4, f32[1024,1152]{1,0:T(8,128)} %collective-permute-done.3, f32[128,1024]{1,0:T(8,128)S(1)} %get-tuple-element.8, f32[]{:T(128)S(6)} %exp.28, s32[128]{0:T(128)S(1)} %iota_add_fusion, ...), kind=kOutput, calls=%fused_computation.2 | convolution fusion | flops 307019776 | bytes 19694596 | tf_op jit(solution)/shard_map/dot_general | solution.py:71
  424.4 2.3 fusion.25
  426.7 128.5 %psum.7 = f32[]{:T(128)} all-reduce(f32[]{:T(128)S(6)} %add.119), channel_id=1, replica_groups=mesh['site'=32,'dp'=8] {'site','dp'}, use_global_device_ids=true, to_apply=%region_6.7 | all-reduce | flops 1 | bytes 8 | tf_op jit(solution)/shard_map/psum | solution.py:84
  555.8 2.2 fusion.24
  558.1 2.4 convolution_add_fusion.2
  560.5 0.7 fusion.11
  561.1 1.0 fusion.10
  562.2 1.2 fusion.16
  563.4 2.1 fusion.15
  (16 shorter events, 0.1 us)
Async XLA Ops:
  7.2 64.4 %all-gather.2.cloned.1.call-start = ((), (), s32[]{:S(2)}) async-start(), calls=%async_computation.1 | async-start | bytes 2654208 | tf_op jit(solution)/shard_map/all_gather | solution.py:39
  10.1 163.6 %copy-start = (bf16[128,1152]{1,0:T(8,128)(2,1)S(1)}, bf16[128,1152]{1,0:T(8,128)(2,1)}, u32[]{:S(2)}) copy-start(bf16[128,1152]{1,0:T(8,128)(2,1)} %param.4) | copy-start | bytes 884740
  10.1 552.0 %reduce-scatter.2.cloned.1.call-start = ((), (), s32[]{:S(2)}) async-start(), calls=%async_computation.2 | async-start | bytes 5308416 | tf_op jit(solution)/shard_map/reduce_scatter | solution.py:83
  71.5 56.8 %collective-permute-start.1 = (bf16[1024,1152]{1,0:T(8,128)(2,1)}, bf16[1024,1152]{1,0:T(8,128)(2,1)S(1)}, u32[]{:S(2)}, u32[]{:S(2)}) collective-permute-start(bf16[1024,1152]{1,0:T(8,128)(2,1)} %all-gather.2.cloned.1.call-done), channel_id=1, source_target_pairs={{16,0},{24,8},{32,16},{40,24},{48,32},{56,40},{64,48},{72,56},{80,... | collective-permute-start | bytes 7077896 | tf_op jit(solution)/shard_map/ppermute | solution.py:15
  72.9 100.8 %collective-permute-start = (bf16[1024,1152]{1,0:T(8,128)(2,1)}, bf16[1024,1152]{1,0:T(8,128)(2,1)}, u32[]{:S(2)}, u32[]{:S(2)}) collective-permute-start(bf16[1024,1152]{1,0:T(8,128)(2,1)} %all-gather.2.cloned.1.call-done), channel_id=1, source_target_pairs={{8,0},{16,8},{24,16},{32,24},{40,32},{48,40},{56,48},{64,56},{72,6... | collective-permute-start | bytes 7077896 | tf_op jit(solution)/shard_map/ppermute | solution.py:15
  76.3 106.7 %collective-permute-start.2 = (bf16[1024,1152]{1,0:T(8,128)(2,1)}, bf16[1024,1152]{1,0:T(8,128)(2,1)}, u32[]{:S(2)}, u32[]{:S(2)}) collective-permute-start(bf16[1024,1152]{1,0:T(8,128)(2,1)} %all-gather.2.cloned.1.call-done), channel_id=1, source_target_pairs={{24,0},{32,8},{40,16},{48,24},{56,32},{64,40},{72,48},{80,56},{88,... | collective-permute-start | bytes 7077896 | tf_op jit(solution)/shard_map/ppermute | solution.py:15
  128.3 2.9 copy-start.2
  189.5 123.0 %collective-permute-start.5 = (f32[1024,1152]{1,0:T(8,128)}, f32[1024,1152]{1,0:T(8,128)}, u32[]{:S(2)}, u32[]{:S(2)}) collective-permute-start(f32[1024,1152]{1,0:T(8,128)} %fusion.23), channel_id=1, source_target_pairs={{232,0},{240,8},{248,16},{0,24},{8,32},{16,40},{24,48},{32,56},{40... | collective-permute-start | bytes 14155784 | tf_op jit(solution)/shard_map/ppermute | solution.py:15
  209.9 106.0 %collective-permute-start.3 = (f32[1024,1152]{1,0:T(8,128)}, f32[1024,1152]{1,0:T(8,128)}, u32[]{:S(2)}, u32[]{:S(2)}) collective-permute-start(f32[1024,1152]{1,0:T(8,128)} %fusion.21), channel_id=1, source_target_pairs={{248,0},{0,8},{8,16},{16,24},{24,32},{32,40},{40,48},{48,56},{56,6... | collective-permute-start | bytes 14155784 | tf_op jit(solution)/shard_map/ppermute | solution.py:15
  209.9 203.7 %collective-permute-start.4 = (f32[1024,1152]{1,0:T(8,128)}, f32[1024,1152]{1,0:T(8,128)}, u32[]{:S(2)}, u32[]{:S(2)}) collective-permute-start(f32[1024,1152]{1,0:T(8,128)} %fusion.22), channel_id=1, source_target_pairs={{240,0},{248,8},{0,16},{8,24},{16,32},{24,40},{32,48},{40,56},{48,... | collective-permute-start | bytes 14155784 | tf_op jit(solution)/shard_map/ppermute | solution.py:15
  558.1 2.4 copy-start.3
  560.5 1.7 copy-start.1
Sparse Core Ops, SparseCore 0:
  10.4 61.1 all-gather.1
  421.9 139.4 reduce-scatter.1
where the time goes:
time: 578 us; the launch traced here: 573 us
  waiting for transfers between devices  353 us (61%)
  blocking collectives  129 us (22%)
  matrix products  37.8 us (7%)
  starting transfers between devices  25.7 us (4%)
  between operations  19.8 us (3%)
  other arithmetic  8.35 us (1%)
    ppermute x6, waiting for transfers between devices, shifted(): return lax.ppermute(block, axis, route)  292 us
    psum x1, blocking collectives, shards(): loss_sum = lax.psum(loss_part, ('site', 'dp'))  129 us
    all_gather x1, waiting for transfers between devices, shards(): own_group = lax.all_gather(txt_unit, 'dp', axis=0, tiled=True)  61.3 us
    ppermute x6, starting transfers between devices, shifted(): return lax.ppermute(block, axis, route)  25.6 us
    dot_general x4, matrix products, shards(): lax.dot_general(couple_weight_entry, img_unit, (((0,), (0,)), ((), ())),...  17.2 us
    dot_general x4, matrix products, shards(): lax.dot_general(img_unit, blocks[segment_shift_amount], (((1,), (1,)), ((...  13 us
  transfers between devices with their start and end apart: 8, of which 6 were waited for; matrix products, arithmetic and copies ran while one was open for 4% of the time, Pallas kernels for 0%

commit v1 on v0

v1 whole, which is shorter than its diff:
```python
import functools

import jax
import jax.numpy as jnp
from jax import lax
from jax.experimental import pallas as pl
from jax.experimental.pallas import tpu as pltpu
from jax.sharding import PartitionSpec as P

BAND = 4
EPS = 1e-06
AXES = ("site", "dp")
Z, YH, CORE, X, YL = 8, 2, 2, 4, 2


def route(move):
    pairs = []
    for source in range(Z * YH * CORE * X * YL):
        rest, yl = divmod(source, YL)
        rest, x = divmod(rest, X)
        rest, core = divmod(rest, CORE)
        z, yh = divmod(rest, YH)
        z, yh, core, x, yl = move(z, yh, core, x, yl)
        target = ((((z % Z) * YH + yh) * CORE + core) * X + x % X) * YL + yl
        pairs.append((source, target))
    return pairs


UP_X = route(lambda z, yh, c, x, yl: (z, yh, c, x + 1, yl))
DOWN_X = route(lambda z, yh, c, x, yl: (z, yh, c, x - 1, yl))
MATE_Y = route(lambda z, yh, c, x, yl: (z, yh, c, x, 1 - yl))
FLIP_Y = route(lambda z, yh, c, x, yl: (z, 1 - yh, c, x, 1 - yl))
DOWN_Z = route(lambda z, yh, c, x, yl: (z - 1, yh, c, x, yl))
UP_Z = route(lambda z, yh, c, x, yl: (z + 1, yh, c, x, yl))
OTHER_CORE = route(lambda z, yh, c, x, yl: (z, yh, 1 - c, x, yl))
LOSS_ROUTES = (
    OTHER_CORE,
    route(lambda z, yh, c, x, yl: (z, yh, c, x ^ 1, yl)),
    route(lambda z, yh, c, x, yl: (z, yh, c, 3 - x, yl)),
    MATE_Y,
    FLIP_Y,
    route(lambda z, yh, c, x, yl: (z ^ 1, yh, c, x, yl)),
    route(lambda z, yh, c, x, yl: (z ^ 2, yh, c, x, yl)),
    route(lambda z, yh, c, x, yl: (z ^ 4, yh, c, x, yl)),
)


def move(block, pairs):
    return lax.ppermute(block, AXES, pairs)


def unit_kernel(image_ref, text_ref, img_unit_ref, txt_unit_ref):
    for source, unit in ((image_ref, img_unit_ref), (text_ref, txt_unit_ref)):
        values = source[...].astype(jnp.float32)
        inverse = lax.rsqrt(jnp.sum(values * values, axis=-1, keepdims=True) + EPS)
        unit[...] = (values * inverse).astype(jnp.bfloat16)


def units(image_embed, text_embed):
    out = jax.ShapeDtypeStruct(image_embed.shape, jnp.bfloat16)
    return pl.pallas_call(unit_kernel, out_shape=(out, out))(image_embed, text_embed)


def pair_kernel(rows, img_sizes, *refs):
    scalars_ref, refs = refs[0], refs[1:]
    img_refs, refs = refs[: len(img_sizes)], refs[len(img_sizes) :]
    txt_refs, refs = refs[:BAND], refs[BAND:]
    img_grad_ref, txt_grad_ref, loss_ref, img, txt = refs
    start = 0
    for ref, size in zip(img_refs, img_sizes):
        img[start : start + size, :] = ref[...]
        start += size
    for k, ref in enumerate(txt_refs):
        txt[k * rows : (k + 1) * rows, :] = ref[...]
    sharpness = scalars_ref[0]
    shift = scalars_ref[1]
    chunk = 2 * rows
    txt_grad_ref[...] = jnp.zeros_like(txt_grad_ref)
    loss_ref[...] = jnp.zeros_like(loss_ref)

    def step(i, carry):
        block = pl.ds(pl.multiple_of(i * chunk, chunk), chunk)
        images = img[block, :]
        score = sharpness * lax.dot_general(
            images, txt[...], (((1,), (1,)), ((), ())), preferred_element_type=jnp.float32
        ) + shift
        row = lax.broadcasted_iota(jnp.int32, score.shape, 0) + i * chunk
        column = lax.broadcasted_iota(jnp.int32, score.shape, 1)
        positive = jnp.logical_and(row == column, row < rows)
        decay = jnp.exp(-jnp.abs(score))
        softplus = jnp.maximum(jnp.where(positive, -score, score), 0.0) + jnp.log1p(decay)
        weight = jnp.where(score >= 0, 1.0, decay) / (1.0 + decay)
        weight = sharpness * (weight - jnp.where(positive, 1.0, 0.0))
        weight = weight.astype(jnp.bfloat16)
        loss_ref[...] += jnp.sum(softplus.reshape(-1, 8, softplus.shape[1]), axis=0)
        img_grad_ref[block, :] = jnp.dot(weight, txt[...], preferred_element_type=jnp.float32)
        txt_grad_ref[...] += lax.dot_general(
            weight, images, (((0,), (0,)), ((), ())), preferred_element_type=jnp.float32
        )
        return carry

    lax.fori_loop(0, img.shape[0] // chunk, step, 0)


def pair_terms(scalars, images, texts):
    rows, width = texts[0].shape
    sizes = tuple(block.shape[0] for block in images)
    total = sum(sizes)
    vmem = pl.BlockSpec(memory_space=pltpu.VMEM)
    return pl.pallas_call(
        functools.partial(pair_kernel, rows, sizes),
        out_shape=(
            jax.ShapeDtypeStruct((total, width), jnp.float32),
            jax.ShapeDtypeStruct((BAND * rows, width), jnp.float32),
            jax.ShapeDtypeStruct((8, BAND * rows), jnp.float32),
        ),
        in_specs=[pl.BlockSpec(memory_space=pltpu.SMEM)] + [vmem] * (len(images) + len(texts)),
        out_specs=(vmem, vmem, vmem),
        scratch_shapes=[
            pltpu.VMEM((total, width), jnp.bfloat16),
            pltpu.VMEM((BAND * rows, width), jnp.bfloat16),
        ],
        compiler_params=pltpu.CompilerParams(vmem_limit_bytes=56 * 1024 * 1024),
    )(scalars, *images, *texts)


def back_norm(embed, upstream):
    values = embed.astype(jnp.float32)
    inverse = lax.rsqrt(jnp.sum(values * values, axis=-1, keepdims=True) + EPS)
    inner = jnp.sum(values * upstream, axis=-1, keepdims=True)
    return inverse * upstream - inverse * inverse * inverse * values * inner


def narrow(block):
    return block.astype(jnp.float16)


def wide(block):
    return block.astype(jnp.float32)


def shards(image_embed, text_embed, log_sharpness_factor, couple_score_shift):
    rows = image_embed.shape[0]
    half = rows // 2
    site = lax.axis_index("site")
    second = (site % CORE) == 1
    upper = (site // CORE) % YH == 1
    scalars = jnp.stack([jnp.exp(log_sharpness_factor), couple_score_shift])
    own_img, own_txt = units(image_embed, text_embed)

    z_txt = move(own_txt, DOWN_Z)
    img_a = move(own_img, UP_X)
    img_b = move(own_img, DOWN_X)
    img_m = move(own_img, MATE_Y)
    y_txt = move(jnp.where(upper, own_txt, z_txt), FLIP_Y)
    img_2a = move(img_b[:half], DOWN_X)
    img_2b = move(img_a[half:], UP_X)
    img_ma = move(img_m, UP_X)
    img_mb = move(img_m, DOWN_X)
    img_m2a = move(img_2a, MATE_Y)
    img_m2b = move(img_2b, MATE_Y)
    c_txt = move(jnp.where(second, own_txt, z_txt), OTHER_CORE)
    d_txt = move(y_txt, OTHER_CORE)

    images = (own_img, img_a, img_b, img_m, img_2a, img_2b, img_ma, img_mb, img_m2a, img_m2b)
    texts = (own_txt, c_txt, y_txt, d_txt)
    img_terms, txt_terms, loss_part = pair_terms(scalars, images, texts)
    of_own, of_a, of_b, of_m, of_2, of_ma, of_mb, of_m2 = (
        img_terms[i * rows : (i + 1) * rows] for i in range(8)
    )
    of_txt, of_c, of_y, of_d = (txt_terms[i * rows : (i + 1) * rows] for i in range(4))

    got_c = wide(move(narrow(of_c), OTHER_CORE))
    got_d = wide(move(narrow(of_d), OTHER_CORE))
    got_m2 = wide(move(narrow(of_m2), MATE_Y))
    got_ma = wide(move(narrow(of_ma), DOWN_X))
    got_mb = wide(move(narrow(of_mb), UP_X))
    got_y = wide(move(narrow(of_y + got_d), FLIP_Y))
    sum_2 = narrow(of_2 + got_m2)
    got_2a = wide(move(sum_2[:half], UP_X))
    got_2b = wide(move(sum_2[half:], DOWN_X))
    got_m = wide(move(narrow(of_m + got_ma + got_mb), MATE_Y))
    for_z = jnp.where(second, 0.0, got_c) + jnp.where(upper, 0.0, got_y)
    got_z = wide(move(narrow(for_z), UP_Z))
    zeros = jnp.zeros((half, image_embed.shape[1]), jnp.float32)
    got_a = wide(move(narrow(of_a + jnp.concatenate([zeros, got_2b], 0)), DOWN_X))
    got_b = wide(move(narrow(of_b + jnp.concatenate([got_2a, zeros], 0)), UP_X))

    loss_sum = jnp.sum(loss_part.reshape(8, -1, 128), axis=1)
    for pairs in LOSS_ROUTES:
        loss_sum = loss_sum + move(loss_sum, pairs)
    pair_loss = jnp.sum(loss_sum) / jnp.float32(image_embed.shape[0] * 256 * BAND * rows * X * YL)
    img_grad = of_own + got_a + got_b + got_m
    txt_grad = of_txt + jnp.where(second, got_c, 0.0) + jnp.where(upper, got_y, 0.0) + got_z
    return pair_loss, back_norm(image_embed, img_grad), back_norm(text_embed, txt_grad)


def solution(mesh):
    return jax.shard_map(
        shards,
        mesh=mesh,
        in_specs=(P(AXES, None), P(AXES, None), P(), P()),
        out_specs=(P(), P(AXES, None), P(AXES, None)),
        check_vma=False,
    )
```

time: 578 us -> 120 us (0.21)
  waiting for transfers between devices: 353 us -> 45.9 us
  blocking collectives: 129 us -> 0 us
  matrix products: 37.8 us -> 0 us
  between operations: 19.8 us -> 4.07 us
  Pallas kernels: 0 us -> 13.7 us
  starting transfers between devices: 25.7 us -> 39.3 us
    ppermute x6 -> x33, waiting for transfers between devices: 292 us -> 45.9 us  [move(): return lax.ppermute(block, AXES, pairs)]
    psum x1 -> x0, blocking collectives: 129 us -> none  [shards(): loss_sum = lax.psum(loss_part, ('site', 'dp'))]
    all_gather x1 -> x0, waiting for transfers between devices: 61.3 us -> none  [shards(): own_group = lax.all_gather(txt_unit, 'dp', axis=0, tiled=True)]
    dot_general x12 -> x0, matrix products: 37.8 us -> none  [the longest x4 17.2 us: shards(): lax.dot_general(couple_weight_entry, img_unit, (((0,), (0,)), ((), ())),...]
    pallas_call x0 -> x2, Pallas kernels: none -> 13.7 us  [the longest x1 11.7 us: pair_terms(): pl.pallas_call(functools.partial(pair_kernel, rows, sizes), out_shape=(ja...]
    ppermute x6 -> x33, starting transfers between devices: 25.6 us -> 39.3 us  [move(): return lax.ppermute(block, AXES, pairs)]
  transfers between devices with their start and end apart: 8 -> 33, of which waited for: 6 -> 17; matrix products, arithmetic and copies ran while one was open for 4% -> 4% of each run, Pallas kernels for 0% -> 0%
where the time goes in v1:
time: 120 us; the launch traced here: 118 us
  waiting for transfers between devices  45.9 us (38%)
  starting transfers between devices  39.3 us (33%)
  Pallas kernels  13.7 us (11%)
  other arithmetic  13.7 us (11%)
  between operations  4.07 us (3%)
  local copies, waits for them, and re-layouts  1.79 us (1%)
    ppermute x33, waiting for transfers between devices, move(): return lax.ppermute(block, AXES, pairs)  45.9 us
    ppermute x33, starting transfers between devices, move(): return lax.ppermute(block, AXES, pairs)  39.3 us
    pallas_call x1, Pallas kernels, pair_terms(): pl.pallas_call(functools.partial(pair_kernel, rows, sizes), out_shape=(ja...  11.7 us
    sub x2, other arithmetic, back_norm(): return inverse * upstream - inverse * inverse * inverse * values * inner  4.52 us
    another operation x2, other arithmetic  2.89 us
  transfers between devices with their start and end apart: 33, of which 17 were waited for; matrix products, arithmetic and copies ran while one was open for 4% of the time, Pallas kernels for 0%

profile of v1, /device:TPU:24, one launch (start us, length us, event | category | flops | bytes accessed | tf_op | source)
XLA Modules:
  0.0 118.4 jit_solution(3006648062934448837)
XLA Ops:
  0.6 2.0 %shard_map.67 = (bf16[128,1152]{1,0:T(8,128)(2,1)}, bf16[128,1152]{1,0:T(8,128)(2,1)}) custom-call(bf16[128,1152]{1,0:T(8,128)(2,1)} %image_ref.1, bf16[128,1152]{1,0:T(8,128)(2,1)} %text_ref.1), custom_call_target="tpu_custom_call" | custom-call | tf_op jit(solution)/shard_map/pallas_call | solution.py:61
  2.6 5.9 %collective-permute-start.9 = (bf16[128,1152]{1,0:T(8,128)(2,1)}, bf16[128,1152]{1,0:T(8,128)(2,1)S(1)}, u32[]{:S(2)}, u32[]{:S(2)}) collective-permute-start(bf16[128,1152]{1,0:T(8,128)(2,1)} %get-tuple-element.9.refs_11_), channel_id=1, source_target_pairs={{0,224},{1,225},{2,226},{3,227},{4,228},{5,229},{6,230},{7,231},{8... | collective-permute-start | bytes 884744 | tf_op jit(solution)/shard_map/ppermute | solution.py:49
  8.5 1.5 %collective-permute-start = (bf16[128,1152]{1,0:T(8,128)(2,1)}, bf16[128,1152]{1,0:T(8,128)(2,1)S(1)}, u32[]{:S(2)}, u32[]{:S(2)}) collective-permute-start(bf16[128,1152]{1,0:T(8,128)(2,1)} %get-tuple-element.8.refs_1_), channel_id=1, source_target_pairs={{0,2},{1,3},{2,4},{3,5},{4,6},{5,7},{6,0},{7,1},{8,10},{9,11},{10,... | collective-permute-start | bytes 884744 | tf_op jit(solution)/shard_map/ppermute | solution.py:49
  10.0 1.7 %collective-permute-start.1 = (bf16[128,1152]{1,0:T(8,128)(2,1)}, bf16[128,1152]{1,0:T(8,128)(2,1)S(1)}, u32[]{:S(2)}, u32[]{:S(2)}) collective-permute-start(bf16[128,1152]{1,0:T(8,128)(2,1)} %get-tuple-element.8.refs_1_), channel_id=1, source_target_pairs={{0,6},{1,7},{2,0},{3,1},{4,2},{5,3},{6,4},{7,5},{8,14},{9,15},{10,... | collective-permute-start | bytes 884744 | tf_op jit(solution)/shard_map/ppermute | solution.py:49
  12.5 2.6 %collective-permute-done.9 = bf16[128,1152]{1,0:T(8,128)(2,1)S(1)} collective-permute-done((bf16[128,1152]{1,0:T(8,128)(2,1)}, bf16[128,1152]{1,0:T(8,128)(2,1)S(1)}, u32[]{:S(2)}, u32[]{:S(2)}) %collective-permute-start.9) | collective-permute-done | bytes 294944 | tf_op jit(solution)/shard_map/ppermute | solution.py:49
  16.4 2.0 %collective-permute-done.1.refs_3_ = bf16[128,1152]{1,0:T(8,128)(2,1)S(1)} collective-permute-done((bf16[128,1152]{1,0:T(8,128)(2,1)}, bf16[128,1152]{1,0:T(8,128)(2,1)S(1)}, u32[]{:S(2)}, u32[]{:S(2)}) %collective-permute-start.1) | collective-permute-done | bytes 294944 | tf_op jit(solution)/shard_map/ppermute | solution.py:49
  18.4 3.0 %collective-permute-start.3 = (bf16[64,1152]{1,0:T(8,128)(2,1)S(1)}, bf16[64,1152]{1,0:T(8,128)(2,1)S(1)}, u32[]{:S(2)}, u32[]{:S(2)}) collective-permute-start(bf16[64,1152]{1,0:T(8,128)(2,1)S(1)} %slice.69), channel_id=1, source_target_pairs={{0,6},{1,7},{2,0},{3,1},{4,2},{5,3},{6,4},{7,5},{8,14},{9,15},{10,... | collective-permute-start | bytes 442376 | tf_op jit(solution)/shard_map/ppermute | solution.py:49
  22.1 2.8 %collective-permute-start.6 = (bf16[128,1152]{1,0:T(8,128)(2,1)S(1)}, bf16[128,1152]{1,0:T(8,128)(2,1)S(1)}, u32[]{:S(2)}, u32[]{:S(2)}) collective-permute-start(bf16[128,1152]{1,0:T(8,128)(2,1)S(1)} %collective-permute-done.2.refs_4_), channel_id=1, source_target_pairs={{0,6},{1,7},{2,0},{3,1},{4,2},{5,3},{6,4},{7,5},{8,14},{9,15},{10,... | collective-permute-start | bytes 884744 | tf_op jit(solution)/shard_map/ppermute | solution.py:49
  26.0 6.8 %collective-permute-done.4.refs_6_ = bf16[64,1152]{1,0:T(8,128)(2,1)S(1)} collective-permute-done((bf16[64,1152]{1,0:T(8,128)(2,1)S(1)}, bf16[64,1152]{1,0:T(8,128)(2,1)S(1)}, u32[]{:S(2)}, u32[]{:S(2)}) %collective-permute-start.4) | collective-permute-done | bytes 147488 | tf_op jit(solution)/shard_map/ppermute | solution.py:49
  33.6 1.3 %collective-permute-start.8 = (bf16[64,1152]{1,0:T(8,128)(2,1)S(1)}, bf16[64,1152]{1,0:T(8,128)(2,1)S(1)}, u32[]{:S(2)}, u32[]{:S(2)}) collective-permute-start(bf16[64,1152]{1,0:T(8,128)(2,1)S(1)} %collective-permute-done.4.refs_6_), channel_id=1, source_target_pairs={{0,1},{1,0},{2,3},{3,2},{4,5},{5,4},{6,7},{7,6},{8,9},{9,8},{10,11... | collective-permute-start | bytes 442376 | tf_op jit(solution)/shard_map/ppermute | solution.py:49
  38.0 1.6 %collective-permute-done.8.refs_10_ = bf16[64,1152]{1,0:T(8,128)(2,1)S(1)} collective-permute-done((bf16[64,1152]{1,0:T(8,128)(2,1)S(1)}, bf16[64,1152]{1,0:T(8,128)(2,1)S(1)}, u32[]{:S(2)}, u32[]{:S(2)}) %collective-permute-start.8) | collective-permute-done | bytes 147488 | tf_op jit(solution)/shard_map/ppermute | solution.py:49
  41.0 11.7 %shard_map.68 = (f32[1024,1152]{1,0:T(8,128)}, f32[512,1152]{1,0:T(8,128)}, f32[8,512]{1,0:T(8,128)}) custom-call(f32[2]{0:T(128)} %pad_maximum_fusion.refs_0_, bf16[128,1152]{1,0:T(8,128)(2,1)} %get-tuple-element.8.refs_1_, bf16[128,1152]{1,0:T(8,128)(2,1)} %copy-done.4, bf16[128,1152]{1,0:T(8,128)(2,1)} %copy-done.5, bf16[128,1152]{1,0:T(8,128)(2,1)} %copy-done.6, ...), custom_call_target="tpu_custom_call" | custom-call | tf_op jit(solution)/shard_map/pallas_call | solution.py:110
  52.7 2.8 %convert.13 = f16[1024,1152]{1,0:T(8,128)(2,1)S(1)} convert(f32[1024,1152]{1,0:T(8,128)} %get-tuple-element.11) | non-fusion elementwise | flops 1179648 | bytes 7077888 | tf_op jit(solution)/shard_map/convert.8
  56.6 3.2 %collective-permute-start.26 = (f16[128,1152]{1,0:T(8,128)(2,1)S(1)}, f16[128,1152]{1,0:T(8,128)(2,1)S(1)}, u32[]{:S(2)}, u32[]{:S(2)}) collective-permute-start(f16[128,1152]{1,0:T(8,128)(2,1)S(1)} %get-tuple-element.22), channel_id=1, source_target_pairs={{0,6},{1,7},{2,0},{3,1},{4,2},{5,3},{6,4},{7,5},{8,14},{9,15},{10,... | collective-permute-start | bytes 884744 | tf_op jit(solution)/shard_map/ppermute | solution.py:49
  60.7 1.9 %collective-permute-done.21 = f16[128,1152]{1,0:T(8,128)(2,1)S(1)} collective-permute-done((f16[128,1152]{1,0:T(8,128)(2,1)S(1)}, f16[128,1152]{1,0:T(8,128)(2,1)S(1)}, u32[]{:S(2)}, u32[]{:S(2)}) %collective-permute-start.21) | collective-permute-done | bytes 294944 | tf_op jit(solution)/shard_map/ppermute | solution.py:49
  62.9 2.0 %collective-permute-start.24 = (f16[64,1152]{1,0:T(8,128)(2,1)S(1)}, f16[64,1152]{1,0:T(8,128)(2,1)S(1)}, u32[]{:S(2)}, u32[]{:S(2)}) collective-permute-start(f16[64,1152]{1,0:T(8,128)(2,1)S(1)} %get-tuple-element.28), channel_id=1, source_target_pairs={{0,2},{1,3},{2,4},{3,5},{4,6},{5,7},{6,0},{7,1},{8,10},{9,11},{10,... | collective-permute-start | bytes 442376 | tf_op jit(solution)/shard_map/ppermute | solution.py:49
  66.3 1.7 %collective-permute-done.22 = f16[64,1152]{1,0:T(8,128)(2,1)S(1)} collective-permute-done((f16[64,1152]{1,0:T(8,128)(2,1)S(1)}, f16[64,1152]{1,0:T(8,128)(2,1)S(1)}, u32[]{:S(2)}, u32[]{:S(2)}) %collective-permute-start.22) | collective-permute-done | bytes 147488 | tf_op jit(solution)/shard_map/ppermute | solution.py:49
  68.0 1.3 %collective-permute-done.24 = f16[64,1152]{1,0:T(8,128)(2,1)S(1)} collective-permute-done((f16[64,1152]{1,0:T(8,128)(2,1)S(1)}, f16[64,1152]{1,0:T(8,128)(2,1)S(1)}, u32[]{:S(2)}, u32[]{:S(2)}) %collective-permute-start.24) | collective-permute-done | bytes 147488 | tf_op jit(solution)/shard_map/ppermute | solution.py:49
  70.4 1.3 %collective-permute-start.28 = (f16[128,1152]{1,0:T(8,128)(2,1)}, f16[128,1152]{1,0:T(8,128)(2,1)}, u32[]{:S(2)}, u32[]{:S(2)}) collective-permute-start(f16[128,1152]{1,0:T(8,128)(2,1)} %get-tuple-element.18), channel_id=1, source_target_pairs={{0,1},{1,0},{2,3},{3,2},{4,5},{5,4},{6,7},{7,6},{8,9},{9,8},{10,11... | collective-permute-start | bytes 884744 | tf_op jit(solution)/shard_map/ppermute | solution.py:49
  71.9 2.9 %collective-permute-start.23 = (f16[128,1152]{1,0:T(8,128)(2,1)}, f16[128,1152]{1,0:T(8,128)(2,1)}, u32[]{:S(2)}, u32[]{:S(2)}) collective-permute-start(f16[128,1152]{1,0:T(8,128)(2,1)} %get-tuple-element.17), channel_id=1, source_target_pairs={{0,6},{1,7},{2,0},{3,1},{4,2},{5,3},{6,4},{7,5},{8,14},{9,15},{10,... | collective-permute-start | bytes 884744 | tf_op jit(solution)/shard_map/ppermute | solution.py:49
  77.0 3.6 %collective-permute-done.14 = f32[8,128]{1,0:T(8,128)S(1)} collective-permute-done((f32[8,128]{1,0:T(8,128)S(1)}, f32[8,128]{1,0:T(8,128)S(1)}, u32[]{:S(2)}, u32[]{:S(2)}) %collective-permute-start.14) | collective-permute-done | bytes 4128 | tf_op jit(solution)/shard_map/ppermute | solution.py:49
  81.4 4.0 %collective-permute-done.15 = f32[8,128]{1,0:T(8,128)S(1)} collective-permute-done((f32[8,128]{1,0:T(8,128)S(1)}, f32[8,128]{1,0:T(8,128)S(1)}, u32[]{:S(2)}, u32[]{:S(2)}) %collective-permute-start.15) | collective-permute-done | bytes 4128 | tf_op jit(solution)/shard_map/ppermute | solution.py:49
  86.2 2.9 %collective-permute-done.16 = f32[8,128]{1,0:T(8,128)S(1)} collective-permute-done((f32[8,128]{1,0:T(8,128)S(1)}, f32[8,128]{1,0:T(8,128)S(1)}, u32[]{:S(2)}, u32[]{:S(2)}) %collective-permute-start.16) | collective-permute-done | bytes 4128 | tf_op jit(solution)/shard_map/ppermute | solution.py:49
  90.2 3.6 %collective-permute-done.17 = f32[8,128]{1,0:T(8,128)S(1)} collective-permute-done((f32[8,128]{1,0:T(8,128)S(1)}, f32[8,128]{1,0:T(8,128)S(1)}, u32[]{:S(2)}, u32[]{:S(2)}) %collective-permute-start.17) | collective-permute-done | bytes 4128 | tf_op jit(solution)/shard_map/ppermute | solution.py:49
  93.9 3.6 %collective-permute-done.18 = f32[8,128]{1,0:T(8,128)S(1)} collective-permute-done((f32[8,128]{1,0:T(8,128)S(1)}, f32[8,128]{1,0:T(8,128)S(1)}, u32[]{:S(2)}, u32[]{:S(2)}) %collective-permute-start.18) | collective-permute-done | bytes 4128 | tf_op jit(solution)/shard_map/ppermute | solution.py:49
  97.5 1.4 %collective-permute-start.19 = (f32[8,128]{1,0:T(8,128)S(1)}, f32[8,128]{1,0:T(8,128)S(1)}, u32[]{:S(2)}, u32[]{:S(2)}) collective-permute-start(f32[8,128]{1,0:T(8,128)S(1)} %add.104), channel_id=1, source_target_pairs={{0,64},{1,65},{2,66},{3,67},{4,68},{5,69},{6,70},{7,71},{8,72},{9,... | collective-permute-start | bytes 12296 | tf_op jit(solution)/shard_map/ppermute | solution.py:49
  98.9 3.1 %collective-permute-done.19 = f32[8,128]{1,0:T(8,128)S(1)} collective-permute-done((f32[8,128]{1,0:T(8,128)S(1)}, f32[8,128]{1,0:T(8,128)S(1)}, u32[]{:S(2)}, u32[]{:S(2)}) %collective-permute-start.19) | collective-permute-done | bytes 4128 | tf_op jit(solution)/shard_map/ppermute | solution.py:49
  102.0 3.3 %collective-permute-start.20 = (f32[8,128]{1,0:T(8,128)S(1)}, f32[8,128]{1,0:T(8,128)S(1)}, u32[]{:S(2)}, u32[]{:S(2)}) collective-permute-start(f32[8,128]{1,0:T(8,128)S(1)} %add.105), channel_id=1, source_target_pairs={{0,128},{1,129},{2,130},{3,131},{4,132},{5,133},{6,134},{7,135},{8... | collective-permute-start | bytes 12296 | tf_op jit(solution)/shard_map/ppermute | solution.py:49
  105.3 4.2 %collective-permute-done.20 = f32[8,128]{1,0:T(8,128)S(1)} collective-permute-done((f32[8,128]{1,0:T(8,128)S(1)}, f32[8,128]{1,0:T(8,128)S(1)}, u32[]{:S(2)}, u32[]{:S(2)}) %collective-permute-start.20) | collective-permute-done | bytes 4128 | tf_op jit(solution)/shard_map/ppermute | solution.py:49
  110.8 1.9 %fusion.5 = (f32[128]{0:T(128)S(1)}, f32[128]{0:T(128)S(1)}, f32[128]{0:T(128)S(1)}, f32[128]{0:T(128)S(1)}) fusion(bf16[128,1152]{1,0:T(8,128)(2,1)S(1)} %copy-done.2, f16[128,1152]{1,0:T(8,128)(2,1)} %collective-permute-done.28, f16[128,1152]{1,0:T(8,128)(2,1)} %collective-permute-done.25, f16[128,1152]{1,0:T(8,128)(2,1)} %collective-permute-done.23, ...), kind=kLoop, calls=%fused_computation.15 | loop fusion | flops 3538432 | bytes 3540994 | tf_op jit(solution)/shard_map/reduce_sum | solution.py:129
  112.8 2.4 %fusion.7 = f32[128,1152]{1,0:T(8,128)} fusion(bf16[128,1152]{1,0:T(8,128)(2,1)S(1)} %copy-done.2, f32[128]{0:T(128)S(1)} %get-tuple-element.16, f32[128]{0:T(128)S(1)} %get-tuple-element.32, f32[128]{0:T(128)S(1)} %get-tuple-element.31, f16[128,1152]{1,0:T(8,128)(2,1)} %collective-permute-done.28, f16[128,1152]{1,0:T(8,128)(2,1)} %collective-permute-done.25, ...), kind=kLoop, calls=%fused_computation.17 | loop fusion | flops 1622016 | bytes 2360832 | tf_op jit(solution)/shard_map/sub | solution.py:131
  115.2 2.1 %fusion.11 = f32[128,1152]{1,0:T(8,128)} fusion(bf16[128,1152]{1,0:T(8,128)(2,1)S(1)} %copy-done.3, f32[128]{0:T(128)S(1)} %get-tuple-element.33, f32[128]{0:T(128)S(1)} %get-tuple-element.30, f32[128]{0:T(128)S(1)} %get-tuple-element.29, f16[128,1152]{1,0:T(8,128)(2,1)} %collective-permute-done.32, f16[128,1152]{1,0:T(8,128)(2,1)S(1)} %collective-permute-done.31, ...), kind=kLoop, calls=%fused_computation.21 | loop fusion | flops 1916928 | bytes 2360834 | tf_op jit(solution)/shard_map/sub | solution.py:131
  (97 shorter events, 18.1 us)
Async XLA Ops:
  2.6 12.4 %collective-permute-start.9 = (bf16[128,1152]{1,0:T(8,128)(2,1)}, bf16[128,1152]{1,0:T(8,128)(2,1)S(1)}, u32[]{:S(2)}, u32[]{:S(2)}) collective-permute-start(bf16[128,1152]{1,0:T(8,128)(2,1)} %get-tuple-element.9.refs_11_), channel_id=1, source_target_pairs={{0,224},{1,225},{2,226},{3,227},{4,228},{5,229},{6,230},{7,231},{8... | collective-permute-start | bytes 884744 | tf_op jit(solution)/shard_map/ppermute | solution.py:49
  8.5 13.0 %collective-permute-start = (bf16[128,1152]{1,0:T(8,128)(2,1)}, bf16[128,1152]{1,0:T(8,128)(2,1)S(1)}, u32[]{:S(2)}, u32[]{:S(2)}) collective-permute-start(bf16[128,1152]{1,0:T(8,128)(2,1)} %get-tuple-element.8.refs_1_), channel_id=1, source_target_pairs={{0,2},{1,3},{2,4},{3,5},{4,6},{5,7},{6,0},{7,1},{8,10},{9,11},{10,... | collective-permute-start | bytes 884744 | tf_op jit(solution)/shard_map/ppermute | solution.py:49
  10.0 8.4 %collective-permute-start.1 = (bf16[128,1152]{1,0:T(8,128)(2,1)}, bf16[128,1152]{1,0:T(8,128)(2,1)S(1)}, u32[]{:S(2)}, u32[]{:S(2)}) collective-permute-start(bf16[128,1152]{1,0:T(8,128)(2,1)} %get-tuple-element.8.refs_1_), channel_id=1, source_target_pairs={{0,6},{1,7},{2,0},{3,1},{4,2},{5,3},{6,4},{7,5},{8,14},{9,15},{10,... | collective-permute-start | bytes 884744 | tf_op jit(solution)/shard_map/ppermute | solution.py:49
  11.7 9.7 %collective-permute-start.2 = (bf16[128,1152]{1,0:T(8,128)(2,1)}, bf16[128,1152]{1,0:T(8,128)(2,1)S(1)}, u32[]{:S(2)}, u32[]{:S(2)}) collective-permute-start(bf16[128,1152]{1,0:T(8,128)(2,1)} %get-tuple-element.8.refs_1_), channel_id=1, source_target_pairs={{0,1},{1,0},{2,3},{3,2},{4,5},{5,4},{6,7},{7,6},{8,9},{9,8},{10,11... | collective-permute-start | bytes 884744 | tf_op jit(solution)/shard_map/ppermute | solution.py:49
  16.1 9.3 %collective-permute-start.11 = (bf16[128,1152]{1,0:T(8,128)(2,1)S(1)}, bf16[128,1152]{1,0:T(8,128)(2,1)S(1)}, u32[]{:S(2)}, u32[]{:S(2)}) collective-permute-start(bf16[128,1152]{1,0:T(8,128)(2,1)S(1)} %get-tuple-element.25), channel_id=1, source_target_pairs={{0,17},{1,16},{2,19},{3,18},{4,21},{5,20},{6,23},{7,22},{8,25},{9,... | collective-permute-start | bytes 884744 | tf_op jit(solution)/shard_map/ppermute | solution.py:49
  18.4 7.0 %collective-permute-start.3 = (bf16[64,1152]{1,0:T(8,128)(2,1)S(1)}, bf16[64,1152]{1,0:T(8,128)(2,1)S(1)}, u32[]{:S(2)}, u32[]{:S(2)}) collective-permute-start(bf16[64,1152]{1,0:T(8,128)(2,1)S(1)} %slice.69), channel_id=1, source_target_pairs={{0,6},{1,7},{2,0},{3,1},{4,2},{5,3},{6,4},{7,5},{8,14},{9,15},{10,... | collective-permute-start | bytes 442376 | tf_op jit(solution)/shard_map/ppermute | solution.py:49
  21.4 12.1 %collective-permute-start.5 = (bf16[128,1152]{1,0:T(8,128)(2,1)S(1)}, bf16[128,1152]{1,0:T(8,128)(2,1)S(1)}, u32[]{:S(2)}, u32[]{:S(2)}) collective-permute-start(bf16[128,1152]{1,0:T(8,128)(2,1)S(1)} %collective-permute-done.2.refs_4_), channel_id=1, source_target_pairs={{0,2},{1,3},{2,4},{3,5},{4,6},{5,7},{6,0},{7,1},{8,10},{9,11},{10,... | collective-permute-start | bytes 884744 | tf_op jit(solution)/shard_map/ppermute | solution.py:49
  21.5 11.3 %collective-permute-start.4 = (bf16[64,1152]{1,0:T(8,128)(2,1)S(1)}, bf16[64,1152]{1,0:T(8,128)(2,1)S(1)}, u32[]{:S(2)}, u32[]{:S(2)}) collective-permute-start(bf16[64,1152]{1,0:T(8,128)(2,1)S(1)} %slice.70), channel_id=1, source_target_pairs={{0,2},{1,3},{2,4},{3,5},{4,6},{5,7},{6,0},{7,1},{8,10},{9,11},{10,... | collective-permute-start | bytes 442376 | tf_op jit(solution)/shard_map/ppermute | solution.py:49
  22.1 14.7 %collective-permute-start.6 = (bf16[128,1152]{1,0:T(8,128)(2,1)S(1)}, bf16[128,1152]{1,0:T(8,128)(2,1)S(1)}, u32[]{:S(2)}, u32[]{:S(2)}) collective-permute-start(bf16[128,1152]{1,0:T(8,128)(2,1)S(1)} %collective-permute-done.2.refs_4_), channel_id=1, source_target_pairs={{0,6},{1,7},{2,0},{3,1},{4,2},{5,3},{6,4},{7,5},{8,14},{9,15},{10,... | collective-permute-start | bytes 884744 | tf_op jit(solution)/shard_map/ppermute | solution.py:49
  25.4 14.1 %collective-permute-start.10 = (bf16[128,1152]{1,0:T(8,128)(2,1)S(1)}, bf16[128,1152]{1,0:T(8,128)(2,1)S(1)}, u32[]{:S(2)}, u32[]{:S(2)}) collective-permute-start(bf16[128,1152]{1,0:T(8,128)(2,1)S(1)} %get-tuple-element.26), channel_id=1, source_target_pairs={{0,8},{1,9},{2,10},{3,11},{4,12},{5,13},{6,14},{7,15},{8,0},{9,1},... | collective-permute-start | bytes 884744 | tf_op jit(solution)/shard_map/ppermute | solution.py:49
  25.4 14.1 %collective-permute-start.12 = (bf16[128,1152]{1,0:T(8,128)(2,1)S(1)}, bf16[128,1152]{1,0:T(8,128)(2,1)S(1)}, u32[]{:S(2)}, u32[]{:S(2)}) collective-permute-start(bf16[128,1152]{1,0:T(8,128)(2,1)S(1)} %collective-permute-done.11.refs_13_), channel_id=1, source_target_pairs={{0,8},{1,9},{2,10},{3,11},{4,12},{5,13},{6,14},{7,15},{8,0},{9,1},... | collective-permute-start | bytes 884744 | tf_op jit(solution)/shard_map/ppermute | solution.py:49
  32.8 5.1 %collective-permute-start.7 = (bf16[64,1152]{1,0:T(8,128)(2,1)S(1)}, bf16[64,1152]{1,0:T(8,128)(2,1)S(1)}, u32[]{:S(2)}, u32[]{:S(2)}) collective-permute-start(bf16[64,1152]{1,0:T(8,128)(2,1)S(1)} %collective-permute-done.3.refs_5_), channel_id=1, source_target_pairs={{0,1},{1,0},{2,3},{3,2},{4,5},{5,4},{6,7},{7,6},{8,9},{9,8},{10,11... | collective-permute-start | bytes 442376 | tf_op jit(solution)/shard_map/ppermute | solution.py:49
  33.6 6.0 %collective-permute-start.8 = (bf16[64,1152]{1,0:T(8,128)(2,1)S(1)}, bf16[64,1152]{1,0:T(8,128)(2,1)S(1)}, u32[]{:S(2)}, u32[]{:S(2)}) collective-permute-start(bf16[64,1152]{1,0:T(8,128)(2,1)S(1)} %collective-permute-done.4.refs_6_), channel_id=1, source_target_pairs={{0,1},{1,0},{2,3},{3,2},{4,5},{5,4},{6,7},{7,6},{8,9},{9,8},{10,11... | collective-permute-start | bytes 442376 | tf_op jit(solution)/shard_map/ppermute | solution.py:49
  55.6 7.0 %collective-permute-start.21 = (f16[128,1152]{1,0:T(8,128)(2,1)S(1)}, f16[128,1152]{1,0:T(8,128)(2,1)S(1)}, u32[]{:S(2)}, u32[]{:S(2)}) collective-permute-start(f16[128,1152]{1,0:T(8,128)(2,1)S(1)} %get-tuple-element.20), channel_id=1, source_target_pairs={{0,1},{1,0},{2,3},{3,2},{4,5},{5,4},{6,7},{7,6},{8,9},{9,8},{10,11... | collective-permute-start | bytes 884744 | tf_op jit(solution)/shard_map/ppermute | solution.py:49
  56.6 8.4 %collective-permute-start.27 = (f16[128,1152]{1,0:T(8,128)(2,1)S(1)}, f16[128,1152]{1,0:T(8,128)(2,1)S(1)}, u32[]{:S(2)}, u32[]{:S(2)}) collective-permute-start(f16[128,1152]{1,0:T(8,128)(2,1)S(1)} %get-tuple-element.21), channel_id=1, source_target_pairs={{0,2},{1,3},{2,4},{3,5},{4,6},{5,7},{6,0},{7,1},{8,10},{9,11},{10,... | collective-permute-start | bytes 884744 | tf_op jit(solution)/shard_map/ppermute | solution.py:49
  56.6 9.6 %collective-permute-start.26 = (f16[128,1152]{1,0:T(8,128)(2,1)S(1)}, f16[128,1152]{1,0:T(8,128)(2,1)S(1)}, u32[]{:S(2)}, u32[]{:S(2)}) collective-permute-start(f16[128,1152]{1,0:T(8,128)(2,1)S(1)} %get-tuple-element.22), channel_id=1, source_target_pairs={{0,6},{1,7},{2,0},{3,1},{4,2},{5,3},{6,4},{7,5},{8,14},{9,15},{10,... | collective-permute-start | bytes 884744 | tf_op jit(solution)/shard_map/ppermute | solution.py:49
  60.1 14.8 %collective-permute-start.29 = (f16[128,1152]{1,0:T(8,128)(2,1)S(1)}, f16[128,1152]{1,0:T(8,128)(2,1)S(1)}, u32[]{:S(2)}, u32[]{:S(2)}) collective-permute-start(f16[128,1152]{1,0:T(8,128)(2,1)S(1)} %get-tuple-element.24), channel_id=1, source_target_pairs={{0,8},{1,9},{2,10},{3,11},{4,12},{5,13},{6,14},{7,15},{8,0},{9,1},... | collective-permute-start | bytes 884744 | tf_op jit(solution)/shard_map/ppermute | solution.py:49
  60.2 2.6 %collective-permute-start.30 = (f16[128,1152]{1,0:T(8,128)(2,1)S(1)}, f16[128,1152]{1,0:T(8,128)(2,1)S(1)}, u32[]{:S(2)}, u32[]{:S(2)}) collective-permute-start(f16[128,1152]{1,0:T(8,128)(2,1)S(1)} %get-tuple-element.23), channel_id=1, source_target_pairs={{0,8},{1,9},{2,10},{3,11},{4,12},{5,13},{6,14},{7,15},{8,0},{9,1},... | collective-permute-start | bytes 884744 | tf_op jit(solution)/shard_map/ppermute | solution.py:49
  62.8 5.2 %collective-permute-start.22 = (f16[64,1152]{1,0:T(8,128)(2,1)S(1)}, f16[64,1152]{1,0:T(8,128)(2,1)S(1)}, u32[]{:S(2)}, u32[]{:S(2)}) collective-permute-start(f16[64,1152]{1,0:T(8,128)(2,1)S(1)} %get-tuple-element.27), channel_id=1, source_target_pairs={{0,6},{1,7},{2,0},{3,1},{4,2},{5,3},{6,4},{7,5},{8,14},{9,15},{10,... | collective-permute-start | bytes 442376 | tf_op jit(solution)/shard_map/ppermute | solution.py:49
  62.9 6.4 %collective-permute-start.24 = (f16[64,1152]{1,0:T(8,128)(2,1)S(1)}, f16[64,1152]{1,0:T(8,128)(2,1)S(1)}, u32[]{:S(2)}, u32[]{:S(2)}) collective-permute-start(f16[64,1152]{1,0:T(8,128)(2,1)S(1)} %get-tuple-element.28), channel_id=1, source_target_pairs={{0,2},{1,3},{2,4},{3,5},{4,6},{5,7},{6,0},{7,1},{8,10},{9,11},{10,... | collective-permute-start | bytes 442376 | tf_op jit(solution)/shard_map/ppermute | solution.py:49
  65.0 9.9 %collective-permute-start.31 = (f16[128,1152]{1,0:T(8,128)(2,1)S(1)}, f16[128,1152]{1,0:T(8,128)(2,1)S(1)}, u32[]{:S(2)}, u32[]{:S(2)}) collective-permute-start(f16[128,1152]{1,0:T(8,128)(2,1)S(1)} %add_convert_fusion), channel_id=1, source_target_pairs={{0,17},{1,16},{2,19},{3,18},{4,21},{5,20},{6,23},{7,22},{8,25},{9,... | collective-permute-start | bytes 884744 | tf_op jit(solution)/shard_map/ppermute | solution.py:49
  70.4 40.4 %collective-permute-start.28 = (f16[128,1152]{1,0:T(8,128)(2,1)}, f16[128,1152]{1,0:T(8,128)(2,1)}, u32[]{:S(2)}, u32[]{:S(2)}) collective-permute-start(f16[128,1152]{1,0:T(8,128)(2,1)} %get-tuple-element.18), channel_id=1, source_target_pairs={{0,1},{1,0},{2,3},{3,2},{4,5},{5,4},{6,7},{7,6},{8,9},{9,8},{10,11... | collective-permute-start | bytes 884744 | tf_op jit(solution)/shard_map/ppermute | solution.py:49
  71.6 39.1 %collective-permute-start.25 = (f16[128,1152]{1,0:T(8,128)(2,1)}, f16[128,1152]{1,0:T(8,128)(2,1)}, u32[]{:S(2)}, u32[]{:S(2)}) collective-permute-start(f16[128,1152]{1,0:T(8,128)(2,1)} %get-tuple-element.19), channel_id=1, source_target_pairs={{0,2},{1,3},{2,4},{3,5},{4,6},{5,7},{6,0},{7,1},{8,10},{9,11},{10,... | collective-permute-start | bytes 884744 | tf_op jit(solution)/shard_map/ppermute | solution.py:49
  71.9 38.8 %collective-permute-start.23 = (f16[128,1152]{1,0:T(8,128)(2,1)}, f16[128,1152]{1,0:T(8,128)(2,1)}, u32[]{:S(2)}, u32[]{:S(2)}) collective-permute-start(f16[128,1152]{1,0:T(8,128)(2,1)} %get-tuple-element.17), channel_id=1, source_target_pairs={{0,6},{1,7},{2,0},{3,1},{4,2},{5,3},{6,4},{7,5},{8,14},{9,15},{10,... | collective-permute-start | bytes 884744 | tf_op jit(solution)/shard_map/ppermute | solution.py:49
  75.7 35.1 %collective-permute-start.32 = (f16[128,1152]{1,0:T(8,128)(2,1)}, f16[128,1152]{1,0:T(8,128)(2,1)}, u32[]{:S(2)}, u32[]{:S(2)}) collective-permute-start(f16[128,1152]{1,0:T(8,128)(2,1)} %fusion.4), channel_id=1, source_target_pairs={{0,32},{1,33},{2,34},{3,35},{4,36},{5,37},{6,38},{7,39},{8,40},{9,... | collective-permute-start | bytes 884744 | tf_op jit(solution)/shard_map/ppermute | solution.py:49
  77.0 3.6 %collective-permute-start.14 = (f32[8,128]{1,0:T(8,128)S(1)}, f32[8,128]{1,0:T(8,128)S(1)}, u32[]{:S(2)}, u32[]{:S(2)}) collective-permute-start(f32[8,128]{1,0:T(8,128)S(1)} %add.99), channel_id=1, source_target_pairs={{0,2},{1,3},{2,0},{3,1},{4,6},{5,7},{6,4},{7,5},{8,10},{9,11},{10,... | collective-permute-start | bytes 12296 | tf_op jit(solution)/shard_map/ppermute | solution.py:49
  80.6 4.8 %collective-permute-start.15 = (f32[8,128]{1,0:T(8,128)S(1)}, f32[8,128]{1,0:T(8,128)S(1)}, u32[]{:S(2)}, u32[]{:S(2)}) collective-permute-start(f32[8,128]{1,0:T(8,128)S(1)} %add.100), channel_id=1, source_target_pairs={{0,6},{1,7},{2,4},{3,5},{4,2},{5,3},{6,0},{7,1},{8,14},{9,15},{10,... | collective-permute-start | bytes 12296 | tf_op jit(solution)/shard_map/ppermute | solution.py:49
  85.4 3.6 %collective-permute-start.16 = (f32[8,128]{1,0:T(8,128)S(1)}, f32[8,128]{1,0:T(8,128)S(1)}, u32[]{:S(2)}, u32[]{:S(2)}) collective-permute-start(f32[8,128]{1,0:T(8,128)S(1)} %add.101), channel_id=1, source_target_pairs={{0,1},{1,0},{2,3},{3,2},{4,5},{5,4},{6,7},{7,6},{8,9},{9,8},{10,11... | collective-permute-start | bytes 12296 | tf_op jit(solution)/shard_map/ppermute | solution.py:49
  89.0 4.8 %collective-permute-start.17 = (f32[8,128]{1,0:T(8,128)S(1)}, f32[8,128]{1,0:T(8,128)S(1)}, u32[]{:S(2)}, u32[]{:S(2)}) collective-permute-start(f32[8,128]{1,0:T(8,128)S(1)} %add.102), channel_id=1, source_target_pairs={{0,17},{1,16},{2,19},{3,18},{4,21},{5,20},{6,23},{7,22},{8,25},{9,... | collective-permute-start | bytes 12296 | tf_op jit(solution)/shard_map/ppermute | solution.py:49
  93.9 3.6 %collective-permute-start.18 = (f32[8,128]{1,0:T(8,128)S(1)}, f32[8,128]{1,0:T(8,128)S(1)}, u32[]{:S(2)}, u32[]{:S(2)}) collective-permute-start(f32[8,128]{1,0:T(8,128)S(1)} %add.103), channel_id=1, source_target_pairs={{0,32},{1,33},{2,34},{3,35},{4,36},{5,37},{6,38},{7,39},{8,40},{9,... | collective-permute-start | bytes 12296 | tf_op jit(solution)/shard_map/ppermute | solution.py:49
  97.5 4.5 %collective-permute-start.19 = (f32[8,128]{1,0:T(8,128)S(1)}, f32[8,128]{1,0:T(8,128)S(1)}, u32[]{:S(2)}, u32[]{:S(2)}) collective-permute-start(f32[8,128]{1,0:T(8,128)S(1)} %add.104), channel_id=1, source_target_pairs={{0,64},{1,65},{2,66},{3,67},{4,68},{5,69},{6,70},{7,71},{8,72},{9,... | collective-permute-start | bytes 12296 | tf_op jit(solution)/shard_map/ppermute | solution.py:49
  102.0 7.5 %collective-permute-start.20 = (f32[8,128]{1,0:T(8,128)S(1)}, f32[8,128]{1,0:T(8,128)S(1)}, u32[]{:S(2)}, u32[]{:S(2)}) collective-permute-start(f32[8,128]{1,0:T(8,128)S(1)} %add.105), channel_id=1, source_target_pairs={{0,128},{1,129},{2,130},{3,131},{4,132},{5,133},{6,134},{7,135},{8... | collective-permute-start | bytes 12296 | tf_op jit(solution)/shard_map/ppermute | solution.py:49
  (18 other events, 218.6 us)

commit v2 on v1

v2 whole, which is shorter than its diff:
```python
import functools

import jax
import jax.numpy as jnp
from jax import lax
from jax.experimental import pallas as pl
from jax.experimental.pallas import tpu as pltpu
from jax.sharding import PartitionSpec as P

BAND = 4
EPS = 1e-06
AXES = ("site", "dp")
Z, YH, CORE, X, YL = 8, 2, 2, 4, 2


def route(move):
    pairs = []
    for source in range(Z * YH * CORE * X * YL):
        rest, yl = divmod(source, YL)
        rest, x = divmod(rest, X)
        rest, core = divmod(rest, CORE)
        z, yh = divmod(rest, YH)
        z, yh, core, x, yl = move(z, yh, core, x, yl)
        target = ((((z % Z) * YH + yh) * CORE + core) * X + x % X) * YL + yl
        pairs.append((source, target))
    return pairs


def inverse(pairs):
    return [(target, source) for source, target in pairs]


UP_X = route(lambda z, yh, c, x, yl: (z, yh, c, x + 1, yl))
DOWN_X = route(lambda z, yh, c, x, yl: (z, yh, c, x - 1, yl))
MATE_Y = route(lambda z, yh, c, x, yl: (z, yh, c, x, 1 - yl))
OTHER_CORE = route(lambda z, yh, c, x, yl: (z, yh, 1 - c, x, yl))
SIDE = route(lambda z, yh, c, x, yl: (z - (c == 0), yh, 1 - c, x, yl))
AHEAD = route(lambda z, yh, c, x, yl: (z - (yh == 0), 1 - yh, c, x, 1 - yl))
LOSS_ROUTES = (
    OTHER_CORE,
    route(lambda z, yh, c, x, yl: (z, yh, c, x ^ 1, yl)),
    route(lambda z, yh, c, x, yl: (z, yh, c, 3 - x, yl)),
    MATE_Y,
    route(lambda z, yh, c, x, yl: (z, 1 - yh, c, x, 1 - yl)),
    route(lambda z, yh, c, x, yl: (z ^ 1, yh, c, x, yl)),
    route(lambda z, yh, c, x, yl: (z ^ 2, yh, c, x, yl)),
    route(lambda z, yh, c, x, yl: (z ^ 4, yh, c, x, yl)),
)


def move(block, pairs):
    return lax.ppermute(block, AXES, pairs)


def unit_kernel(image_ref, text_ref, img_unit_ref, txt_unit_ref):
    for source, unit in ((image_ref, img_unit_ref), (text_ref, txt_unit_ref)):
        values = source[...].astype(jnp.float32)
        inverse = lax.rsqrt(jnp.sum(values * values, axis=-1, keepdims=True) + EPS)
        unit[...] = (values * inverse).astype(jnp.bfloat16)


def units(image_embed, text_embed):
    out = jax.ShapeDtypeStruct(image_embed.shape, jnp.bfloat16)
    return pl.pallas_call(unit_kernel, out_shape=(out, out))(image_embed, text_embed)


def dot(left, right, dims):
    return lax.dot_general(left, right, ((dims[:1], dims[1:]), ((), ())), preferred_element_type=jnp.float32)


def spread(values, refs):
    start = 0
    for ref in refs:
        ref[...] = values[start : start + ref.shape[0], :]
        start += ref.shape[0]


def score_kernel(scalars_ref, *refs):
    img_refs, txt_refs, refs = refs[:9], refs[9:13], refs[13:]
    img, txt, weights, loss_ref = refs[:4]
    grad_refs = refs[4:]
    rows = txt_refs[0].shape[0]
    start = 0
    for ref in img_refs:
        img[start : start + ref.shape[0], :] = ref[...]
        start += ref.shape[0]
    for k, ref in enumerate(txt_refs):
        txt[k * rows : (k + 1) * rows, :] = ref[...]
    sharpness = scalars_ref[0]
    shift = scalars_ref[1]
    chunk = 2 * rows
    texts = txt[...]
    loss = jnp.zeros((8, texts.shape[0]), jnp.float32)
    for i in range(img.shape[0] // chunk):
        block = slice(i * chunk, (i + 1) * chunk)
        score = sharpness * dot(img[block, :], texts, (1, 1)) + shift
        decay = jnp.exp(-jnp.abs(score))
        softplus = jnp.maximum(score, 0.0) + jnp.log1p(decay)
        sigmoid = jnp.where(score >= 0, 1.0, decay) / (1.0 + decay)
        if i == 2:
            row = lax.broadcasted_iota(jnp.int32, score.shape, 0)
            column = lax.broadcasted_iota(jnp.int32, score.shape, 1)
            positive = row + 3 * rows == column
            softplus = jnp.where(positive, jnp.maximum(-score, 0.0) + jnp.log1p(decay), softplus)
            sigmoid = sigmoid - jnp.where(positive, 1.0, 0.0)
        loss = loss + jnp.sum(softplus.reshape(-1, 8, softplus.shape[1]), axis=0)
        weight = (sharpness * sigmoid).astype(jnp.bfloat16)
        weights[block, :] = weight
        if 2 * i < len(grad_refs):
            spread(dot(weight, texts, (1, 0)), grad_refs[2 * i : 2 * i + 2])
    loss_ref[...] = sum(loss[:, i * 128 : (i + 1) * 128] for i in range(texts.shape[0] // 128))


def text_kernel(weights, img, *grad_refs):
    chunk = 2 * grad_refs[0].shape[0]
    for i in range(0, len(grad_refs), 2):
        start = i // 2 * chunk
        spread(dot(weights[:, start : start + chunk], img[...], (0, 0)), grad_refs[i : i + 2])


def image_kernel(weights, txt, *grad_refs):
    chunk = 2 * grad_refs[0].shape[0]
    first = weights.shape[0] - chunk * len(grad_refs) // 2
    for i in range(0, len(grad_refs), 2):
        start = first + i // 2 * chunk
        spread(dot(weights[start : start + chunk, :], txt[...], (1, 0)), grad_refs[i : i + 2])


VMEM = pl.BlockSpec(memory_space=pltpu.VMEM)
SMEM = pl.BlockSpec(memory_space=pltpu.SMEM)
PARAMS = pltpu.CompilerParams(vmem_limit_bytes=30 * 1024 * 1024)


def grads(count, rows, width):
    return (jax.ShapeDtypeStruct((rows, width), jnp.float32),) * count


def score_terms(scalars, images, texts):
    rows, width = texts[0].shape
    img_rows, txt_rows = rows * X * YL, rows * BAND
    out_shape = (
        jax.ShapeDtypeStruct((img_rows, width), jnp.bfloat16),
        jax.ShapeDtypeStruct((txt_rows, width), jnp.bfloat16),
        jax.ShapeDtypeStruct((img_rows, txt_rows), jnp.bfloat16),
        jax.ShapeDtypeStruct((8, 128), jnp.float32),
        *grads(4, rows, width),
    )
    return pl.pallas_call(
        score_kernel,
        out_shape=out_shape,
        in_specs=[SMEM] + [VMEM] * (len(images) + len(texts)),
        out_specs=(VMEM,) * len(out_shape),
        compiler_params=PARAMS,
    )(scalars, *images, *texts)


def text_terms(weights, img, rows):
    out_shape = grads(4, rows, img.shape[1])
    return pl.pallas_call(text_kernel, out_shape=out_shape, compiler_params=PARAMS)(weights, img)


def image_terms(weights, txt, rows):
    out_shape = grads(4, rows, txt.shape[1])
    return pl.pallas_call(image_kernel, out_shape=out_shape, compiler_params=PARAMS)(weights, txt)


def final_kernel(embed_ref, upstream_ref, grad_ref):
    values = embed_ref[...].astype(jnp.float32)
    upstream = upstream_ref[...]
    inverse = lax.rsqrt(jnp.sum(values * values, axis=-1, keepdims=True) + EPS)
    inner = jnp.sum(values * upstream, axis=-1, keepdims=True)
    grad_ref[...] = inverse * upstream - inverse * inverse * inverse * values * inner


def back_norm(embed, upstream):
    return pl.pallas_call(
        final_kernel, out_shape=jax.ShapeDtypeStruct(upstream.shape, jnp.float32)
    )(embed, upstream)


def narrow(block):
    return block.astype(jnp.float16)


def wide(block):
    return block.astype(jnp.float32)


def together(*values):
    return lax.optimization_barrier(values)


def loss_step(total, index):
    return total + move(total, LOSS_ROUTES[index])


def shards(image_embed, text_embed, log_sharpness_factor, couple_score_shift):
    rows, width = image_embed.shape
    half = rows // 2
    scalars = jnp.stack([jnp.exp(log_sharpness_factor), couple_score_shift])
    own_img, own_txt = units(image_embed, text_embed)

    txt_y = move(own_txt, AHEAD)
    txt_c = move(own_txt, SIDE)
    img_m = move(own_img, MATE_Y)
    img_b = move(own_img, DOWN_X)
    img_a = move(own_img, UP_X)
    img_a, img_b, img_m = together(img_a, img_b, img_m)
    img_ma = move(img_a, MATE_Y)
    img_mb = move(img_m, DOWN_X)
    img_2 = move(img_a, UP_X)
    txt_y, txt_c, img_a2, img_mb2 = together(txt_y, txt_c, img_2, img_mb)
    txt_d = move(txt_y, OTHER_CORE)
    img_m2b = move(img_mb2[half:], DOWN_X)
    img_m2a = move(img_a2[:half], MATE_Y)

    images = (img_m2a, img_m2b, img_2, img_mb, img_ma, own_img, img_a, img_b, img_m)
    texts = (txt_c, txt_d, txt_y, own_txt)
    img, txt, weights, loss, of_m2, of_2, of_mb, of_ma = score_terms(scalars, images, texts)
    got_m2a = move(narrow(of_m2[:half]), MATE_Y)
    got_m2b = move(narrow(of_m2[half:]), UP_X)
    loss = loss_step(loss, 0)
    of_c, of_d, of_y, own_txt_grad = text_terms(weights, img, rows)
    got_d = move(narrow(of_d), OTHER_CORE)
    own_img_grad, of_a, of_b, of_m = image_terms(weights, txt, rows)
    loss, of_m = together(loss, of_m)
    loss = loss_step(loss, 1)
    got_m2a, loss = together(got_m2a, loss)
    got_m2a, got_m2b, got_d, own_img_grad = together(got_m2a, got_m2b, got_d, own_img_grad)
    zeros = jnp.zeros((half, width), jnp.float32)
    got_ma = move(narrow(of_ma), MATE_Y)
    got_2 = move(narrow(of_2 + jnp.concatenate([wide(got_m2a), zeros], 0)), DOWN_X)
    got_mb = move(narrow(of_mb + jnp.concatenate([zeros, wide(got_m2b)], 0)), UP_X)
    got_y = move(narrow(of_y + wide(got_d)), inverse(AHEAD))
    got_c = move(narrow(of_c), inverse(SIDE))
    loss = loss_step(loss, 2)
    loss = loss_step(loss, 3)
    got_ma, loss = together(got_ma, loss)
    got_ma, got_2, got_mb = together(got_ma, got_2, got_mb)
    got_b = move(narrow(of_b), UP_X)
    got_m = move(narrow(of_m + wide(got_mb)), MATE_Y)
    got_a = move(narrow(of_a + wide(got_2) + wide(got_ma)), DOWN_X)
    loss = loss_step(loss, 4)
    loss = loss_step(loss, 5)
    got_y, loss = together(got_y, loss)
    got_y, got_c = together(got_y, got_c)
    txt_grad = own_txt_grad + wide(got_c) + wide(got_y)
    grad_text = back_norm(text_embed, txt_grad)
    got_a, got_b, got_m, grad_text = together(got_a, got_b, got_m, grad_text)
    loss = loss_step(loss, 6)
    loss = loss_step(loss, 7)
    img_grad = own_img_grad + wide(got_a) + wide(got_b) + wide(got_m)
    grad_image = back_norm(image_embed, img_grad)
    pair_loss = jnp.sum(loss) / jnp.float32(rows * 256 * BAND * rows * X * YL)
    return pair_loss, grad_image, grad_text


def solution(mesh):
    return jax.shard_map(
        shards,
        mesh=mesh,
        in_specs=(P(AXES, None), P(AXES, None), P(), P()),
        out_specs=(P(), P(AXES, None), P(AXES, None)),
        check_vma=False,
    )
```

time: 120 us -> 88.8 us (0.74)
  waiting for transfers between devices: 45.9 us -> 23.2 us
  other arithmetic: 13.7 us -> 3.14 us
  starting transfers between devices: 39.3 us -> 42.1 us
    ppermute x33 -> x30, waiting for transfers between devices: 45.9 us -> 23.2 us  [move(): return lax.ppermute(block, AXES, pairs)]
    sub x2 -> x0, other arithmetic: 4.52 us -> none  [back_norm(): return inverse * upstream - inverse * inverse * inverse * values * inner]
    another operation x2 -> x1, other arithmetic: 2.89 us -> 0.04 us
    ppermute x33 -> x30, starting transfers between devices: 39.3 us -> 42.1 us  [move(): return lax.ppermute(block, AXES, pairs)]
    reduce_sum x3 -> x1, other arithmetic: 2.55 us -> 0.6 us  [shards(): pair_loss = jnp.sum(loss) / jnp.float32(rows * 256 * BAND * rows * X * YL)]
    add x7 -> x9, other arithmetic: 0.02 us -> 1.86 us  [the longest x1 0.94 us: shards(): img_grad = own_img_grad + wide(got_a) + wide(got_b) + wide(got_m)]
    convert_element_type x4 -> x9, other arithmetic: 2.05 us -> 0.57 us  [narrow(): return block.astype(jnp.float16)]
    pallas_call x1 -> x5, Pallas kernels: 11.7 us -> 10.9 us  [the longest x2 4.39 us: back_norm(): pl.pallas_call(final_kernel, out_shape=jax.ShapeDtypeStruct(upstream.shap...]
  transfers between devices with their start and end apart: 33 -> 30, of which waited for: 17 -> 12; matrix products, arithmetic and copies ran while one was open for 4% -> 3% of each run, Pallas kernels for 0% -> 3%
where the time goes in v2:
time: 88.8 us; the launch traced here: 87.3 us
  starting transfers between devices  42.1 us (47%)
  waiting for transfers between devices  23.2 us (26%)
  Pallas kernels  12.9 us (15%)
  between operations  3.94 us (4%)
  other arithmetic  3.14 us (4%)
  local copies, waits for them, and re-layouts  2 us (2%)
    ppermute x30, starting transfers between devices, move(): return lax.ppermute(block, AXES, pairs)  42.1 us
    ppermute x30, waiting for transfers between devices, move(): return lax.ppermute(block, AXES, pairs)  23.2 us
    pallas_call x2, Pallas kernels, back_norm(): pl.pallas_call(final_kernel, out_shape=jax.ShapeDtypeStruct(upstream.shap...  4.39 us
    pallas_call x1, Pallas kernels, score_terms(): pl.pallas_call(score_kernel, out_shape=out_shape, in_specs=[SMEM] + [VMEM...  4.09 us
    pallas_call x1, Pallas kernels, units(): pl.pallas_call(unit_kernel, out_shape=(out, out))(image_embed, text_embed)  2.02 us
    unnamed x4, local copies, waits for them, and re-layouts  1.92 us
  transfers between devices with their start and end apart: 30, of which 12 were waited for; matrix products, arithmetic and copies ran while one was open for 3% of the time, Pallas kernels for 3%

profile of v2, /device:TPU:24, one launch (start us, length us, event | category | flops | bytes accessed | tf_op | source)
XLA Modules:
  0.0 87.3 jit_solution(9989279962701828294)
XLA Ops:
  0.6 2.0 %shard_map.67 = (bf16[128,1152]{1,0:T(8,128)(2,1)}, bf16[128,1152]{1,0:T(8,128)(2,1)}) custom-call(bf16[128,1152]{1,0:T(8,128)(2,1)} %embed_ref.3, bf16[128,1152]{1,0:T(8,128)(2,1)} %embed_ref.2), custom_call_target="tpu_custom_call" | custom-call | tf_op jit(solution)/shard_map/pallas_call | solution.py:64
  3.4 2.8 %collective-permute-start.3 = (bf16[128,1152]{1,0:T(8,128)(2,1)}, bf16[128,1152]{1,0:T(8,128)(2,1)S(1)}, u32[]{:S(2)}, u32[]{:S(2)}) collective-permute-start(bf16[128,1152]{1,0:T(8,128)(2,1)} %get-tuple-element.50.refs_5_), channel_id=1, source_target_pairs={{0,6},{1,7},{2,0},{3,1},{4,2},{5,3},{6,4},{7,5},{8,14},{9,15},{10,... | collective-permute-start | bytes 884744 | tf_op jit(solution)/shard_map/ppermute | solution.py:52
  6.2 4.7 %collective-permute-start.1 = (bf16[128,1152]{1,0:T(8,128)(2,1)}, bf16[128,1152]{1,0:T(8,128)(2,1)S(1)}, u32[]{:S(2)}, u32[]{:S(2)}) collective-permute-start(bf16[128,1152]{1,0:T(8,128)(2,1)} %get-tuple-element.49.refs_12_), channel_id=1, source_target_pairs={{0,232},{1,233},{2,234},{3,235},{4,236},{5,237},{6,238},{7,239},{8... | collective-permute-start | bytes 884744 | tf_op jit(solution)/shard_map/ppermute | solution.py:52
  10.9 1.1 %collective-permute-start = (bf16[128,1152]{1,0:T(8,128)(2,1)}, bf16[128,1152]{1,0:T(8,128)(2,1)S(1)}, u32[]{:S(2)}, u32[]{:S(2)}) collective-permute-start(bf16[128,1152]{1,0:T(8,128)(2,1)} %get-tuple-element.49.refs_12_), channel_id=1, source_target_pairs={{0,241},{1,240},{2,243},{3,242},{4,245},{5,244},{6,247},{7,246},{8... | collective-permute-start | bytes 884744 | tf_op jit(solution)/shard_map/ppermute | solution.py:52
  12.5 3.3 %collective-permute-done.2.refs_6_ = bf16[128,1152]{1,0:T(8,128)(2,1)S(1)} collective-permute-done((bf16[128,1152]{1,0:T(8,128)(2,1)}, bf16[128,1152]{1,0:T(8,128)(2,1)S(1)}, u32[]{:S(2)}, u32[]{:S(2)}) %collective-permute-start.2) | collective-permute-done | bytes 294944 | tf_op jit(solution)/shard_map/ppermute | solution.py:52
  16.0 1.7 %collective-permute-start.5 = (bf16[128,1152]{1,0:T(8,128)(2,1)S(1)}, bf16[128,1152]{1,0:T(8,128)(2,1)S(1)}, u32[]{:S(2)}, u32[]{:S(2)}) collective-permute-start(bf16[128,1152]{1,0:T(8,128)(2,1)S(1)} %collective-permute-done.2.refs_6_), channel_id=1, source_target_pairs={{0,2},{1,3},{2,4},{3,5},{4,6},{5,7},{6,0},{7,1},{8,10},{9,11},{10,... | collective-permute-start | bytes 884744 | tf_op jit(solution)/shard_map/ppermute | solution.py:52
  17.8 1.3 %collective-permute-start.9 = (bf16[128,1152]{1,0:T(8,128)(2,1)S(1)}, bf16[128,1152]{1,0:T(8,128)(2,1)S(1)}, u32[]{:S(2)}, u32[]{:S(2)}) collective-permute-start(bf16[128,1152]{1,0:T(8,128)(2,1)S(1)} %collective-permute-done.2.refs_6_), channel_id=1, source_target_pairs={{0,1},{1,0},{2,3},{3,2},{4,5},{5,4},{6,7},{7,6},{8,9},{9,8},{10,11... | collective-permute-start | bytes 884744 | tf_op jit(solution)/shard_map/ppermute | solution.py:52
  19.9 3.1 %collective-permute-done.6.refs_3_ = bf16[128,1152]{1,0:T(8,128)(2,1)S(1)} collective-permute-done((bf16[128,1152]{1,0:T(8,128)(2,1)S(1)}, bf16[128,1152]{1,0:T(8,128)(2,1)S(1)}, u32[]{:S(2)}, u32[]{:S(2)}) %collective-permute-start.6) | collective-permute-done | bytes 294944 | tf_op jit(solution)/shard_map/ppermute | solution.py:52
  23.0 1.5 %collective-permute-done.5.refs_2_ = bf16[128,1152]{1,0:T(8,128)(2,1)S(1)} collective-permute-done((bf16[128,1152]{1,0:T(8,128)(2,1)S(1)}, bf16[128,1152]{1,0:T(8,128)(2,1)S(1)}, u32[]{:S(2)}, u32[]{:S(2)}) %collective-permute-start.5) | collective-permute-done | bytes 294944 | tf_op jit(solution)/shard_map/ppermute | solution.py:52
  24.9 1.3 %collective-permute-start.7 = (bf16[64,1152]{1,0:T(8,128)(2,1)S(1)}, bf16[64,1152]{1,0:T(8,128)(2,1)S(1)}, u32[]{:S(2)}, u32[]{:S(2)}) collective-permute-start(bf16[64,1152]{1,0:T(8,128)(2,1)S(1)} %slice.14), channel_id=1, source_target_pairs={{0,1},{1,0},{2,3},{3,2},{4,5},{5,4},{6,7},{7,6},{8,9},{9,8},{10,11... | collective-permute-start | bytes 442376 | tf_op jit(solution)/shard_map/ppermute | solution.py:52
  27.6 3.3 %collective-permute-done.8.refs_1_ = bf16[64,1152]{1,0:T(8,128)(2,1)S(1)} collective-permute-done((bf16[64,1152]{1,0:T(8,128)(2,1)S(1)}, bf16[64,1152]{1,0:T(8,128)(2,1)S(1)}, u32[]{:S(2)}, u32[]{:S(2)}) %collective-permute-start.8) | collective-permute-done | bytes 147488 | tf_op jit(solution)/shard_map/ppermute | solution.py:52
  31.0 1.0 %copy-done = bf16[128,1152]{1,0:T(8,128)(2,1)S(1)} copy-done((bf16[128,1152]{1,0:T(8,128)(2,1)S(1)}, bf16[128,1152]{1,0:T(8,128)(2,1)}, u32[]{:S(2)}) %copy-start) | copy-done | bytes 294936
  32.0 1.0 %copy-done.1 = bf16[128,1152]{1,0:T(8,128)(2,1)S(1)} copy-done((bf16[128,1152]{1,0:T(8,128)(2,1)S(1)}, bf16[128,1152]{1,0:T(8,128)(2,1)}, u32[]{:S(2)}) %copy-start.1) | copy-done | bytes 294936
  32.9 4.1 %shard_map.68 = (bf16[1024,1152]{1,0:T(8,128)(2,1)S(1)}, bf16[512,1152]{1,0:T(8,128)(2,1)S(1)}, bf16[1024,512]{1,0:T(8,128)(2,1)S(1)}, f32[8,128]{1,0:T(8,128)S(...) custom-call(f32[2]{0:T(128)S(1)} %pad_maximum_fusion.scalars_ref, ...), custom_call_target="tpu_custom_call" | custom-call | tf_op jit(solution)/shard_map/pallas_call | solution.py:148
  37.0 1.6 %shard_map.69 = (f32[128,1152]{1,0:T(8,128)S(1)}, f32[128,1152]{1,0:T(8,128)S(1)}, f32[128,1152]{1,0:T(8,128)S(1)}, f32[128,1152]{1,0:T(8,128)S(1)}) custom-call(bf16[1024,512]{1,0:T(8,128)(2,1)S(1)} %get-tuple-element.58.weights, bf16[1024,1152]{1,0:T(8,128)(2,1)S(1)} %get-tuple-element.59.img), custom_call_target="tpu_custom_call" | custom-call | tf_op jit(solution)/shard_map/pallas_call | solution.py:159
  38.9 1.5 %collective-permute-start.11 = (f16[64,1152]{1,0:T(8,128)(2,1)S(1)}, f16[64,1152]{1,0:T(8,128)(2,1)S(1)}, u32[]{:S(2)}, u32[]{:S(2)}) collective-permute-start(f16[64,1152]{1,0:T(8,128)(2,1)S(1)} %get-tuple-element.96), channel_id=1, source_target_pairs={{0,1},{1,0},{2,3},{3,2},{4,5},{5,4},{6,7},{7,6},{8,9},{9,8},{10,11... | collective-permute-start | bytes 442376 | tf_op jit(solution)/shard_map/ppermute | solution.py:52
  40.4 1.6 %collective-permute-start.14 = (f16[64,1152]{1,0:T(8,128)(2,1)S(1)}, f16[64,1152]{1,0:T(8,128)(2,1)S(1)}, u32[]{:S(2)}, u32[]{:S(2)}) collective-permute-start(f16[64,1152]{1,0:T(8,128)(2,1)S(1)} %get-tuple-element.95), channel_id=1, source_target_pairs={{0,2},{1,3},{2,4},{3,5},{4,6},{5,7},{6,0},{7,1},{8,10},{9,11},{10,... | collective-permute-start | bytes 442376 | tf_op jit(solution)/shard_map/ppermute | solution.py:52
  43.5 3.4 %collective-permute-done.13 = f32[8,128]{1,0:T(8,128)S(1)} collective-permute-done((f32[8,128]{1,0:T(8,128)S(1)}, f32[8,128]{1,0:T(8,128)S(1)}, u32[]{:S(2)}, u32[]{:S(2)}) %collective-permute-start.13) | collective-permute-done | bytes 4128 | tf_op jit(solution)/shard_map/ppermute | solution.py:52
  46.9 1.6 %collective-permute-start.18 = (f32[8,128]{1,0:T(8,128)S(1)}, f32[8,128]{1,0:T(8,128)S(1)}, u32[]{:S(2)}, u32[]{:S(2)}) collective-permute-start(f32[8,128]{1,0:T(8,128)S(1)} %add.62), channel_id=1, source_target_pairs={{0,6},{1,7},{2,4},{3,5},{4,2},{5,3},{6,0},{7,1},{8,14},{9,15},{10,... | collective-permute-start | bytes 12296 | tf_op jit(solution)/shard_map/ppermute | solution.py:52
  49.4 2.3 %collective-permute-done.18 = f32[8,128]{1,0:T(8,128)S(1)} collective-permute-done((f32[8,128]{1,0:T(8,128)S(1)}, f32[8,128]{1,0:T(8,128)S(1)}, u32[]{:S(2)}, u32[]{:S(2)}) %collective-permute-start.18) | collective-permute-done | bytes 4128 | tf_op jit(solution)/shard_map/ppermute | solution.py:52
  52.5 2.5 %collective-permute-start.16 = (f16[128,1152]{1,0:T(8,128)(2,1)S(1)}, f16[128,1152]{1,0:T(8,128)(2,1)S(1)}, u32[]{:S(2)}, u32[]{:S(2)}) collective-permute-start(f16[128,1152]{1,0:T(8,128)(2,1)S(1)} %add_convert_fusion.4), channel_id=1, source_target_pairs={{241,0},{240,1},{243,2},{242,3},{245,4},{244,5},{247,6},{246,7},{2... | collective-permute-start | bytes 884744 | tf_op jit(solution)/shard_map/ppermute | solution.py:52
  55.1 1.7 %collective-permute-start.24 = (f16[128,1152]{1,0:T(8,128)(2,1)S(1)}, f16[128,1152]{1,0:T(8,128)(2,1)S(1)}, u32[]{:S(2)}, u32[]{:S(2)}) collective-permute-start(f16[128,1152]{1,0:T(8,128)(2,1)S(1)} %add_convert_fusion.3), channel_id=1, source_target_pairs={{0,6},{1,7},{2,0},{3,1},{4,2},{5,3},{6,4},{7,5},{8,14},{9,15},{10,... | collective-permute-start | bytes 884744 | tf_op jit(solution)/shard_map/ppermute | solution.py:52
  57.3 2.5 %collective-permute-start.20 = (f32[8,128]{1,0:T(8,128)S(1)}, f32[8,128]{1,0:T(8,128)S(1)}, u32[]{:S(2)}, u32[]{:S(2)}) collective-permute-start(f32[8,128]{1,0:T(8,128)S(1)} %add.65), channel_id=1, source_target_pairs={{0,17},{1,16},{2,19},{3,18},{4,21},{5,20},{6,23},{7,22},{8,25},{9,... | collective-permute-start | bytes 12296 | tf_op jit(solution)/shard_map/ppermute | solution.py:52
  59.9 2.9 %collective-permute-done.20 = f32[8,128]{1,0:T(8,128)S(1)} collective-permute-done((f32[8,128]{1,0:T(8,128)S(1)}, f32[8,128]{1,0:T(8,128)S(1)}, u32[]{:S(2)}, u32[]{:S(2)}) %collective-permute-start.20) | collective-permute-done | bytes 4128 | tf_op jit(solution)/shard_map/ppermute | solution.py:52
  62.8 1.9 %collective-permute-start.21 = (f32[8,128]{1,0:T(8,128)S(1)}, f32[8,128]{1,0:T(8,128)S(1)}, u32[]{:S(2)}, u32[]{:S(2)}) collective-permute-start(f32[8,128]{1,0:T(8,128)S(1)} %add.66), channel_id=1, source_target_pairs={{0,32},{1,33},{2,34},{3,35},{4,36},{5,37},{6,38},{7,39},{8,40},{9,... | collective-permute-start | bytes 12296 | tf_op jit(solution)/shard_map/ppermute | solution.py:52
  64.7 1.6 %collective-permute-done.21 = f32[8,128]{1,0:T(8,128)S(1)} collective-permute-done((f32[8,128]{1,0:T(8,128)S(1)}, f32[8,128]{1,0:T(8,128)S(1)}, u32[]{:S(2)}, u32[]{:S(2)}) %collective-permute-start.21) | collective-permute-done | bytes 4128 | tf_op jit(solution)/shard_map/ppermute | solution.py:52
  66.9 3.7 %collective-permute-start.22 = (f32[8,128]{1,0:T(8,128)S(1)}, f32[8,128]{1,0:T(8,128)S(1)}, u32[]{:S(2)}, u32[]{:S(2)}) collective-permute-start(f32[8,128]{1,0:T(8,128)S(1)} %add.67), channel_id=1, source_target_pairs={{0,64},{1,65},{2,66},{3,67},{4,68},{5,69},{6,70},{7,71},{8,72},{9,... | collective-permute-start | bytes 12296 | tf_op jit(solution)/shard_map/ppermute | solution.py:52
  70.7 3.2 %collective-permute-start.26 = (f16[128,1152]{1,0:T(8,128)(2,1)S(1)}, f16[128,1152]{1,0:T(8,128)(2,1)S(1)}, u32[]{:S(2)}, u32[]{:S(2)}) collective-permute-start(f16[128,1152]{1,0:T(8,128)(2,1)S(1)} %add_convert_fusion.1), channel_id=1, source_target_pairs={{0,6},{1,7},{2,0},{3,1},{4,2},{5,3},{6,4},{7,5},{8,14},{9,15},{10,... | collective-permute-start | bytes 884744 | tf_op jit(solution)/shard_map/ppermute | solution.py:52
  74.1 4.6 %collective-permute-start.23 = (f32[8,128]{1,0:T(8,128)S(1)}, f32[8,128]{1,0:T(8,128)S(1)}, u32[]{:S(2)}, u32[]{:S(2)}) collective-permute-start(f32[8,128]{1,0:T(8,128)S(1)} %add.68), channel_id=1, source_target_pairs={{0,128},{1,129},{2,130},{3,131},{4,132},{5,133},{6,134},{7,135},{8... | collective-permute-start | bytes 12296 | tf_op jit(solution)/shard_map/ppermute | solution.py:52
  79.6 2.2 %shard_map.71 = f32[128,1152]{1,0:T(8,128)} custom-call(bf16[128,1152]{1,0:T(8,128)(2,1)} %embed_ref.2, f32[128,1152]{1,0:T(8,128)} %convert_add_fusion.1.upstream_ref), custom_call_target="tpu_custom_call" | custom-call | tf_op jit(solution)/shard_map/pallas_call | solution.py:176
  83.1 0.9 %convert_add_fusion.upstream_ref = f32[128,1152]{1,0:T(8,128)} fusion(f16[128,1152]{1,0:T(8,128)(2,1)S(1)} %collective-permute-done.28, f16[128,1152]{1,0:T(8,128)(2,1)S(1)} %collective-permute-done.27, f32[128,1152]{1,0:T(8,128)S(1)} %get-tuple-element.74, f16[128,1152]{1,0:T(8,128)(2,1)S(1)} %collective-permute-done.26), kind=kLoop, calls=%fused_computation | loop fusion | flops 884736 | bytes 2064384 | tf_op jit(solution)/shard_map/add | solution.py:252
  84.0 2.2 %shard_map.72 = f32[128,1152]{1,0:T(8,128)} custom-call(bf16[128,1152]{1,0:T(8,128)(2,1)} %embed_ref.3, f32[128,1152]{1,0:T(8,128)} %convert_add_fusion.upstream_ref), custom_call_target="tpu_custom_call" | custom-call | tf_op jit(solution)/shard_map/pallas_call | solution.py:176
  (62 shorter events, 9.4 us)
Async XLA Ops:
  2.6 9.3 %collective-permute-start.4 = (bf16[128,1152]{1,0:T(8,128)(2,1)}, bf16[128,1152]{1,0:T(8,128)(2,1)S(1)}, u32[]{:S(2)}, u32[]{:S(2)}) collective-permute-start(bf16[128,1152]{1,0:T(8,128)(2,1)} %get-tuple-element.50.refs_5_), channel_id=1, source_target_pairs={{0,1},{1,0},{2,3},{3,2},{4,5},{5,4},{6,7},{7,6},{8,9},{9,8},{10,11... | collective-permute-start | bytes 884744 | tf_op jit(solution)/shard_map/ppermute | solution.py:52
  3.4 9.1 %collective-permute-start.3 = (bf16[128,1152]{1,0:T(8,128)(2,1)}, bf16[128,1152]{1,0:T(8,128)(2,1)S(1)}, u32[]{:S(2)}, u32[]{:S(2)}) collective-permute-start(bf16[128,1152]{1,0:T(8,128)(2,1)} %get-tuple-element.50.refs_5_), channel_id=1, source_target_pairs={{0,6},{1,7},{2,0},{3,1},{4,2},{5,3},{6,4},{7,5},{8,14},{9,15},{10,... | collective-permute-start | bytes 884744 | tf_op jit(solution)/shard_map/ppermute | solution.py:52
  6.1 9.6 %collective-permute-start.2 = (bf16[128,1152]{1,0:T(8,128)(2,1)}, bf16[128,1152]{1,0:T(8,128)(2,1)S(1)}, u32[]{:S(2)}, u32[]{:S(2)}) collective-permute-start(bf16[128,1152]{1,0:T(8,128)(2,1)} %get-tuple-element.50.refs_5_), channel_id=1, source_target_pairs={{0,2},{1,3},{2,4},{3,5},{4,6},{5,7},{6,0},{7,1},{8,10},{9,11},{10,... | collective-permute-start | bytes 884744 | tf_op jit(solution)/shard_map/ppermute | solution.py:52
  6.2 12.9 %collective-permute-start.1 = (bf16[128,1152]{1,0:T(8,128)(2,1)}, bf16[128,1152]{1,0:T(8,128)(2,1)S(1)}, u32[]{:S(2)}, u32[]{:S(2)}) collective-permute-start(bf16[128,1152]{1,0:T(8,128)(2,1)} %get-tuple-element.49.refs_12_), channel_id=1, source_target_pairs={{0,232},{1,233},{2,234},{3,235},{4,236},{5,237},{6,238},{7,239},{8... | collective-permute-start | bytes 884744 | tf_op jit(solution)/shard_map/ppermute | solution.py:52
  10.9 9.0 %collective-permute-start = (bf16[128,1152]{1,0:T(8,128)(2,1)}, bf16[128,1152]{1,0:T(8,128)(2,1)S(1)}, u32[]{:S(2)}, u32[]{:S(2)}) collective-permute-start(bf16[128,1152]{1,0:T(8,128)(2,1)} %get-tuple-element.49.refs_12_), channel_id=1, source_target_pairs={{0,241},{1,240},{2,243},{3,242},{4,245},{5,244},{6,247},{7,246},{8... | collective-permute-start | bytes 884744 | tf_op jit(solution)/shard_map/ppermute | solution.py:52
  15.8 7.3 %collective-permute-start.6 = (bf16[128,1152]{1,0:T(8,128)(2,1)S(1)}, bf16[128,1152]{1,0:T(8,128)(2,1)S(1)}, u32[]{:S(2)}, u32[]{:S(2)}) collective-permute-start(bf16[128,1152]{1,0:T(8,128)(2,1)S(1)} %collective-permute-done.4.refs_8_), channel_id=1, source_target_pairs={{0,6},{1,7},{2,0},{3,1},{4,2},{5,3},{6,4},{7,5},{8,14},{9,15},{10,... | collective-permute-start | bytes 884744 | tf_op jit(solution)/shard_map/ppermute | solution.py:52
  16.0 8.5 %collective-permute-start.5 = (bf16[128,1152]{1,0:T(8,128)(2,1)S(1)}, bf16[128,1152]{1,0:T(8,128)(2,1)S(1)}, u32[]{:S(2)}, u32[]{:S(2)}) collective-permute-start(bf16[128,1152]{1,0:T(8,128)(2,1)S(1)} %collective-permute-done.2.refs_6_), channel_id=1, source_target_pairs={{0,2},{1,3},{2,4},{3,5},{4,6},{5,7},{6,0},{7,1},{8,10},{9,11},{10,... | collective-permute-start | bytes 884744 | tf_op jit(solution)/shard_map/ppermute | solution.py:52
  17.8 9.8 %collective-permute-start.9 = (bf16[128,1152]{1,0:T(8,128)(2,1)S(1)}, bf16[128,1152]{1,0:T(8,128)(2,1)S(1)}, u32[]{:S(2)}, u32[]{:S(2)}) collective-permute-start(bf16[128,1152]{1,0:T(8,128)(2,1)S(1)} %collective-permute-done.2.refs_6_), channel_id=1, source_target_pairs={{0,1},{1,0},{2,3},{3,2},{4,5},{5,4},{6,7},{7,6},{8,9},{9,8},{10,11... | collective-permute-start | bytes 884744 | tf_op jit(solution)/shard_map/ppermute | solution.py:52
  24.5 6.5 %collective-permute-start.10 = (bf16[128,1152]{1,0:T(8,128)(2,1)S(1)}, bf16[128,1152]{1,0:T(8,128)(2,1)S(1)}, u32[]{:S(2)}, u32[]{:S(2)}) collective-permute-start(bf16[128,1152]{1,0:T(8,128)(2,1)S(1)} %collective-permute-done.refs_11_), channel_id=1, source_target_pairs={{0,8},{1,9},{2,10},{3,11},{4,12},{5,13},{6,14},{7,15},{8,0},{9,1},... | collective-permute-start | bytes 884744 | tf_op jit(solution)/shard_map/ppermute | solution.py:52
  24.6 6.3 %collective-permute-start.8 = (bf16[64,1152]{1,0:T(8,128)(2,1)S(1)}, bf16[64,1152]{1,0:T(8,128)(2,1)S(1)}, u32[]{:S(2)}, u32[]{:S(2)}) collective-permute-start(bf16[64,1152]{1,0:T(8,128)(2,1)S(1)} %slice.15), channel_id=1, source_target_pairs={{0,6},{1,7},{2,0},{3,1},{4,2},{5,3},{6,4},{7,5},{8,14},{9,15},{10,... | collective-permute-start | bytes 442376 | tf_op jit(solution)/shard_map/ppermute | solution.py:52
  24.9 6.1 %collective-permute-start.7 = (bf16[64,1152]{1,0:T(8,128)(2,1)S(1)}, bf16[64,1152]{1,0:T(8,128)(2,1)S(1)}, u32[]{:S(2)}, u32[]{:S(2)}) collective-permute-start(bf16[64,1152]{1,0:T(8,128)(2,1)S(1)} %slice.14), channel_id=1, source_target_pairs={{0,1},{1,0},{2,3},{3,2},{4,5},{5,4},{6,7},{7,6},{8,9},{9,8},{10,11... | collective-permute-start | bytes 442376 | tf_op jit(solution)/shard_map/ppermute | solution.py:52
  31.0 1.0 %copy-start = (bf16[128,1152]{1,0:T(8,128)(2,1)S(1)}, bf16[128,1152]{1,0:T(8,128)(2,1)}, u32[]{:S(2)}) copy-start(bf16[128,1152]{1,0:T(8,128)(2,1)} %get-tuple-element.50.refs_5_) | copy-start | bytes 884740
  32.0 1.0 %copy-start.1 = (bf16[128,1152]{1,0:T(8,128)(2,1)S(1)}, bf16[128,1152]{1,0:T(8,128)(2,1)}, u32[]{:S(2)}) copy-start(bf16[128,1152]{1,0:T(8,128)(2,1)} %get-tuple-element.49.refs_12_) | copy-start | bytes 884740
  38.7 13.7 %collective-permute-start.15 = (f16[128,1152]{1,0:T(8,128)(2,1)S(1)}, f16[128,1152]{1,0:T(8,128)(2,1)S(1)}, u32[]{:S(2)}, u32[]{:S(2)}) collective-permute-start(f16[128,1152]{1,0:T(8,128)(2,1)S(1)} %convert_element_type.58), channel_id=1, source_target_pairs={{0,8},{1,9},{2,10},{3,11},{4,12},{5,13},{6,14},{7,15},{8,0},{9,1},... | collective-permute-start | bytes 884744 | tf_op jit(solution)/shard_map/ppermute | solution.py:52
  38.9 8.0 %collective-permute-start.11 = (f16[64,1152]{1,0:T(8,128)(2,1)S(1)}, f16[64,1152]{1,0:T(8,128)(2,1)S(1)}, u32[]{:S(2)}, u32[]{:S(2)}) collective-permute-start(f16[64,1152]{1,0:T(8,128)(2,1)S(1)} %get-tuple-element.96), channel_id=1, source_target_pairs={{0,1},{1,0},{2,3},{3,2},{4,5},{5,4},{6,7},{7,6},{8,9},{9,8},{10,11... | collective-permute-start | bytes 442376 | tf_op jit(solution)/shard_map/ppermute | solution.py:52
  40.4 12.0 %collective-permute-start.14 = (f16[64,1152]{1,0:T(8,128)(2,1)S(1)}, f16[64,1152]{1,0:T(8,128)(2,1)S(1)}, u32[]{:S(2)}, u32[]{:S(2)}) collective-permute-start(f16[64,1152]{1,0:T(8,128)(2,1)S(1)} %get-tuple-element.95), channel_id=1, source_target_pairs={{0,2},{1,3},{2,4},{3,5},{4,6},{5,7},{6,0},{7,1},{8,10},{9,11},{10,... | collective-permute-start | bytes 442376 | tf_op jit(solution)/shard_map/ppermute | solution.py:52
  42.1 1.2 %collective-permute-start.12 = (f32[8,128]{1,0:T(8,128)S(1)}, f32[8,128]{1,0:T(8,128)S(1)}, u32[]{:S(2)}, u32[]{:S(2)}) collective-permute-start(f32[8,128]{1,0:T(8,128)S(1)} %get-tuple-element.62), channel_id=1, source_target_pairs={{0,8},{1,9},{2,10},{3,11},{4,12},{5,13},{6,14},{7,15},{8,0},{9,1},... | collective-permute-start | bytes 12296 | tf_op jit(solution)/shard_map/ppermute | solution.py:52
  43.2 3.6 %collective-permute-start.13 = (f32[8,128]{1,0:T(8,128)S(1)}, f32[8,128]{1,0:T(8,128)S(1)}, u32[]{:S(2)}, u32[]{:S(2)}) collective-permute-start(f32[8,128]{1,0:T(8,128)S(1)} %add.61), channel_id=1, source_target_pairs={{0,2},{1,3},{2,0},{3,1},{4,6},{5,7},{6,4},{7,5},{8,10},{9,11},{10,... | collective-permute-start | bytes 12296 | tf_op jit(solution)/shard_map/ppermute | solution.py:52
  46.9 4.8 %collective-permute-start.18 = (f32[8,128]{1,0:T(8,128)S(1)}, f32[8,128]{1,0:T(8,128)S(1)}, u32[]{:S(2)}, u32[]{:S(2)}) collective-permute-start(f32[8,128]{1,0:T(8,128)S(1)} %add.62), channel_id=1, source_target_pairs={{0,6},{1,7},{2,4},{3,5},{4,2},{5,3},{6,0},{7,1},{8,14},{9,15},{10,... | collective-permute-start | bytes 12296 | tf_op jit(solution)/shard_map/ppermute | solution.py:52
  48.5 8.8 %collective-permute-start.17 = (f16[128,1152]{1,0:T(8,128)(2,1)S(1)}, f16[128,1152]{1,0:T(8,128)(2,1)S(1)}, u32[]{:S(2)}, u32[]{:S(2)}) collective-permute-start(f16[128,1152]{1,0:T(8,128)(2,1)S(1)} %convert_element_type.61), channel_id=1, source_target_pairs={{0,1},{1,0},{2,3},{3,2},{4,5},{5,4},{6,7},{7,6},{8,9},{9,8},{10,11... | collective-permute-start | bytes 884744 | tf_op jit(solution)/shard_map/ppermute | solution.py:52
  49.4 17.5 %collective-permute-start.29 = (f16[128,1152]{1,0:T(8,128)(2,1)S(1)}, f16[128,1152]{1,0:T(8,128)(2,1)S(1)}, u32[]{:S(2)}, u32[]{:S(2)}) collective-permute-start(f16[128,1152]{1,0:T(8,128)(2,1)S(1)} %convert_element_type.70), channel_id=1, source_target_pairs={{232,0},{233,1},{234,2},{235,3},{236,4},{237,5},{238,6},{239,7},{0... | collective-permute-start | bytes 884744 | tf_op jit(solution)/shard_map/ppermute | solution.py:52
  51.7 5.1 %collective-permute-start.19 = (f32[8,128]{1,0:T(8,128)S(1)}, f32[8,128]{1,0:T(8,128)S(1)}, u32[]{:S(2)}, u32[]{:S(2)}) collective-permute-start(f32[8,128]{1,0:T(8,128)S(1)} %add.64), channel_id=1, source_target_pairs={{0,1},{1,0},{2,3},{3,2},{4,5},{5,4},{6,7},{7,6},{8,9},{9,8},{10,11... | collective-permute-start | bytes 12296 | tf_op jit(solution)/shard_map/ppermute | solution.py:52
  52.5 14.4 %collective-permute-start.16 = (f16[128,1152]{1,0:T(8,128)(2,1)S(1)}, f16[128,1152]{1,0:T(8,128)(2,1)S(1)}, u32[]{:S(2)}, u32[]{:S(2)}) collective-permute-start(f16[128,1152]{1,0:T(8,128)(2,1)S(1)} %add_convert_fusion.4), channel_id=1, source_target_pairs={{241,0},{240,1},{243,2},{242,3},{245,4},{244,5},{247,6},{246,7},{2... | collective-permute-start | bytes 884744 | tf_op jit(solution)/shard_map/ppermute | solution.py:52
  55.1 15.5 %collective-permute-start.24 = (f16[128,1152]{1,0:T(8,128)(2,1)S(1)}, f16[128,1152]{1,0:T(8,128)(2,1)S(1)}, u32[]{:S(2)}, u32[]{:S(2)}) collective-permute-start(f16[128,1152]{1,0:T(8,128)(2,1)S(1)} %add_convert_fusion.3), channel_id=1, source_target_pairs={{0,6},{1,7},{2,0},{3,1},{4,2},{5,3},{6,4},{7,5},{8,14},{9,15},{10,... | collective-permute-start | bytes 884744 | tf_op jit(solution)/shard_map/ppermute | solution.py:52
  56.8 13.7 %collective-permute-start.25 = (f16[128,1152]{1,0:T(8,128)(2,1)S(1)}, f16[128,1152]{1,0:T(8,128)(2,1)S(1)}, u32[]{:S(2)}, u32[]{:S(2)}) collective-permute-start(f16[128,1152]{1,0:T(8,128)(2,1)S(1)} %add_convert_fusion.2), channel_id=1, source_target_pairs={{0,2},{1,3},{2,4},{3,5},{4,6},{5,7},{6,0},{7,1},{8,10},{9,11},{10,... | collective-permute-start | bytes 884744 | tf_op jit(solution)/shard_map/ppermute | solution.py:52
  57.3 5.4 %collective-permute-start.20 = (f32[8,128]{1,0:T(8,128)S(1)}, f32[8,128]{1,0:T(8,128)S(1)}, u32[]{:S(2)}, u32[]{:S(2)}) collective-permute-start(f32[8,128]{1,0:T(8,128)S(1)} %add.65), channel_id=1, source_target_pairs={{0,17},{1,16},{2,19},{3,18},{4,21},{5,20},{6,23},{7,22},{8,25},{9,... | collective-permute-start | bytes 12296 | tf_op jit(solution)/shard_map/ppermute | solution.py:52
  62.8 3.6 %collective-permute-start.21 = (f32[8,128]{1,0:T(8,128)S(1)}, f32[8,128]{1,0:T(8,128)S(1)}, u32[]{:S(2)}, u32[]{:S(2)}) collective-permute-start(f32[8,128]{1,0:T(8,128)S(1)} %add.66), channel_id=1, source_target_pairs={{0,32},{1,33},{2,34},{3,35},{4,36},{5,37},{6,38},{7,39},{8,40},{9,... | collective-permute-start | bytes 12296 | tf_op jit(solution)/shard_map/ppermute | solution.py:52
  66.4 16.6 %collective-permute-start.27 = (f16[128,1152]{1,0:T(8,128)(2,1)S(1)}, f16[128,1152]{1,0:T(8,128)(2,1)S(1)}, u32[]{:S(2)}, u32[]{:S(2)}) collective-permute-start(f16[128,1152]{1,0:T(8,128)(2,1)S(1)} %convert_element_type.67), channel_id=1, source_target_pairs={{0,2},{1,3},{2,4},{3,5},{4,6},{5,7},{6,0},{7,1},{8,10},{9,11},{10,... | collective-permute-start | bytes 884744 | tf_op jit(solution)/shard_map/ppermute | solution.py:52
  66.9 7.2 %collective-permute-start.22 = (f32[8,128]{1,0:T(8,128)S(1)}, f32[8,128]{1,0:T(8,128)S(1)}, u32[]{:S(2)}, u32[]{:S(2)}) collective-permute-start(f32[8,128]{1,0:T(8,128)S(1)} %add.67), channel_id=1, source_target_pairs={{0,64},{1,65},{2,66},{3,67},{4,68},{5,69},{6,70},{7,71},{8,72},{9,... | collective-permute-start | bytes 12296 | tf_op jit(solution)/shard_map/ppermute | solution.py:52
  70.7 12.3 %collective-permute-start.26 = (f16[128,1152]{1,0:T(8,128)(2,1)S(1)}, f16[128,1152]{1,0:T(8,128)(2,1)S(1)}, u32[]{:S(2)}, u32[]{:S(2)}) collective-permute-start(f16[128,1152]{1,0:T(8,128)(2,1)S(1)} %add_convert_fusion.1), channel_id=1, source_target_pairs={{0,6},{1,7},{2,0},{3,1},{4,2},{5,3},{6,4},{7,5},{8,14},{9,15},{10,... | collective-permute-start | bytes 884744 | tf_op jit(solution)/shard_map/ppermute | solution.py:52
  74.0 9.1 %collective-permute-start.28 = (f16[128,1152]{1,0:T(8,128)(2,1)S(1)}, f16[128,1152]{1,0:T(8,128)(2,1)S(1)}, u32[]{:S(2)}, u32[]{:S(2)}) collective-permute-start(f16[128,1152]{1,0:T(8,128)(2,1)S(1)} %add_convert_fusion), channel_id=1, source_target_pairs={{0,1},{1,0},{2,3},{3,2},{4,5},{5,4},{6,7},{7,6},{8,9},{9,8},{10,11... | collective-permute-start | bytes 884744 | tf_op jit(solution)/shard_map/ppermute | solution.py:52
  74.1 7.7 %collective-permute-start.23 = (f32[8,128]{1,0:T(8,128)S(1)}, f32[8,128]{1,0:T(8,128)S(1)}, u32[]{:S(2)}, u32[]{:S(2)}) collective-permute-start(f32[8,128]{1,0:T(8,128)S(1)} %add.68), channel_id=1, source_target_pairs={{0,128},{1,129},{2,130},{3,131},{4,132},{5,133},{6,134},{7,135},{8... | collective-permute-start | bytes 12296 | tf_op jit(solution)/shard_map/ppermute | solution.py:52

commit v3 on v2

--- a/solution.py
+++ b/solution.py
@@ -52,16 +52,15 @@
     return lax.ppermute(block, AXES, pairs)
 
 
-def unit_kernel(image_ref, text_ref, img_unit_ref, txt_unit_ref):
-    for source, unit in ((image_ref, img_unit_ref), (text_ref, txt_unit_ref)):
-        values = source[...].astype(jnp.float32)
-        inverse = lax.rsqrt(jnp.sum(values * values, axis=-1, keepdims=True) + EPS)
-        unit[...] = (values * inverse).astype(jnp.bfloat16)
-
-
-def units(image_embed, text_embed):
-    out = jax.ShapeDtypeStruct(image_embed.shape, jnp.bfloat16)
-    return pl.pallas_call(unit_kernel, out_shape=(out, out))(image_embed, text_embed)
+def unit_kernel(embed_ref, unit_ref):
+    values = embed_ref[...].astype(jnp.float32)
+    inverse = lax.rsqrt(jnp.sum(values * values, axis=-1, keepdims=True) + EPS)
+    unit_ref[...] = (values * inverse).astype(jnp.bfloat16)
+
+
+def unit(embed):
+    out_shape = jax.ShapeDtypeStruct(embed.shape, jnp.bfloat16)
+    return pl.pallas_call(unit_kernel, out_shape=out_shape, compiler_params=SMALL)(embed)
 
 
 def dot(left, right, dims):
@@ -76,7 +75,7 @@
 
 
 def score_kernel(scalars_ref, *refs):
-    img_refs, txt_refs, refs = refs[:9], refs[9:13], refs[13:]
+    img_refs, txt_refs, refs = refs[:8], refs[8:12], refs[12:]
     img, txt, weights, loss_ref = refs[:4]
     grad_refs = refs[4:]
     rows = txt_refs[0].shape[0]
@@ -128,7 +127,8 @@
 
 VMEM = pl.BlockSpec(memory_space=pltpu.VMEM)
 SMEM = pl.BlockSpec(memory_space=pltpu.SMEM)
-PARAMS = pltpu.CompilerParams(vmem_limit_bytes=30 * 1024 * 1024)
+LARGE = pltpu.CompilerParams(vmem_limit_bytes=16 * 1024 * 1024)
+SMALL = pltpu.CompilerParams(vmem_limit_bytes=4 * 1024 * 1024)
 
 
 def grads(count, rows, width):
@@ -150,18 +150,18 @@
         out_shape=out_shape,
         in_specs=[SMEM] + [VMEM] * (len(images) + len(texts)),
         out_specs=(VMEM,) * len(out_shape),
-        compiler_params=PARAMS,
+        compiler_params=LARGE,
     )(scalars, *images, *texts)
 
 
 def text_terms(weights, img, rows):
     out_shape = grads(4, rows, img.shape[1])
-    return pl.pallas_call(text_kernel, out_shape=out_shape, compiler_params=PARAMS)(weights, img)
+    return pl.pallas_call(text_kernel, out_shape=out_shape, compiler_params=LARGE)(weights, img)
 
 
 def image_terms(weights, txt, rows):
     out_shape = grads(4, rows, txt.shape[1])
-    return pl.pallas_call(image_kernel, out_shape=out_shape, compiler_params=PARAMS)(weights, txt)
+    return pl.pallas_call(image_kernel, out_shape=out_shape, compiler_params=LARGE)(weights, txt)
 
 
 def final_kernel(embed_ref, upstream_ref, grad_ref):
@@ -174,7 +174,9 @@
 
 def back_norm(embed, upstream):
     return pl.pallas_call(
-        final_kernel, out_shape=jax.ShapeDtypeStruct(upstream.shape, jnp.float32)
+        final_kernel,
+        out_shape=jax.ShapeDtypeStruct(upstream.shape, jnp.float32),
+        compiler_params=SMALL,
     )(embed, upstream)
 
 
@@ -196,9 +198,9 @@
 
 def shards(image_embed, text_embed, log_sharpness_factor, couple_score_shift):
     rows, width = image_embed.shape
-    half = rows // 2
     scalars = jnp.stack([jnp.exp(log_sharpness_factor), couple_score_shift])
-    own_img, own_txt = units(image_embed, text_embed)
+    own_img = unit(image_embed)
+    own_txt = unit(text_embed)
 
     txt_y = move(own_txt, AHEAD)
     txt_c = move(own_txt, SIDE)
@@ -209,36 +211,32 @@
     img_ma = move(img_a, MATE_Y)
     img_mb = move(img_m, DOWN_X)
     img_2 = move(img_a, UP_X)
-    txt_y, txt_c, img_a2, img_mb2 = together(txt_y, txt_c, img_2, img_mb)
+    txt_y, txt_c, img_2 = together(txt_y, txt_c, img_2)
     txt_d = move(txt_y, OTHER_CORE)
-    img_m2b = move(img_mb2[half:], DOWN_X)
-    img_m2a = move(img_a2[:half], MATE_Y)
-
-    images = (img_m2a, img_m2b, img_2, img_mb, img_ma, own_img, img_a, img_b, img_m)
+    img_m2 = move(img_2, MATE_Y)
+    images = (img_m2, img_2, img_mb, img_ma, own_img, img_a, img_b, img_m)
     texts = (txt_c, txt_d, txt_y, own_txt)
     img, txt, weights, loss, of_m2, of_2, of_mb, of_ma = score_terms(scalars, images, texts)
-    got_m2a = move(narrow(of_m2[:half]), MATE_Y)
-    got_m2b = move(narrow(of_m2[half:]), UP_X)
+    got_m2 = move(narrow(of_m2), MATE_Y)
+    got_mb = move(narrow(of_mb), UP_X)
     loss = loss_step(loss, 0)
     of_c, of_d, of_y, own_txt_grad = text_terms(weights, img, rows)
     got_d = move(narrow(of_d), OTHER_CORE)
+    got_ma = move(narrow(of_ma), MATE_Y)
     own_img_grad, of_a, of_b, of_m = image_terms(weights, txt, rows)
     loss, of_m = together(loss, of_m)
     loss = loss_step(loss, 1)
-    got_m2a, loss = together(got_m2a, loss)
-    got_m2a, got_m2b, got_d, own_img_grad = together(got_m2a, got_m2b, got_d, own_img_grad)
-    zeros = jnp.zeros((half, width), jnp.float32)
-    got_ma = move(narrow(of_ma), MATE_Y)
-    got_2 = move(narrow(of_2 + jnp.concatenate([wide(got_m2a), zeros], 0)), DOWN_X)
-    got_mb = move(narrow(of_mb + jnp.concatenate([zeros, wide(got_m2b)], 0)), UP_X)
+    got_m2, loss = together(got_m2, loss)
+    got_m2, got_mb, got_d, own_img_grad = together(got_m2, got_mb, got_d, own_img_grad)
+    got_2 = move(narrow(of_2 + wide(got_m2)), DOWN_X)
     got_y = move(narrow(of_y + wide(got_d)), inverse(AHEAD))
     got_c = move(narrow(of_c), inverse(SIDE))
+    got_m = move(narrow(of_m + wide(got_mb)), MATE_Y)
     loss = loss_step(loss, 2)
     loss = loss_step(loss, 3)
     got_ma, loss = together(got_ma, loss)
-    got_ma, got_2, got_mb = together(got_ma, got_2, got_mb)
+    got_ma, got_2, of_b = together(got_ma, got_2, of_b)
     got_b = move(narrow(of_b), UP_X)
-    got_m = move(narrow(of_m + wide(got_mb)), MATE_Y)
     got_a = move(narrow(of_a + wide(got_2) + wide(got_ma)), DOWN_X)
     loss = loss_step(loss, 4)
     loss = loss_step(loss, 5)
@@ -251,6 +249,7 @@
     loss = loss_step(loss, 7)
     img_grad = own_img_grad + wide(got_a) + wide(got_b) + wide(got_m)
     grad_image = back_norm(image_embed, img_grad)
+    loss, grad_image = together(loss, grad_image)
     pair_loss = jnp.sum(loss) / jnp.float32(rows * 256 * BAND * rows * X * YL)
     return pair_loss, grad_image, grad_text
 

time: 88.8 us -> 81 us (0.912); the launches traced: 87.3 us -> 80.8 us
  Pallas kernels: 12.9 us -> 8.91 us
  other arithmetic: 3.14 us -> 1.46 us
    pallas_call x2, Pallas kernels: 4.39 us -> 2.09 us  [back_norm(): pl.pallas_call(final_kernel, out_shape=jax.ShapeDtypeStruct(upstream.shap...]
    pallas_call x3 -> x4, Pallas kernels: 4.46 us -> 2.73 us  [the longest x1 1.58 us: text_terms(): pl.pallas_call(text_kernel, out_shape=out_shape, compiler_params=LARGE)]
    ppermute x30 -> x28, starting transfers between devices: 42.1 us -> 41.6 us  [move(): return lax.ppermute(block, AXES, pairs)]
    ppermute x30 -> x28, waiting for transfers between devices: 23.2 us -> 23 us  [move(): return lax.ppermute(block, AXES, pairs)]
    unnamed x4 -> x8, local copies, waits for them, and re-layouts: 1.92 us -> 1.93 us
  transfers between devices with their start and end apart: 30 -> 28, of which waited for: 12 -> 11; matrix products, arithmetic and copies ran while one was open for 3% -> 1% of each run, Pallas kernels for 3% -> 4%
where the time goes in v3:
time: 81 us; the launch traced here: 80.8 us
  starting transfers between devices  41.6 us (51%)
  waiting for transfers between devices  23 us (28%)
  Pallas kernels  8.91 us (11%)
  between operations  3.93 us (5%)
  local copies, waits for them, and re-layouts  1.93 us (2%)
  other arithmetic  1.46 us (2%)
    ppermute x28, starting transfers between devices, move(): return lax.ppermute(block, AXES, pairs)  41.6 us
    ppermute x28, waiting for transfers between devices, move(): return lax.ppermute(block, AXES, pairs)  23 us
    pallas_call x1, Pallas kernels, score_terms(): pl.pallas_call(score_kernel, out_shape=out_shape, in_specs=[SMEM] + [VMEM...  4.09 us
    pallas_call x2, Pallas kernels, back_norm(): pl.pallas_call(final_kernel, out_shape=jax.ShapeDtypeStruct(upstream.shap...  2.09 us
    unnamed x8, local copies, waits for them, and re-layouts  1.93 us
  transfers between devices with their start and end apart: 28, of which 11 were waited for; matrix products, arithmetic and copies ran while one was open for 1% of the time, Pallas kernels for 4%

profile of v3, /device:TPU:24, one launch (start us, length us, event | category | flops | bytes accessed | tf_op | source)
XLA Modules:
  0.0 80.8 jit_solution(4327055425258861292)
XLA Ops:
  0.6 1.0 %copy-done.2 = bf16[128,1152]{1,0:T(8,128)(2,1)S(1)} copy-done((bf16[128,1152]{1,0:T(8,128)(2,1)S(1)}, bf16[128,1152]{1,0:T(8,128)(2,1)}, u32[]{:S(2)}) %copy-start.2) | copy-done | bytes 294936
  1.7 0.8 %collective-permute-start.4 = (bf16[128,1152]{1,0:T(8,128)(2,1)S(1)}, bf16[128,1152]{1,0:T(8,128)(2,1)S(1)}, u32[]{:S(2)}, u32[]{:S(2)}) collective-permute-start(bf16[128,1152]{1,0:T(8,128)(2,1)S(1)} %shard_map.68.refs_4_), channel_id=1, source_target_pairs={{0,1},{1,0},{2,3},{3,2},{4,5},{5,4},{6,7},{7,6},{8,9},{9,8},{10,11... | collective-permute-start | bytes 884744 | tf_op jit(solution)/shard_map/ppermute | solution.py:52
  2.6 2.8 %collective-permute-start.3 = (bf16[128,1152]{1,0:T(8,128)(2,1)S(1)}, bf16[128,1152]{1,0:T(8,128)(2,1)S(1)}, u32[]{:S(2)}, u32[]{:S(2)}) collective-permute-start(bf16[128,1152]{1,0:T(8,128)(2,1)S(1)} %shard_map.68.refs_4_), channel_id=1, source_target_pairs={{0,6},{1,7},{2,0},{3,1},{4,2},{5,3},{6,4},{7,5},{8,14},{9,15},{10,... | collective-permute-start | bytes 884744 | tf_op jit(solution)/shard_map/ppermute | solution.py:52
  5.3 1.0 %copy-done = bf16[128,1152]{1,0:T(8,128)(2,1)S(1)} copy-done((bf16[128,1152]{1,0:T(8,128)(2,1)S(1)}, bf16[128,1152]{1,0:T(8,128)(2,1)}, u32[]{:S(2)}) %copy-start) | copy-done | bytes 294936
  6.5 4.7 %collective-permute-start.1 = (bf16[128,1152]{1,0:T(8,128)(2,1)S(1)}, bf16[128,1152]{1,0:T(8,128)(2,1)S(1)}, u32[]{:S(2)}, u32[]{:S(2)}) collective-permute-start(bf16[128,1152]{1,0:T(8,128)(2,1)S(1)} %shard_map.67.refs_11_), channel_id=1, source_target_pairs={{0,232},{1,233},{2,234},{3,235},{4,236},{5,237},{6,238},{7,239},{8... | collective-permute-start | bytes 884744 | tf_op jit(solution)/shard_map/ppermute | solution.py:52
  11.2 1.1 %collective-permute-start = (bf16[128,1152]{1,0:T(8,128)(2,1)S(1)}, bf16[128,1152]{1,0:T(8,128)(2,1)S(1)}, u32[]{:S(2)}, u32[]{:S(2)}) collective-permute-start(bf16[128,1152]{1,0:T(8,128)(2,1)S(1)} %shard_map.67.refs_11_), channel_id=1, source_target_pairs={{0,241},{1,240},{2,243},{3,242},{4,245},{5,244},{6,247},{7,246},{8... | collective-permute-start | bytes 884744 | tf_op jit(solution)/shard_map/ppermute | solution.py:52
  12.3 2.5 %collective-permute-done.2.refs_5_ = bf16[128,1152]{1,0:T(8,128)(2,1)S(1)} collective-permute-done((bf16[128,1152]{1,0:T(8,128)(2,1)S(1)}, bf16[128,1152]{1,0:T(8,128)(2,1)S(1)}, u32[]{:S(2)}, u32[]{:S(2)}) %collective-permute-start.2) | collective-permute-done | bytes 294944 | tf_op jit(solution)/shard_map/ppermute | solution.py:52
  14.7 1.3 %collective-permute-start.8 = (bf16[128,1152]{1,0:T(8,128)(2,1)S(1)}, bf16[128,1152]{1,0:T(8,128)(2,1)S(1)}, u32[]{:S(2)}, u32[]{:S(2)}) collective-permute-start(bf16[128,1152]{1,0:T(8,128)(2,1)S(1)} %collective-permute-done.2.refs_5_), channel_id=1, source_target_pairs={{0,1},{1,0},{2,3},{3,2},{4,5},{5,4},{6,7},{7,6},{8,9},{9,8},{10,11... | collective-permute-start | bytes 884744 | tf_op jit(solution)/shard_map/ppermute | solution.py:52
  16.0 3.2 %collective-permute-start.7 = (bf16[128,1152]{1,0:T(8,128)(2,1)S(1)}, bf16[128,1152]{1,0:T(8,128)(2,1)S(1)}, u32[]{:S(2)}, u32[]{:S(2)}) collective-permute-start(bf16[128,1152]{1,0:T(8,128)(2,1)S(1)} %collective-permute-done.4.refs_7_), channel_id=1, source_target_pairs={{0,6},{1,7},{2,0},{3,1},{4,2},{5,3},{6,4},{7,5},{8,14},{9,15},{10,... | collective-permute-start | bytes 884744 | tf_op jit(solution)/shard_map/ppermute | solution.py:52
  20.0 3.2 %collective-permute-done.5.refs_1_ = bf16[128,1152]{1,0:T(8,128)(2,1)S(1)} collective-permute-done((bf16[128,1152]{1,0:T(8,128)(2,1)S(1)}, bf16[128,1152]{1,0:T(8,128)(2,1)S(1)}, u32[]{:S(2)}, u32[]{:S(2)}) %collective-permute-start.5) | collective-permute-done | bytes 294944 | tf_op jit(solution)/shard_map/ppermute | solution.py:52
  23.2 1.3 %collective-permute-start.6 = (bf16[128,1152]{1,0:T(8,128)(2,1)S(1)}, bf16[128,1152]{1,0:T(8,128)(2,1)S(1)}, u32[]{:S(2)}, u32[]{:S(2)}) collective-permute-start(bf16[128,1152]{1,0:T(8,128)(2,1)S(1)} %collective-permute-done.5.refs_1_), channel_id=1, source_target_pairs={{0,1},{1,0},{2,3},{3,2},{4,5},{5,4},{6,7},{7,6},{8,9},{9,8},{10,11... | collective-permute-start | bytes 884744 | tf_op jit(solution)/shard_map/ppermute | solution.py:52
  25.9 4.0 %collective-permute-done.6.refs_0_ = bf16[128,1152]{1,0:T(8,128)(2,1)S(1)} collective-permute-done((bf16[128,1152]{1,0:T(8,128)(2,1)S(1)}, bf16[128,1152]{1,0:T(8,128)(2,1)S(1)}, u32[]{:S(2)}, u32[]{:S(2)}) %collective-permute-start.6) | collective-permute-done | bytes 294944 | tf_op jit(solution)/shard_map/ppermute | solution.py:52
  29.9 4.1 %shard_map.69 = (bf16[1024,1152]{1,0:T(8,128)(2,1)S(1)}, bf16[512,1152]{1,0:T(8,128)(2,1)S(1)}, bf16[1024,512]{1,0:T(8,128)(2,1)S(1)}, f32[8,128]{1,0:T(8,128)S(...) custom-call(f32[2]{0:T(128)S(1)} %pad_maximum_fusion.scalars_ref, ...), custom_call_target="tpu_custom_call" | custom-call | tf_op jit(solution)/shard_map/pallas_call | solution.py:148
  34.1 1.4 %collective-permute-start.10 = (f16[128,1152]{1,0:T(8,128)(2,1)S(1)}, f16[128,1152]{1,0:T(8,128)(2,1)S(1)}, u32[]{:S(2)}, u32[]{:S(2)}) collective-permute-start(f16[128,1152]{1,0:T(8,128)(2,1)S(1)} %convert_element_type.60), channel_id=1, source_target_pairs={{0,1},{1,0},{2,3},{3,2},{4,5},{5,4},{6,7},{7,6},{8,9},{9,8},{10,11... | collective-permute-start | bytes 884744 | tf_op jit(solution)/shard_map/ppermute | solution.py:52
  35.4 1.6 %shard_map.70 = (f32[128,1152]{1,0:T(8,128)S(1)}, f32[128,1152]{1,0:T(8,128)S(1)}, f32[128,1152]{1,0:T(8,128)S(1)}, f32[128,1152]{1,0:T(8,128)S(1)}) custom-call(bf16[1024,512]{1,0:T(8,128)(2,1)S(1)} %get-tuple-element.54.weights, bf16[1024,1152]{1,0:T(8,128)(2,1)S(1)} %get-tuple-element.55.img), custom_call_target="tpu_custom_call" | custom-call | tf_op jit(solution)/shard_map/pallas_call | solution.py:159
  38.0 0.9 %shard_map.71 = (f32[128,1152]{1,0:T(8,128)S(1)}, f32[128,1152]{1,0:T(8,128)S(1)}, f32[128,1152]{1,0:T(8,128)S(1)}, f32[128,1152]{1,0:T(8,128)S(1)}) custom-call(bf16[1024,512]{1,0:T(8,128)(2,1)S(1)} %get-tuple-element.54.weights, bf16[512,1152]{1,0:T(8,128)(2,1)S(1)} %get-tuple-element.59.txt), custom_call_target="tpu_custom_call" | custom-call | tf_op jit(solution)/shard_map/pallas_call | solution.py:164
  39.1 3.6 %collective-permute-done.12 = f32[8,128]{1,0:T(8,128)S(1)} collective-permute-done((f32[8,128]{1,0:T(8,128)S(1)}, f32[8,128]{1,0:T(8,128)S(1)}, u32[]{:S(2)}, u32[]{:S(2)}) %collective-permute-start.12) | collective-permute-done | bytes 4128 | tf_op jit(solution)/shard_map/ppermute | solution.py:52
  42.7 3.0 %collective-permute-start.17 = (f32[8,128]{1,0:T(8,128)S(1)}, f32[8,128]{1,0:T(8,128)S(1)}, u32[]{:S(2)}, u32[]{:S(2)}) collective-permute-start(f32[8,128]{1,0:T(8,128)S(1)} %add.55), channel_id=1, source_target_pairs={{0,6},{1,7},{2,4},{3,5},{4,2},{5,3},{6,0},{7,1},{8,14},{9,15},{10,... | collective-permute-start | bytes 12296 | tf_op jit(solution)/shard_map/ppermute | solution.py:52
  45.7 0.8 %collective-permute-start.16 = (f16[128,1152]{1,0:T(8,128)(2,1)S(1)}, f16[128,1152]{1,0:T(8,128)(2,1)S(1)}, u32[]{:S(2)}, u32[]{:S(2)}) collective-permute-start(f16[128,1152]{1,0:T(8,128)(2,1)S(1)} %convert_element_type.65), channel_id=1, source_target_pairs={{0,1},{1,0},{2,3},{3,2},{4,5},{5,4},{6,7},{7,6},{8,9},{9,8},{10,11... | collective-permute-start | bytes 884744 | tf_op jit(solution)/shard_map/ppermute | solution.py:52
  46.6 0.9 %collective-permute-done.17 = f32[8,128]{1,0:T(8,128)S(1)} collective-permute-done((f32[8,128]{1,0:T(8,128)S(1)}, f32[8,128]{1,0:T(8,128)S(1)}, u32[]{:S(2)}, u32[]{:S(2)}) %collective-permute-start.17) | collective-permute-done | bytes 4128 | tf_op jit(solution)/shard_map/ppermute | solution.py:52
  48.4 2.5 %collective-permute-start.15 = (f16[128,1152]{1,0:T(8,128)(2,1)S(1)}, f16[128,1152]{1,0:T(8,128)(2,1)S(1)}, u32[]{:S(2)}, u32[]{:S(2)}) collective-permute-start(f16[128,1152]{1,0:T(8,128)(2,1)S(1)} %add_convert_fusion.3), channel_id=1, source_target_pairs={{241,0},{240,1},{243,2},{242,3},{245,4},{244,5},{247,6},{246,7},{2... | collective-permute-start | bytes 884744 | tf_op jit(solution)/shard_map/ppermute | solution.py:52
  50.8 3.1 %collective-permute-done.18 = f32[8,128]{1,0:T(8,128)S(1)} collective-permute-done((f32[8,128]{1,0:T(8,128)S(1)}, f32[8,128]{1,0:T(8,128)S(1)}, u32[]{:S(2)}, u32[]{:S(2)}) %collective-permute-start.18) | collective-permute-done | bytes 4128 | tf_op jit(solution)/shard_map/ppermute | solution.py:52
  53.9 3.3 %collective-permute-start.19 = (f32[8,128]{1,0:T(8,128)S(1)}, f32[8,128]{1,0:T(8,128)S(1)}, u32[]{:S(2)}, u32[]{:S(2)}) collective-permute-start(f32[8,128]{1,0:T(8,128)S(1)} %add.58), channel_id=1, source_target_pairs={{0,17},{1,16},{2,19},{3,18},{4,21},{5,20},{6,23},{7,22},{8,25},{9,... | collective-permute-start | bytes 12296 | tf_op jit(solution)/shard_map/ppermute | solution.py:52
  57.3 0.8 collective-permute-start.23
  58.1 2.0 %collective-permute-done.19 = f32[8,128]{1,0:T(8,128)S(1)} collective-permute-done((f32[8,128]{1,0:T(8,128)S(1)}, f32[8,128]{1,0:T(8,128)S(1)}, u32[]{:S(2)}, u32[]{:S(2)}) %collective-permute-start.19) | collective-permute-done | bytes 4128 | tf_op jit(solution)/shard_map/ppermute | solution.py:52
  60.1 1.0 %collective-permute-start.20 = (f32[8,128]{1,0:T(8,128)S(1)}, f32[8,128]{1,0:T(8,128)S(1)}, u32[]{:S(2)}, u32[]{:S(2)}) collective-permute-start(f32[8,128]{1,0:T(8,128)S(1)} %add.59), channel_id=1, source_target_pairs={{0,32},{1,33},{2,34},{3,35},{4,36},{5,37},{6,38},{7,39},{8,40},{9,... | collective-permute-start | bytes 12296 | tf_op jit(solution)/shard_map/ppermute | solution.py:52
  61.7 2.0 %collective-permute-done.20 = f32[8,128]{1,0:T(8,128)S(1)} collective-permute-done((f32[8,128]{1,0:T(8,128)S(1)}, f32[8,128]{1,0:T(8,128)S(1)}, u32[]{:S(2)}, u32[]{:S(2)}) %collective-permute-start.20) | collective-permute-done | bytes 4128 | tf_op jit(solution)/shard_map/ppermute | solution.py:52
  63.7 2.5 %collective-permute-start.21 = (f32[8,128]{1,0:T(8,128)S(1)}, f32[8,128]{1,0:T(8,128)S(1)}, u32[]{:S(2)}, u32[]{:S(2)}) collective-permute-start(f32[8,128]{1,0:T(8,128)S(1)} %add.60), channel_id=1, source_target_pairs={{0,64},{1,65},{2,66},{3,67},{4,68},{5,69},{6,70},{7,71},{8,72},{9,... | collective-permute-start | bytes 12296 | tf_op jit(solution)/shard_map/ppermute | solution.py:52
  66.8 2.9 %collective-permute-start.24 = (f16[128,1152]{1,0:T(8,128)(2,1)S(1)}, f16[128,1152]{1,0:T(8,128)(2,1)S(1)}, u32[]{:S(2)}, u32[]{:S(2)}) collective-permute-start(f16[128,1152]{1,0:T(8,128)(2,1)S(1)} %add_convert_fusion.1), channel_id=1, source_target_pairs={{0,6},{1,7},{2,0},{3,1},{4,2},{5,3},{6,4},{7,5},{8,14},{9,15},{10,... | collective-permute-start | bytes 884744 | tf_op jit(solution)/shard_map/ppermute | solution.py:52
  69.7 5.7 %collective-permute-start.22 = (f32[8,128]{1,0:T(8,128)S(1)}, f32[8,128]{1,0:T(8,128)S(1)}, u32[]{:S(2)}, u32[]{:S(2)}) collective-permute-start(f32[8,128]{1,0:T(8,128)S(1)} %add.61), channel_id=1, source_target_pairs={{0,128},{1,129},{2,130},{3,131},{4,132},{5,133},{6,134},{7,135},{8... | collective-permute-start | bytes 12296 | tf_op jit(solution)/shard_map/ppermute | solution.py:52
  75.5 1.0 %shard_map.72 = f32[128,1152]{1,0:T(8,128)} custom-call(bf16[128,1152]{1,0:T(8,128)(2,1)S(1)} %copy-done.1, f32[128,1152]{1,0:T(8,128)S(1)} %convert_add_fusion.1.upstream_ref), custom_call_target="tpu_custom_call" | custom-call | tf_op jit(solution)/shard_map/pallas_call | solution.py:176
  77.4 1.0 %shard_map.73 = f32[128,1152]{1,0:T(8,128)} custom-call(bf16[128,1152]{1,0:T(8,128)(2,1)S(1)} %copy-done.3, f32[128,1152]{1,0:T(8,128)S(1)} %convert_add_fusion.upstream_ref), custom_call_target="tpu_custom_call" | custom-call | tf_op jit(solution)/shard_map/pallas_call | solution.py:176
  (61 shorter events, 6.1 us)
Async XLA Ops:
  0.6 1.0 %copy-start.2 = (bf16[128,1152]{1,0:T(8,128)(2,1)S(1)}, bf16[128,1152]{1,0:T(8,128)(2,1)}, u32[]{:S(2)}) copy-start(bf16[128,1152]{1,0:T(8,128)(2,1)} %embed_ref.7) | copy-start | bytes 884740
  1.7 10.5 %collective-permute-start.4 = (bf16[128,1152]{1,0:T(8,128)(2,1)S(1)}, bf16[128,1152]{1,0:T(8,128)(2,1)S(1)}, u32[]{:S(2)}, u32[]{:S(2)}) collective-permute-start(bf16[128,1152]{1,0:T(8,128)(2,1)S(1)} %shard_map.68.refs_4_), channel_id=1, source_target_pairs={{0,1},{1,0},{2,3},{3,2},{4,5},{5,4},{6,7},{7,6},{8,9},{9,8},{10,11... | collective-permute-start | bytes 884744 | tf_op jit(solution)/shard_map/ppermute | solution.py:52
  2.6 9.7 %collective-permute-start.3 = (bf16[128,1152]{1,0:T(8,128)(2,1)S(1)}, bf16[128,1152]{1,0:T(8,128)(2,1)S(1)}, u32[]{:S(2)}, u32[]{:S(2)}) collective-permute-start(bf16[128,1152]{1,0:T(8,128)(2,1)S(1)} %shard_map.68.refs_4_), channel_id=1, source_target_pairs={{0,6},{1,7},{2,0},{3,1},{4,2},{5,3},{6,4},{7,5},{8,14},{9,15},{10,... | collective-permute-start | bytes 884744 | tf_op jit(solution)/shard_map/ppermute | solution.py:52
  5.3 9.4 %collective-permute-start.2 = (bf16[128,1152]{1,0:T(8,128)(2,1)S(1)}, bf16[128,1152]{1,0:T(8,128)(2,1)S(1)}, u32[]{:S(2)}, u32[]{:S(2)}) collective-permute-start(bf16[128,1152]{1,0:T(8,128)(2,1)S(1)} %shard_map.68.refs_4_), channel_id=1, source_target_pairs={{0,2},{1,3},{2,4},{3,5},{4,6},{5,7},{6,0},{7,1},{8,10},{9,11},{10,... | collective-permute-start | bytes 884744 | tf_op jit(solution)/shard_map/ppermute | solution.py:52
  5.3 1.0 %copy-start = (bf16[128,1152]{1,0:T(8,128)(2,1)S(1)}, bf16[128,1152]{1,0:T(8,128)(2,1)}, u32[]{:S(2)}) copy-start(bf16[128,1152]{1,0:T(8,128)(2,1)} %embed_ref.6) | copy-start | bytes 884740
  6.5 12.8 %collective-permute-start.1 = (bf16[128,1152]{1,0:T(8,128)(2,1)S(1)}, bf16[128,1152]{1,0:T(8,128)(2,1)S(1)}, u32[]{:S(2)}, u32[]{:S(2)}) collective-permute-start(bf16[128,1152]{1,0:T(8,128)(2,1)S(1)} %shard_map.67.refs_11_), channel_id=1, source_target_pairs={{0,232},{1,233},{2,234},{3,235},{4,236},{5,237},{6,238},{7,239},{8... | collective-permute-start | bytes 884744 | tf_op jit(solution)/shard_map/ppermute | solution.py:52
  11.2 8.8 %collective-permute-start = (bf16[128,1152]{1,0:T(8,128)(2,1)S(1)}, bf16[128,1152]{1,0:T(8,128)(2,1)S(1)}, u32[]{:S(2)}, u32[]{:S(2)}) collective-permute-start(bf16[128,1152]{1,0:T(8,128)(2,1)S(1)} %shard_map.67.refs_11_), channel_id=1, source_target_pairs={{0,241},{1,240},{2,243},{3,242},{4,245},{5,244},{6,247},{7,246},{8... | collective-permute-start | bytes 884744 | tf_op jit(solution)/shard_map/ppermute | solution.py:52
  14.7 8.5 %collective-permute-start.5 = (bf16[128,1152]{1,0:T(8,128)(2,1)S(1)}, bf16[128,1152]{1,0:T(8,128)(2,1)S(1)}, u32[]{:S(2)}, u32[]{:S(2)}) collective-permute-start(bf16[128,1152]{1,0:T(8,128)(2,1)S(1)} %collective-permute-done.2.refs_5_), channel_id=1, source_target_pairs={{0,2},{1,3},{2,4},{3,5},{4,6},{5,7},{6,0},{7,1},{8,10},{9,11},{10,... | collective-permute-start | bytes 884744 | tf_op jit(solution)/shard_map/ppermute | solution.py:52
  14.7 11.2 %collective-permute-start.8 = (bf16[128,1152]{1,0:T(8,128)(2,1)S(1)}, bf16[128,1152]{1,0:T(8,128)(2,1)S(1)}, u32[]{:S(2)}, u32[]{:S(2)}) collective-permute-start(bf16[128,1152]{1,0:T(8,128)(2,1)S(1)} %collective-permute-done.2.refs_5_), channel_id=1, source_target_pairs={{0,1},{1,0},{2,3},{3,2},{4,5},{5,4},{6,7},{7,6},{8,9},{9,8},{10,11... | collective-permute-start | bytes 884744 | tf_op jit(solution)/shard_map/ppermute | solution.py:52
  16.0 9.9 %collective-permute-start.7 = (bf16[128,1152]{1,0:T(8,128)(2,1)S(1)}, bf16[128,1152]{1,0:T(8,128)(2,1)S(1)}, u32[]{:S(2)}, u32[]{:S(2)}) collective-permute-start(bf16[128,1152]{1,0:T(8,128)(2,1)S(1)} %collective-permute-done.4.refs_7_), channel_id=1, source_target_pairs={{0,6},{1,7},{2,0},{3,1},{4,2},{5,3},{6,4},{7,5},{8,14},{9,15},{10,... | collective-permute-start | bytes 884744 | tf_op jit(solution)/shard_map/ppermute | solution.py:52
  23.2 6.7 %collective-permute-start.6 = (bf16[128,1152]{1,0:T(8,128)(2,1)S(1)}, bf16[128,1152]{1,0:T(8,128)(2,1)S(1)}, u32[]{:S(2)}, u32[]{:S(2)}) collective-permute-start(bf16[128,1152]{1,0:T(8,128)(2,1)S(1)} %collective-permute-done.5.refs_1_), channel_id=1, source_target_pairs={{0,1},{1,0},{2,3},{3,2},{4,5},{5,4},{6,7},{7,6},{8,9},{9,8},{10,11... | collective-permute-start | bytes 884744 | tf_op jit(solution)/shard_map/ppermute | solution.py:52
  24.5 5.4 %collective-permute-start.9 = (bf16[128,1152]{1,0:T(8,128)(2,1)S(1)}, bf16[128,1152]{1,0:T(8,128)(2,1)S(1)}, u32[]{:S(2)}, u32[]{:S(2)}) collective-permute-start(bf16[128,1152]{1,0:T(8,128)(2,1)S(1)} %collective-permute-done.refs_10_), channel_id=1, source_target_pairs={{0,8},{1,9},{2,10},{3,11},{4,12},{5,13},{6,14},{7,15},{8,0},{9,1},... | collective-permute-start | bytes 884744 | tf_op jit(solution)/shard_map/ppermute | solution.py:52
  34.1 8.6 %collective-permute-start.10 = (f16[128,1152]{1,0:T(8,128)(2,1)S(1)}, f16[128,1152]{1,0:T(8,128)(2,1)S(1)}, u32[]{:S(2)}, u32[]{:S(2)}) collective-permute-start(f16[128,1152]{1,0:T(8,128)(2,1)S(1)} %convert_element_type.60), channel_id=1, source_target_pairs={{0,1},{1,0},{2,3},{3,2},{4,5},{5,4},{6,7},{7,6},{8,9},{9,8},{10,11... | collective-permute-start | bytes 884744 | tf_op jit(solution)/shard_map/ppermute | solution.py:52
  37.1 9.4 %collective-permute-start.13 = (f16[128,1152]{1,0:T(8,128)(2,1)S(1)}, f16[128,1152]{1,0:T(8,128)(2,1)S(1)}, u32[]{:S(2)}, u32[]{:S(2)}) collective-permute-start(f16[128,1152]{1,0:T(8,128)(2,1)S(1)} %convert_element_type.61), channel_id=1, source_target_pairs={{0,2},{1,3},{2,4},{3,5},{4,6},{5,7},{6,0},{7,1},{8,10},{9,11},{10,... | collective-permute-start | bytes 884744 | tf_op jit(solution)/shard_map/ppermute | solution.py:52
  37.2 9.4 %collective-permute-start.14 = (f16[128,1152]{1,0:T(8,128)(2,1)S(1)}, f16[128,1152]{1,0:T(8,128)(2,1)S(1)}, u32[]{:S(2)}, u32[]{:S(2)}) collective-permute-start(f16[128,1152]{1,0:T(8,128)(2,1)S(1)} %convert_element_type.62), channel_id=1, source_target_pairs={{0,8},{1,9},{2,10},{3,11},{4,12},{5,13},{6,14},{7,15},{8,0},{9,1},... | collective-permute-start | bytes 884744 | tf_op jit(solution)/shard_map/ppermute | solution.py:52
  37.5 1.6 %collective-permute-start.11 = (f32[8,128]{1,0:T(8,128)S(1)}, f32[8,128]{1,0:T(8,128)S(1)}, u32[]{:S(2)}, u32[]{:S(2)}) collective-permute-start(f32[8,128]{1,0:T(8,128)S(1)} %get-tuple-element.58), channel_id=1, source_target_pairs={{0,8},{1,9},{2,10},{3,11},{4,12},{5,13},{6,14},{7,15},{8,0},{9,1},... | collective-permute-start | bytes 12296 | tf_op jit(solution)/shard_map/ppermute | solution.py:52
  39.1 3.6 %collective-permute-start.12 = (f32[8,128]{1,0:T(8,128)S(1)}, f32[8,128]{1,0:T(8,128)S(1)}, u32[]{:S(2)}, u32[]{:S(2)}) collective-permute-start(f32[8,128]{1,0:T(8,128)S(1)} %add.54), channel_id=1, source_target_pairs={{0,2},{1,3},{2,0},{3,1},{4,6},{5,7},{6,4},{7,5},{8,10},{9,11},{10,... | collective-permute-start | bytes 12296 | tf_op jit(solution)/shard_map/ppermute | solution.py:52
  42.7 4.8 %collective-permute-start.17 = (f32[8,128]{1,0:T(8,128)S(1)}, f32[8,128]{1,0:T(8,128)S(1)}, u32[]{:S(2)}, u32[]{:S(2)}) collective-permute-start(f32[8,128]{1,0:T(8,128)S(1)} %add.55), channel_id=1, source_target_pairs={{0,6},{1,7},{2,4},{3,5},{4,2},{5,3},{6,0},{7,1},{8,14},{9,15},{10,... | collective-permute-start | bytes 12296 | tf_op jit(solution)/shard_map/ppermute | solution.py:52
  45.7 8.2 %collective-permute-start.16 = (f16[128,1152]{1,0:T(8,128)(2,1)S(1)}, f16[128,1152]{1,0:T(8,128)(2,1)S(1)}, u32[]{:S(2)}, u32[]{:S(2)}) collective-permute-start(f16[128,1152]{1,0:T(8,128)(2,1)S(1)} %convert_element_type.65), channel_id=1, source_target_pairs={{0,1},{1,0},{2,3},{3,2},{4,5},{5,4},{6,7},{7,6},{8,9},{9,8},{10,11... | collective-permute-start | bytes 884744 | tf_op jit(solution)/shard_map/ppermute | solution.py:52
  46.6 17.2 %collective-permute-start.27 = (f16[128,1152]{1,0:T(8,128)(2,1)S(1)}, f16[128,1152]{1,0:T(8,128)(2,1)S(1)}, u32[]{:S(2)}, u32[]{:S(2)}) collective-permute-start(f16[128,1152]{1,0:T(8,128)(2,1)S(1)} %convert_element_type.74), channel_id=1, source_target_pairs={{232,0},{233,1},{234,2},{235,3},{236,4},{237,5},{238,6},{239,7},{0... | collective-permute-start | bytes 884744 | tf_op jit(solution)/shard_map/ppermute | solution.py:52
  47.5 6.4 %collective-permute-start.18 = (f32[8,128]{1,0:T(8,128)S(1)}, f32[8,128]{1,0:T(8,128)S(1)}, u32[]{:S(2)}, u32[]{:S(2)}) collective-permute-start(f32[8,128]{1,0:T(8,128)S(1)} %add.57), channel_id=1, source_target_pairs={{0,1},{1,0},{2,3},{3,2},{4,5},{5,4},{6,7},{7,6},{8,9},{9,8},{10,11... | collective-permute-start | bytes 12296 | tf_op jit(solution)/shard_map/ppermute | solution.py:52
  48.4 15.4 %collective-permute-start.15 = (f16[128,1152]{1,0:T(8,128)(2,1)S(1)}, f16[128,1152]{1,0:T(8,128)(2,1)S(1)}, u32[]{:S(2)}, u32[]{:S(2)}) collective-permute-start(f16[128,1152]{1,0:T(8,128)(2,1)S(1)} %add_convert_fusion.3), channel_id=1, source_target_pairs={{241,0},{240,1},{243,2},{242,3},{245,4},{244,5},{247,6},{246,7},{2... | collective-permute-start | bytes 884744 | tf_op jit(solution)/shard_map/ppermute | solution.py:52
  53.9 6.2 %collective-permute-start.19 = (f32[8,128]{1,0:T(8,128)S(1)}, f32[8,128]{1,0:T(8,128)S(1)}, u32[]{:S(2)}, u32[]{:S(2)}) collective-permute-start(f32[8,128]{1,0:T(8,128)S(1)} %add.58), channel_id=1, source_target_pairs={{0,17},{1,16},{2,19},{3,18},{4,21},{5,20},{6,23},{7,22},{8,25},{9,... | collective-permute-start | bytes 12296 | tf_op jit(solution)/shard_map/ppermute | solution.py:52
  57.3 8.9 %collective-permute-start.23 = (f16[128,1152]{1,0:T(8,128)(2,1)S(1)}, f16[128,1152]{1,0:T(8,128)(2,1)S(1)}, u32[]{:S(2)}, u32[]{:S(2)}) collective-permute-start(f16[128,1152]{1,0:T(8,128)(2,1)S(1)} %add_convert_fusion.2), channel_id=1, source_target_pairs={{0,6},{1,7},{2,0},{3,1},{4,2},{5,3},{6,4},{7,5},{8,14},{9,15},{10,... | collective-permute-start | bytes 884744 | tf_op jit(solution)/shard_map/ppermute | solution.py:52
  60.1 3.6 %collective-permute-start.20 = (f32[8,128]{1,0:T(8,128)S(1)}, f32[8,128]{1,0:T(8,128)S(1)}, u32[]{:S(2)}, u32[]{:S(2)}) collective-permute-start(f32[8,128]{1,0:T(8,128)S(1)} %add.59), channel_id=1, source_target_pairs={{0,32},{1,33},{2,34},{3,35},{4,36},{5,37},{6,38},{7,39},{8,40},{9,... | collective-permute-start | bytes 12296 | tf_op jit(solution)/shard_map/ppermute | solution.py:52
  61.2 14.3 %copy-start.1 = (bf16[128,1152]{1,0:T(8,128)(2,1)S(1)}, bf16[128,1152]{1,0:T(8,128)(2,1)}, u32[]{:S(2)}) copy-start(bf16[128,1152]{1,0:T(8,128)(2,1)} %embed_ref.6) | copy-start | bytes 884740
  61.2 16.0 %collective-permute-start.26 = (f16[128,1152]{1,0:T(8,128)(2,1)S(1)}, f16[128,1152]{1,0:T(8,128)(2,1)S(1)}, u32[]{:S(2)}, u32[]{:S(2)}) collective-permute-start(f16[128,1152]{1,0:T(8,128)(2,1)S(1)} %add_convert_fusion), channel_id=1, source_target_pairs={{0,1},{1,0},{2,3},{3,2},{4,5},{5,4},{6,7},{7,6},{8,9},{9,8},{10,11... | collective-permute-start | bytes 884744 | tf_op jit(solution)/shard_map/ppermute | solution.py:52
  63.7 6.0 %collective-permute-start.21 = (f32[8,128]{1,0:T(8,128)S(1)}, f32[8,128]{1,0:T(8,128)S(1)}, u32[]{:S(2)}, u32[]{:S(2)}) collective-permute-start(f32[8,128]{1,0:T(8,128)S(1)} %add.60), channel_id=1, source_target_pairs={{0,64},{1,65},{2,66},{3,67},{4,68},{5,69},{6,70},{7,71},{8,72},{9,... | collective-permute-start | bytes 12296 | tf_op jit(solution)/shard_map/ppermute | solution.py:52
  66.2 11.0 %collective-permute-start.25 = (f16[128,1152]{1,0:T(8,128)(2,1)S(1)}, f16[128,1152]{1,0:T(8,128)(2,1)S(1)}, u32[]{:S(2)}, u32[]{:S(2)}) collective-permute-start(f16[128,1152]{1,0:T(8,128)(2,1)S(1)} %convert_element_type.71), channel_id=1, source_target_pairs={{0,2},{1,3},{2,4},{3,5},{4,6},{5,7},{6,0},{7,1},{8,10},{9,11},{10,... | collective-permute-start | bytes 884744 | tf_op jit(solution)/shard_map/ppermute | solution.py:52
  66.8 10.4 %collective-permute-start.24 = (f16[128,1152]{1,0:T(8,128)(2,1)S(1)}, f16[128,1152]{1,0:T(8,128)(2,1)S(1)}, u32[]{:S(2)}, u32[]{:S(2)}) collective-permute-start(f16[128,1152]{1,0:T(8,128)(2,1)S(1)} %add_convert_fusion.1), channel_id=1, source_target_pairs={{0,6},{1,7},{2,0},{3,1},{4,2},{5,3},{6,4},{7,5},{8,14},{9,15},{10,... | collective-permute-start | bytes 884744 | tf_op jit(solution)/shard_map/ppermute | solution.py:52
  69.7 7.5 %collective-permute-start.22 = (f32[8,128]{1,0:T(8,128)S(1)}, f32[8,128]{1,0:T(8,128)S(1)}, u32[]{:S(2)}, u32[]{:S(2)}) collective-permute-start(f32[8,128]{1,0:T(8,128)S(1)} %add.61), channel_id=1, source_target_pairs={{0,128},{1,129},{2,130},{3,131},{4,132},{5,133},{6,134},{7,135},{8... | collective-permute-start | bytes 12296 | tf_op jit(solution)/shard_map/ppermute | solution.py:52
  75.4 2.0 %copy-start.3 = (bf16[128,1152]{1,0:T(8,128)(2,1)S(1)}, bf16[128,1152]{1,0:T(8,128)(2,1)}, u32[]{:S(2)}) copy-start(bf16[128,1152]{1,0:T(8,128)(2,1)} %embed_ref.7) | copy-start | bytes 884740

commit v4 on v3

--- a/solution.py
+++ b/solution.py
@@ -45,6 +45,28 @@
     route(lambda z, yh, c, x, yl: (z ^ 1, yh, c, x, yl)),
     route(lambda z, yh, c, x, yl: (z ^ 2, yh, c, x, yl)),
     route(lambda z, yh, c, x, yl: (z ^ 4, yh, c, x, yl)),
+)
+
+
+def quad(total, pairs):
+    first, second, third = (move(total, route) for route in pairs)
+    return (total + first) + (second + third)
+
+
+X_QUAD = (
+    route(lambda z, yh, c, x, yl: (z, yh, c, x ^ 1, yl)),
+    route(lambda z, yh, c, x, yl: (z, yh, c, x ^ 2, yl)),
+    route(lambda z, yh, c, x, yl: (z, yh, c, x ^ 3, yl)),
+)
+Y_QUAD = (
+    MATE_Y,
+    route(lambda z, yh, c, x, yl: (z, 1 - yh, c, x, yl)),
+    route(lambda z, yh, c, x, yl: (z, 1 - yh, c, x, 1 - yl)),
+)
+Z_QUAD = (
+    route(lambda z, yh, c, x, yl: (z ^ 1, yh, c, x, yl)),
+    route(lambda z, yh, c, x, yl: (z ^ 2, yh, c, x, yl)),
+    route(lambda z, yh, c, x, yl: (z ^ 3, yh, c, x, yl)),
 )
 
 
@@ -239,13 +261,12 @@
     got_b = move(narrow(of_b), UP_X)
     got_a = move(narrow(of_a + wide(got_2) + wide(got_ma)), DOWN_X)
     loss = loss_step(loss, 4)
-    loss = loss_step(loss, 5)
     got_y, loss = together(got_y, loss)
     got_y, got_c = together(got_y, got_c)
     txt_grad = own_txt_grad + wide(got_c) + wide(got_y)
     grad_text = back_norm(text_embed, txt_grad)
     got_a, got_b, got_m, grad_text = together(got_a, got_b, got_m, grad_text)
-    loss = loss_step(loss, 6)
+    loss = quad(loss, Z_QUAD)
     loss = loss_step(loss, 7)
     img_grad = own_img_grad + wide(got_a) + wide(got_b) + wide(got_m)
     grad_image = back_norm(image_embed, img_grad)

time: 81 us -> 78.9 us (0.974); the launches traced: 80.8 us -> 77.5 us
  waiting for transfers between devices: 23 us -> 16.5 us
  starting transfers between devices: 41.6 us -> 44.8 us
    ppermute x28 -> x29, waiting for transfers between devices: 23 us -> 16.5 us  [move(): return lax.ppermute(block, AXES, pairs)]
    ppermute x28 -> x29, starting transfers between devices: 41.6 us -> 44.8 us  [move(): return lax.ppermute(block, AXES, pairs)]
  transfers between devices with their start and end apart: 28 -> 29, of which waited for: 11 -> 11; matrix products, arithmetic and copies ran while one was open for 1% -> 1% of each run, Pallas kernels for 4% -> 5%
where the time goes in v4:
time: 78.9 us; the launch traced here: 77.5 us
  starting transfers between devices  44.8 us (57%)
  waiting for transfers between devices  16.5 us (21%)
  Pallas kernels  8.91 us (11%)
  between operations  3.95 us (5%)
  local copies, waits for them, and re-layouts  1.93 us (2%)
  other arithmetic  1.46 us (2%)
    ppermute x29, starting transfers between devices, move(): return lax.ppermute(block, AXES, pairs)  44.8 us
    ppermute x29, waiting for transfers between devices, move(): return lax.ppermute(block, AXES, pairs)  16.5 us
    pallas_call x1, Pallas kernels, score_terms(): pl.pallas_call(score_kernel, out_shape=out_shape, in_specs=[SMEM] + [VMEM...  4.09 us
    pallas_call x2, Pallas kernels, back_norm(): pl.pallas_call(final_kernel, out_shape=jax.ShapeDtypeStruct(upstream.shap...  2.09 us
    unnamed x8, local copies, waits for them, and re-layouts  1.93 us
    pallas_call x1, Pallas kernels, text_terms(): pl.pallas_call(text_kernel, out_shape=out_shape, compiler_params=LARGE)  1.58 us
  transfers between devices with their start and end apart: 29, of which 11 were waited for; matrix products, arithmetic and copies ran while one was open for 1% of the time, Pallas kernels for 5%

profile of v4, /device:TPU:24, one launch (start us, length us, event | category | flops | bytes accessed | tf_op | source)
XLA Modules:
  0.0 77.5 jit_solution(5154575181199454942)
XLA Ops:
  0.6 1.0 %copy-done.2 = bf16[128,1152]{1,0:T(8,128)(2,1)S(1)} copy-done((bf16[128,1152]{1,0:T(8,128)(2,1)S(1)}, bf16[128,1152]{1,0:T(8,128)(2,1)}, u32[]{:S(2)}) %copy-start.2) | copy-done | bytes 294936
  1.7 0.8 %collective-permute-start.4 = (bf16[128,1152]{1,0:T(8,128)(2,1)S(1)}, bf16[128,1152]{1,0:T(8,128)(2,1)S(1)}, u32[]{:S(2)}, u32[]{:S(2)}) collective-permute-start(bf16[128,1152]{1,0:T(8,128)(2,1)S(1)} %shard_map.68.refs_4_), channel_id=1, source_target_pairs={{0,1},{1,0},{2,3},{3,2},{4,5},{5,4},{6,7},{7,6},{8,9},{9,8},{10,11... | collective-permute-start | bytes 884744 | tf_op jit(solution)/shard_map/ppermute | solution.py:74
  2.6 2.8 %collective-permute-start.3 = (bf16[128,1152]{1,0:T(8,128)(2,1)S(1)}, bf16[128,1152]{1,0:T(8,128)(2,1)S(1)}, u32[]{:S(2)}, u32[]{:S(2)}) collective-permute-start(bf16[128,1152]{1,0:T(8,128)(2,1)S(1)} %shard_map.68.refs_4_), channel_id=1, source_target_pairs={{0,6},{1,7},{2,0},{3,1},{4,2},{5,3},{6,4},{7,5},{8,14},{9,15},{10,... | collective-permute-start | bytes 884744 | tf_op jit(solution)/shard_map/ppermute | solution.py:74
  5.3 1.0 %copy-done = bf16[128,1152]{1,0:T(8,128)(2,1)S(1)} copy-done((bf16[128,1152]{1,0:T(8,128)(2,1)S(1)}, bf16[128,1152]{1,0:T(8,128)(2,1)}, u32[]{:S(2)}) %copy-start) | copy-done | bytes 294936
  6.5 4.7 %collective-permute-start.1 = (bf16[128,1152]{1,0:T(8,128)(2,1)S(1)}, bf16[128,1152]{1,0:T(8,128)(2,1)S(1)}, u32[]{:S(2)}, u32[]{:S(2)}) collective-permute-start(bf16[128,1152]{1,0:T(8,128)(2,1)S(1)} %shard_map.67.refs_11_), channel_id=1, source_target_pairs={{0,232},{1,233},{2,234},{3,235},{4,236},{5,237},{6,238},{7,239},{8... | collective-permute-start | bytes 884744 | tf_op jit(solution)/shard_map/ppermute | solution.py:74
  11.2 1.1 %collective-permute-start = (bf16[128,1152]{1,0:T(8,128)(2,1)S(1)}, bf16[128,1152]{1,0:T(8,128)(2,1)S(1)}, u32[]{:S(2)}, u32[]{:S(2)}) collective-permute-start(bf16[128,1152]{1,0:T(8,128)(2,1)S(1)} %shard_map.67.refs_11_), channel_id=1, source_target_pairs={{0,241},{1,240},{2,243},{3,242},{4,245},{5,244},{6,247},{7,246},{8... | collective-permute-start | bytes 884744 | tf_op jit(solution)/shard_map/ppermute | solution.py:74
  12.3 2.5 %collective-permute-done.2.refs_5_ = bf16[128,1152]{1,0:T(8,128)(2,1)S(1)} collective-permute-done((bf16[128,1152]{1,0:T(8,128)(2,1)S(1)}, bf16[128,1152]{1,0:T(8,128)(2,1)S(1)}, u32[]{:S(2)}, u32[]{:S(2)}) %collective-permute-start.2) | collective-permute-done | bytes 294944 | tf_op jit(solution)/shard_map/ppermute | solution.py:74
  14.7 1.3 %collective-permute-start.8 = (bf16[128,1152]{1,0:T(8,128)(2,1)S(1)}, bf16[128,1152]{1,0:T(8,128)(2,1)S(1)}, u32[]{:S(2)}, u32[]{:S(2)}) collective-permute-start(bf16[128,1152]{1,0:T(8,128)(2,1)S(1)} %collective-permute-done.2.refs_5_), channel_id=1, source_target_pairs={{0,1},{1,0},{2,3},{3,2},{4,5},{5,4},{6,7},{7,6},{8,9},{9,8},{10,11... | collective-permute-start | bytes 884744 | tf_op jit(solution)/shard_map/ppermute | solution.py:74
  16.0 3.2 %collective-permute-start.7 = (bf16[128,1152]{1,0:T(8,128)(2,1)S(1)}, bf16[128,1152]{1,0:T(8,128)(2,1)S(1)}, u32[]{:S(2)}, u32[]{:S(2)}) collective-permute-start(bf16[128,1152]{1,0:T(8,128)(2,1)S(1)} %collective-permute-done.4.refs_7_), channel_id=1, source_target_pairs={{0,6},{1,7},{2,0},{3,1},{4,2},{5,3},{6,4},{7,5},{8,14},{9,15},{10,... | collective-permute-start | bytes 884744 | tf_op jit(solution)/shard_map/ppermute | solution.py:74
  19.3 0.8 collective-permute-done.refs_10_
  20.0 3.2 %collective-permute-done.5.refs_1_ = bf16[128,1152]{1,0:T(8,128)(2,1)S(1)} collective-permute-done((bf16[128,1152]{1,0:T(8,128)(2,1)S(1)}, bf16[128,1152]{1,0:T(8,128)(2,1)S(1)}, u32[]{:S(2)}, u32[]{:S(2)}) %collective-permute-start.5) | collective-permute-done | bytes 294944 | tf_op jit(solution)/shard_map/ppermute | solution.py:74
  23.2 1.3 %collective-permute-start.6 = (bf16[128,1152]{1,0:T(8,128)(2,1)S(1)}, bf16[128,1152]{1,0:T(8,128)(2,1)S(1)}, u32[]{:S(2)}, u32[]{:S(2)}) collective-permute-start(bf16[128,1152]{1,0:T(8,128)(2,1)S(1)} %collective-permute-done.5.refs_1_), channel_id=1, source_target_pairs={{0,1},{1,0},{2,3},{3,2},{4,5},{5,4},{6,7},{7,6},{8,9},{9,8},{10,11... | collective-permute-start | bytes 884744 | tf_op jit(solution)/shard_map/ppermute | solution.py:74
  25.9 4.0 %collective-permute-done.6.refs_0_ = bf16[128,1152]{1,0:T(8,128)(2,1)S(1)} collective-permute-done((bf16[128,1152]{1,0:T(8,128)(2,1)S(1)}, bf16[128,1152]{1,0:T(8,128)(2,1)S(1)}, u32[]{:S(2)}, u32[]{:S(2)}) %collective-permute-start.6) | collective-permute-done | bytes 294944 | tf_op jit(solution)/shard_map/ppermute | solution.py:74
  29.9 4.1 %shard_map.69 = (bf16[1024,1152]{1,0:T(8,128)(2,1)S(1)}, bf16[512,1152]{1,0:T(8,128)(2,1)S(1)}, bf16[1024,512]{1,0:T(8,128)(2,1)S(1)}, f32[8,128]{1,0:T(8,128)S(...) custom-call(f32[2]{0:T(128)S(1)} %pad_maximum_fusion.scalars_ref, ...), custom_call_target="tpu_custom_call" | custom-call | tf_op jit(solution)/shard_map/pallas_call | solution.py:170
  34.1 1.4 %collective-permute-start.10 = (f16[128,1152]{1,0:T(8,128)(2,1)S(1)}, f16[128,1152]{1,0:T(8,128)(2,1)S(1)}, u32[]{:S(2)}, u32[]{:S(2)}) collective-permute-start(f16[128,1152]{1,0:T(8,128)(2,1)S(1)} %convert_element_type.60), channel_id=1, source_target_pairs={{0,1},{1,0},{2,3},{3,2},{4,5},{5,4},{6,7},{7,6},{8,9},{9,8},{10,11... | collective-permute-start | bytes 884744 | tf_op jit(solution)/shard_map/ppermute | solution.py:74
  35.4 1.6 %shard_map.70 = (f32[128,1152]{1,0:T(8,128)S(1)}, f32[128,1152]{1,0:T(8,128)S(1)}, f32[128,1152]{1,0:T(8,128)S(1)}, f32[128,1152]{1,0:T(8,128)S(1)}) custom-call(bf16[1024,512]{1,0:T(8,128)(2,1)S(1)} %get-tuple-element.54.weights, bf16[1024,1152]{1,0:T(8,128)(2,1)S(1)} %get-tuple-element.55.img), custom_call_target="tpu_custom_call" | custom-call | tf_op jit(solution)/shard_map/pallas_call | solution.py:181
  38.0 0.9 %shard_map.71 = (f32[128,1152]{1,0:T(8,128)S(1)}, f32[128,1152]{1,0:T(8,128)S(1)}, f32[128,1152]{1,0:T(8,128)S(1)}, f32[128,1152]{1,0:T(8,128)S(1)}) custom-call(bf16[1024,512]{1,0:T(8,128)(2,1)S(1)} %get-tuple-element.54.weights, bf16[512,1152]{1,0:T(8,128)(2,1)S(1)} %get-tuple-element.59.txt), custom_call_target="tpu_custom_call" | custom-call | tf_op jit(solution)/shard_map/pallas_call | solution.py:186
  39.2 0.8 %collective-permute-start.16 = (f16[128,1152]{1,0:T(8,128)(2,1)S(1)}, f16[128,1152]{1,0:T(8,128)(2,1)S(1)}, u32[]{:S(2)}, u32[]{:S(2)}) collective-permute-start(f16[128,1152]{1,0:T(8,128)(2,1)S(1)} %convert_element_type.65), channel_id=1, source_target_pairs={{0,1},{1,0},{2,3},{3,2},{4,5},{5,4},{6,7},{7,6},{8,9},{9,8},{10,11... | collective-permute-start | bytes 884744 | tf_op jit(solution)/shard_map/ppermute | solution.py:74
  40.0 2.7 %collective-permute-done.12 = f32[8,128]{1,0:T(8,128)S(1)} collective-permute-done((f32[8,128]{1,0:T(8,128)S(1)}, f32[8,128]{1,0:T(8,128)S(1)}, u32[]{:S(2)}, u32[]{:S(2)}) %collective-permute-start.12) | collective-permute-done | bytes 4128 | tf_op jit(solution)/shard_map/ppermute | solution.py:74
  42.7 3.0 %collective-permute-start.17 = (f32[8,128]{1,0:T(8,128)S(1)}, f32[8,128]{1,0:T(8,128)S(1)}, u32[]{:S(2)}, u32[]{:S(2)}) collective-permute-start(f32[8,128]{1,0:T(8,128)S(1)} %add.58), channel_id=1, source_target_pairs={{0,6},{1,7},{2,4},{3,5},{4,2},{5,3},{6,0},{7,1},{8,14},{9,15},{10,... | collective-permute-start | bytes 12296 | tf_op jit(solution)/shard_map/ppermute | solution.py:74
  45.8 1.7 %collective-permute-start.15 = (f16[128,1152]{1,0:T(8,128)(2,1)S(1)}, f16[128,1152]{1,0:T(8,128)(2,1)S(1)}, u32[]{:S(2)}, u32[]{:S(2)}) collective-permute-start(f16[128,1152]{1,0:T(8,128)(2,1)S(1)} %add_convert_fusion.3), channel_id=1, source_target_pairs={{241,0},{240,1},{243,2},{242,3},{245,4},{244,5},{247,6},{246,7},{2... | collective-permute-start | bytes 884744 | tf_op jit(solution)/shard_map/ppermute | solution.py:74
  47.6 0.9 %collective-permute-start.18 = (f32[8,128]{1,0:T(8,128)S(1)}, f32[8,128]{1,0:T(8,128)S(1)}, u32[]{:S(2)}, u32[]{:S(2)}) collective-permute-start(f32[8,128]{1,0:T(8,128)S(1)} %add.60), channel_id=1, source_target_pairs={{0,1},{1,0},{2,3},{3,2},{4,5},{5,4},{6,7},{7,6},{8,9},{9,8},{10,11... | collective-permute-start | bytes 12296 | tf_op jit(solution)/shard_map/ppermute | solution.py:74
  48.6 2.9 %collective-permute-start.24 = (f16[128,1152]{1,0:T(8,128)(2,1)S(1)}, f16[128,1152]{1,0:T(8,128)(2,1)S(1)}, u32[]{:S(2)}, u32[]{:S(2)}) collective-permute-start(f16[128,1152]{1,0:T(8,128)(2,1)S(1)} %add_convert_fusion.2), channel_id=1, source_target_pairs={{0,6},{1,7},{2,0},{3,1},{4,2},{5,3},{6,4},{7,5},{8,14},{9,15},{10,... | collective-permute-start | bytes 884744 | tf_op jit(solution)/shard_map/ppermute | solution.py:74
  51.5 4.6 %collective-permute-start.19 = (f32[8,128]{1,0:T(8,128)S(1)}, f32[8,128]{1,0:T(8,128)S(1)}, u32[]{:S(2)}, u32[]{:S(2)}) collective-permute-start(f32[8,128]{1,0:T(8,128)S(1)} %add.61), channel_id=1, source_target_pairs={{0,17},{1,16},{2,19},{3,18},{4,21},{5,20},{6,23},{7,22},{8,25},{9,... | collective-permute-start | bytes 12296 | tf_op jit(solution)/shard_map/ppermute | solution.py:74
  56.3 1.4 %collective-permute-done.19 = f32[8,128]{1,0:T(8,128)S(1)} collective-permute-done((f32[8,128]{1,0:T(8,128)S(1)}, f32[8,128]{1,0:T(8,128)S(1)}, u32[]{:S(2)}, u32[]{:S(2)}) %collective-permute-start.19) | collective-permute-done | bytes 4128 | tf_op jit(solution)/shard_map/ppermute | solution.py:74
  57.7 4.1 %collective-permute-start.22 = (f32[8,128]{1,0:T(8,128)S(1)}, f32[8,128]{1,0:T(8,128)S(1)}, u32[]{:S(2)}, u32[]{:S(2)}) collective-permute-start(f32[8,128]{1,0:T(8,128)S(1)} %add.62), channel_id=1, source_target_pairs={{0,96},{1,97},{2,98},{3,99},{4,100},{5,101},{6,102},{7,103},{8,104... | collective-permute-start | bytes 12296 | tf_op jit(solution)/shard_map/ppermute | solution.py:74
  62.7 0.7 collective-permute-done.22
  63.4 2.6 %collective-permute-start.25 = (f16[128,1152]{1,0:T(8,128)(2,1)S(1)}, f16[128,1152]{1,0:T(8,128)(2,1)S(1)}, u32[]{:S(2)}, u32[]{:S(2)}) collective-permute-start(f16[128,1152]{1,0:T(8,128)(2,1)S(1)} %add_convert_fusion.1), channel_id=1, source_target_pairs={{0,6},{1,7},{2,0},{3,1},{4,2},{5,3},{6,4},{7,5},{8,14},{9,15},{10,... | collective-permute-start | bytes 884744 | tf_op jit(solution)/shard_map/ppermute | solution.py:74
  66.3 5.8 %collective-permute-start.23 = (f32[8,128]{1,0:T(8,128)S(1)}, f32[8,128]{1,0:T(8,128)S(1)}, u32[]{:S(2)}, u32[]{:S(2)}) collective-permute-start(f32[8,128]{1,0:T(8,128)S(1)} %add_add_fusion), channel_id=1, source_target_pairs={{0,128},{1,129},{2,130},{3,131},{4,132},{5,133},{6,134},{7,135},{8... | collective-permute-start | bytes 12296 | tf_op jit(solution)/shard_map/ppermute | solution.py:74
  72.2 1.0 %shard_map.72 = f32[128,1152]{1,0:T(8,128)} custom-call(bf16[128,1152]{1,0:T(8,128)(2,1)S(1)} %copy-done.1, f32[128,1152]{1,0:T(8,128)S(1)} %convert_add_fusion.1.upstream_ref), custom_call_target="tpu_custom_call" | custom-call | tf_op jit(solution)/shard_map/pallas_call | solution.py:198
  73.3 0.7 collective-permute-done.23
  74.1 1.0 %shard_map.73 = f32[128,1152]{1,0:T(8,128)} custom-call(bf16[128,1152]{1,0:T(8,128)(2,1)S(1)} %copy-done.3, f32[128,1152]{1,0:T(8,128)S(1)} %convert_add_fusion.upstream_ref), custom_call_target="tpu_custom_call" | custom-call | tf_op jit(solution)/shard_map/pallas_call | solution.py:198
  (62 shorter events, 4.2 us)
Async XLA Ops:
  0.6 1.0 %copy-start.2 = (bf16[128,1152]{1,0:T(8,128)(2,1)S(1)}, bf16[128,1152]{1,0:T(8,128)(2,1)}, u32[]{:S(2)}) copy-start(bf16[128,1152]{1,0:T(8,128)(2,1)} %embed_ref.7) | copy-start | bytes 884740
  1.7 10.5 %collective-permute-start.4 = (bf16[128,1152]{1,0:T(8,128)(2,1)S(1)}, bf16[128,1152]{1,0:T(8,128)(2,1)S(1)}, u32[]{:S(2)}, u32[]{:S(2)}) collective-permute-start(bf16[128,1152]{1,0:T(8,128)(2,1)S(1)} %shard_map.68.refs_4_), channel_id=1, source_target_pairs={{0,1},{1,0},{2,3},{3,2},{4,5},{5,4},{6,7},{7,6},{8,9},{9,8},{10,11... | collective-permute-start | bytes 884744 | tf_op jit(solution)/shard_map/ppermute | solution.py:74
  2.6 9.7 %collective-permute-start.3 = (bf16[128,1152]{1,0:T(8,128)(2,1)S(1)}, bf16[128,1152]{1,0:T(8,128)(2,1)S(1)}, u32[]{:S(2)}, u32[]{:S(2)}) collective-permute-start(bf16[128,1152]{1,0:T(8,128)(2,1)S(1)} %shard_map.68.refs_4_), channel_id=1, source_target_pairs={{0,6},{1,7},{2,0},{3,1},{4,2},{5,3},{6,4},{7,5},{8,14},{9,15},{10,... | collective-permute-start | bytes 884744 | tf_op jit(solution)/shard_map/ppermute | solution.py:74
  5.3 9.4 %collective-permute-start.2 = (bf16[128,1152]{1,0:T(8,128)(2,1)S(1)}, bf16[128,1152]{1,0:T(8,128)(2,1)S(1)}, u32[]{:S(2)}, u32[]{:S(2)}) collective-permute-start(bf16[128,1152]{1,0:T(8,128)(2,1)S(1)} %shard_map.68.refs_4_), channel_id=1, source_target_pairs={{0,2},{1,3},{2,4},{3,5},{4,6},{5,7},{6,0},{7,1},{8,10},{9,11},{10,... | collective-permute-start | bytes 884744 | tf_op jit(solution)/shard_map/ppermute | solution.py:74
  6.5 12.8 %collective-permute-start.1 = (bf16[128,1152]{1,0:T(8,128)(2,1)S(1)}, bf16[128,1152]{1,0:T(8,128)(2,1)S(1)}, u32[]{:S(2)}, u32[]{:S(2)}) collective-permute-start(bf16[128,1152]{1,0:T(8,128)(2,1)S(1)} %shard_map.67.refs_11_), channel_id=1, source_target_pairs={{0,232},{1,233},{2,234},{3,235},{4,236},{5,237},{6,238},{7,239},{8... | collective-permute-start | bytes 884744 | tf_op jit(solution)/shard_map/ppermute | solution.py:74
  11.2 8.8 %collective-permute-start = (bf16[128,1152]{1,0:T(8,128)(2,1)S(1)}, bf16[128,1152]{1,0:T(8,128)(2,1)S(1)}, u32[]{:S(2)}, u32[]{:S(2)}) collective-permute-start(bf16[128,1152]{1,0:T(8,128)(2,1)S(1)} %shard_map.67.refs_11_), channel_id=1, source_target_pairs={{0,241},{1,240},{2,243},{3,242},{4,245},{5,244},{6,247},{7,246},{8... | collective-permute-start | bytes 884744 | tf_op jit(solution)/shard_map/ppermute | solution.py:74
  14.7 8.5 %collective-permute-start.5 = (bf16[128,1152]{1,0:T(8,128)(2,1)S(1)}, bf16[128,1152]{1,0:T(8,128)(2,1)S(1)}, u32[]{:S(2)}, u32[]{:S(2)}) collective-permute-start(bf16[128,1152]{1,0:T(8,128)(2,1)S(1)} %collective-permute-done.2.refs_5_), channel_id=1, source_target_pairs={{0,2},{1,3},{2,4},{3,5},{4,6},{5,7},{6,0},{7,1},{8,10},{9,11},{10,... | collective-permute-start | bytes 884744 | tf_op jit(solution)/shard_map/ppermute | solution.py:74
  14.7 11.2 %collective-permute-start.8 = (bf16[128,1152]{1,0:T(8,128)(2,1)S(1)}, bf16[128,1152]{1,0:T(8,128)(2,1)S(1)}, u32[]{:S(2)}, u32[]{:S(2)}) collective-permute-start(bf16[128,1152]{1,0:T(8,128)(2,1)S(1)} %collective-permute-done.2.refs_5_), channel_id=1, source_target_pairs={{0,1},{1,0},{2,3},{3,2},{4,5},{5,4},{6,7},{7,6},{8,9},{9,8},{10,11... | collective-permute-start | bytes 884744 | tf_op jit(solution)/shard_map/ppermute | solution.py:74
  16.0 9.9 %collective-permute-start.7 = (bf16[128,1152]{1,0:T(8,128)(2,1)S(1)}, bf16[128,1152]{1,0:T(8,128)(2,1)S(1)}, u32[]{:S(2)}, u32[]{:S(2)}) collective-permute-start(bf16[128,1152]{1,0:T(8,128)(2,1)S(1)} %collective-permute-done.4.refs_7_), channel_id=1, source_target_pairs={{0,6},{1,7},{2,0},{3,1},{4,2},{5,3},{6,4},{7,5},{8,14},{9,15},{10,... | collective-permute-start | bytes 884744 | tf_op jit(solution)/shard_map/ppermute | solution.py:74
  23.2 6.7 %collective-permute-start.6 = (bf16[128,1152]{1,0:T(8,128)(2,1)S(1)}, bf16[128,1152]{1,0:T(8,128)(2,1)S(1)}, u32[]{:S(2)}, u32[]{:S(2)}) collective-permute-start(bf16[128,1152]{1,0:T(8,128)(2,1)S(1)} %collective-permute-done.5.refs_1_), channel_id=1, source_target_pairs={{0,1},{1,0},{2,3},{3,2},{4,5},{5,4},{6,7},{7,6},{8,9},{9,8},{10,11... | collective-permute-start | bytes 884744 | tf_op jit(solution)/shard_map/ppermute | solution.py:74
  24.5 5.4 %collective-permute-start.9 = (bf16[128,1152]{1,0:T(8,128)(2,1)S(1)}, bf16[128,1152]{1,0:T(8,128)(2,1)S(1)}, u32[]{:S(2)}, u32[]{:S(2)}) collective-permute-start(bf16[128,1152]{1,0:T(8,128)(2,1)S(1)} %collective-permute-done.refs_10_), channel_id=1, source_target_pairs={{0,8},{1,9},{2,10},{3,11},{4,12},{5,13},{6,14},{7,15},{8,0},{9,1},... | collective-permute-start | bytes 884744 | tf_op jit(solution)/shard_map/ppermute | solution.py:74
  34.1 8.6 %collective-permute-start.10 = (f16[128,1152]{1,0:T(8,128)(2,1)S(1)}, f16[128,1152]{1,0:T(8,128)(2,1)S(1)}, u32[]{:S(2)}, u32[]{:S(2)}) collective-permute-start(f16[128,1152]{1,0:T(8,128)(2,1)S(1)} %convert_element_type.60), channel_id=1, source_target_pairs={{0,1},{1,0},{2,3},{3,2},{4,5},{5,4},{6,7},{7,6},{8,9},{9,8},{10,11... | collective-permute-start | bytes 884744 | tf_op jit(solution)/shard_map/ppermute | solution.py:74
  37.1 8.6 %collective-permute-start.13 = (f16[128,1152]{1,0:T(8,128)(2,1)S(1)}, f16[128,1152]{1,0:T(8,128)(2,1)S(1)}, u32[]{:S(2)}, u32[]{:S(2)}) collective-permute-start(f16[128,1152]{1,0:T(8,128)(2,1)S(1)} %convert_element_type.61), channel_id=1, source_target_pairs={{0,2},{1,3},{2,4},{3,5},{4,6},{5,7},{6,0},{7,1},{8,10},{9,11},{10,... | collective-permute-start | bytes 884744 | tf_op jit(solution)/shard_map/ppermute | solution.py:74
  37.2 8.5 %collective-permute-start.14 = (f16[128,1152]{1,0:T(8,128)(2,1)S(1)}, f16[128,1152]{1,0:T(8,128)(2,1)S(1)}, u32[]{:S(2)}, u32[]{:S(2)}) collective-permute-start(f16[128,1152]{1,0:T(8,128)(2,1)S(1)} %convert_element_type.62), channel_id=1, source_target_pairs={{0,8},{1,9},{2,10},{3,11},{4,12},{5,13},{6,14},{7,15},{8,0},{9,1},... | collective-permute-start | bytes 884744 | tf_op jit(solution)/shard_map/ppermute | solution.py:74
  37.5 1.6 %collective-permute-start.11 = (f32[8,128]{1,0:T(8,128)S(1)}, f32[8,128]{1,0:T(8,128)S(1)}, u32[]{:S(2)}, u32[]{:S(2)}) collective-permute-start(f32[8,128]{1,0:T(8,128)S(1)} %get-tuple-element.58), channel_id=1, source_target_pairs={{0,8},{1,9},{2,10},{3,11},{4,12},{5,13},{6,14},{7,15},{8,0},{9,1},... | collective-permute-start | bytes 12296 | tf_op jit(solution)/shard_map/ppermute | solution.py:74
  39.1 3.6 %collective-permute-start.12 = (f32[8,128]{1,0:T(8,128)S(1)}, f32[8,128]{1,0:T(8,128)S(1)}, u32[]{:S(2)}, u32[]{:S(2)}) collective-permute-start(f32[8,128]{1,0:T(8,128)S(1)} %add.57), channel_id=1, source_target_pairs={{0,2},{1,3},{2,0},{3,1},{4,6},{5,7},{6,4},{7,5},{8,10},{9,11},{10,... | collective-permute-start | bytes 12296 | tf_op jit(solution)/shard_map/ppermute | solution.py:74
  39.2 12.3 %collective-permute-start.16 = (f16[128,1152]{1,0:T(8,128)(2,1)S(1)}, f16[128,1152]{1,0:T(8,128)(2,1)S(1)}, u32[]{:S(2)}, u32[]{:S(2)}) collective-permute-start(f16[128,1152]{1,0:T(8,128)(2,1)S(1)} %convert_element_type.65), channel_id=1, source_target_pairs={{0,1},{1,0},{2,3},{3,2},{4,5},{5,4},{6,7},{7,6},{8,9},{9,8},{10,11... | collective-permute-start | bytes 884744 | tf_op jit(solution)/shard_map/ppermute | solution.py:74
  42.7 19.2 %collective-permute-start.28 = (f16[128,1152]{1,0:T(8,128)(2,1)S(1)}, f16[128,1152]{1,0:T(8,128)(2,1)S(1)}, u32[]{:S(2)}, u32[]{:S(2)}) collective-permute-start(f16[128,1152]{1,0:T(8,128)(2,1)S(1)} %convert_element_type.74), channel_id=1, source_target_pairs={{232,0},{233,1},{234,2},{235,3},{236,4},{237,5},{238,6},{239,7},{0... | collective-permute-start | bytes 884744 | tf_op jit(solution)/shard_map/ppermute | solution.py:74
  42.7 4.9 %collective-permute-start.17 = (f32[8,128]{1,0:T(8,128)S(1)}, f32[8,128]{1,0:T(8,128)S(1)}, u32[]{:S(2)}, u32[]{:S(2)}) collective-permute-start(f32[8,128]{1,0:T(8,128)S(1)} %add.58), channel_id=1, source_target_pairs={{0,6},{1,7},{2,4},{3,5},{4,2},{5,3},{6,0},{7,1},{8,14},{9,15},{10,... | collective-permute-start | bytes 12296 | tf_op jit(solution)/shard_map/ppermute | solution.py:74
  45.8 11.8 %collective-permute-start.15 = (f16[128,1152]{1,0:T(8,128)(2,1)S(1)}, f16[128,1152]{1,0:T(8,128)(2,1)S(1)}, u32[]{:S(2)}, u32[]{:S(2)}) collective-permute-start(f16[128,1152]{1,0:T(8,128)(2,1)S(1)} %add_convert_fusion.3), channel_id=1, source_target_pairs={{241,0},{240,1},{243,2},{242,3},{245,4},{244,5},{247,6},{246,7},{2... | collective-permute-start | bytes 884744 | tf_op jit(solution)/shard_map/ppermute | solution.py:74
  47.6 3.9 %collective-permute-start.18 = (f32[8,128]{1,0:T(8,128)S(1)}, f32[8,128]{1,0:T(8,128)S(1)}, u32[]{:S(2)}, u32[]{:S(2)}) collective-permute-start(f32[8,128]{1,0:T(8,128)S(1)} %add.60), channel_id=1, source_target_pairs={{0,1},{1,0},{2,3},{3,2},{4,5},{5,4},{6,7},{7,6},{8,9},{9,8},{10,11... | collective-permute-start | bytes 12296 | tf_op jit(solution)/shard_map/ppermute | solution.py:74
  48.6 13.9 %collective-permute-start.24 = (f16[128,1152]{1,0:T(8,128)(2,1)S(1)}, f16[128,1152]{1,0:T(8,128)(2,1)S(1)}, u32[]{:S(2)}, u32[]{:S(2)}) collective-permute-start(f16[128,1152]{1,0:T(8,128)(2,1)S(1)} %add_convert_fusion.2), channel_id=1, source_target_pairs={{0,6},{1,7},{2,0},{3,1},{4,2},{5,3},{6,4},{7,5},{8,14},{9,15},{10,... | collective-permute-start | bytes 884744 | tf_op jit(solution)/shard_map/ppermute | solution.py:74
  51.5 6.2 %collective-permute-start.19 = (f32[8,128]{1,0:T(8,128)S(1)}, f32[8,128]{1,0:T(8,128)S(1)}, u32[]{:S(2)}, u32[]{:S(2)}) collective-permute-start(f32[8,128]{1,0:T(8,128)S(1)} %add.61), channel_id=1, source_target_pairs={{0,17},{1,16},{2,19},{3,18},{4,21},{5,20},{6,23},{7,22},{8,25},{9,... | collective-permute-start | bytes 12296 | tf_op jit(solution)/shard_map/ppermute | solution.py:74
  56.1 16.1 %copy-start.1 = (bf16[128,1152]{1,0:T(8,128)(2,1)S(1)}, bf16[128,1152]{1,0:T(8,128)(2,1)}, u32[]{:S(2)}) copy-start(bf16[128,1152]{1,0:T(8,128)(2,1)} %embed_ref.6) | copy-start | bytes 884740
  56.1 17.8 %collective-permute-start.27 = (f16[128,1152]{1,0:T(8,128)(2,1)S(1)}, f16[128,1152]{1,0:T(8,128)(2,1)S(1)}, u32[]{:S(2)}, u32[]{:S(2)}) collective-permute-start(f16[128,1152]{1,0:T(8,128)(2,1)S(1)} %add_convert_fusion), channel_id=1, source_target_pairs={{0,1},{1,0},{2,3},{3,2},{4,5},{5,4},{6,7},{7,6},{8,9},{9,8},{10,11... | collective-permute-start | bytes 884744 | tf_op jit(solution)/shard_map/ppermute | solution.py:74
  57.7 5.7 %collective-permute-start.22 = (f32[8,128]{1,0:T(8,128)S(1)}, f32[8,128]{1,0:T(8,128)S(1)}, u32[]{:S(2)}, u32[]{:S(2)}) collective-permute-start(f32[8,128]{1,0:T(8,128)S(1)} %add.62), channel_id=1, source_target_pairs={{0,96},{1,97},{2,98},{3,99},{4,100},{5,101},{6,102},{7,103},{8,104... | collective-permute-start | bytes 12296 | tf_op jit(solution)/shard_map/ppermute | solution.py:74
  61.8 4.5 %collective-permute-start.21 = (f32[8,128]{1,0:T(8,128)S(1)}, f32[8,128]{1,0:T(8,128)S(1)}, u32[]{:S(2)}, u32[]{:S(2)}) collective-permute-start(f32[8,128]{1,0:T(8,128)S(1)} %add.62), channel_id=1, source_target_pairs={{0,64},{1,65},{2,66},{3,67},{4,68},{5,69},{6,70},{7,71},{8,72},{9,... | collective-permute-start | bytes 12296 | tf_op jit(solution)/shard_map/ppermute | solution.py:74
  61.8 4.5 %collective-permute-start.20 = (f32[8,128]{1,0:T(8,128)S(1)}, f32[8,128]{1,0:T(8,128)S(1)}, u32[]{:S(2)}, u32[]{:S(2)}) collective-permute-start(f32[8,128]{1,0:T(8,128)S(1)} %add.62), channel_id=1, source_target_pairs={{0,32},{1,33},{2,34},{3,35},{4,36},{5,37},{6,38},{7,39},{8,40},{9,... | collective-permute-start | bytes 12296 | tf_op jit(solution)/shard_map/ppermute | solution.py:74
  62.5 11.4 %collective-permute-start.26 = (f16[128,1152]{1,0:T(8,128)(2,1)S(1)}, f16[128,1152]{1,0:T(8,128)(2,1)S(1)}, u32[]{:S(2)}, u32[]{:S(2)}) collective-permute-start(f16[128,1152]{1,0:T(8,128)(2,1)S(1)} %convert_element_type.71), channel_id=1, source_target_pairs={{0,2},{1,3},{2,4},{3,5},{4,6},{5,7},{6,0},{7,1},{8,10},{9,11},{10,... | collective-permute-start | bytes 884744 | tf_op jit(solution)/shard_map/ppermute | solution.py:74
  63.4 10.6 %collective-permute-start.25 = (f16[128,1152]{1,0:T(8,128)(2,1)S(1)}, f16[128,1152]{1,0:T(8,128)(2,1)S(1)}, u32[]{:S(2)}, u32[]{:S(2)}) collective-permute-start(f16[128,1152]{1,0:T(8,128)(2,1)S(1)} %add_convert_fusion.1), channel_id=1, source_target_pairs={{0,6},{1,7},{2,0},{3,1},{4,2},{5,3},{6,4},{7,5},{8,14},{9,15},{10,... | collective-permute-start | bytes 884744 | tf_op jit(solution)/shard_map/ppermute | solution.py:74
  66.3 7.6 %collective-permute-start.23 = (f32[8,128]{1,0:T(8,128)S(1)}, f32[8,128]{1,0:T(8,128)S(1)}, u32[]{:S(2)}, u32[]{:S(2)}) collective-permute-start(f32[8,128]{1,0:T(8,128)S(1)} %add_add_fusion), channel_id=1, source_target_pairs={{0,128},{1,129},{2,130},{3,131},{4,132},{5,133},{6,134},{7,135},{8... | collective-permute-start | bytes 12296 | tf_op jit(solution)/shard_map/ppermute | solution.py:74
  72.1 2.0 %copy-start.3 = (bf16[128,1152]{1,0:T(8,128)(2,1)S(1)}, bf16[128,1152]{1,0:T(8,128)(2,1)}, u32[]{:S(2)}) copy-start(bf16[128,1152]{1,0:T(8,128)(2,1)} %embed_ref.7) | copy-start | bytes 884740
  (1 other events, 1.0 us)
